TPU v7x, 128 devices: a whole 4x4x4 slice. The times are simulated.
128 devices in a mesh: dp: 64 (over z, x_hi, y, core), tensor: 2 (over x_lo).
Axes of the slice: x: 4 (x_hi: 2, x_lo: 2; x = x_hi * 2 + x_lo), y: 4, z: 4, core: 2. Of those that a mesh axis runs over, the one named last changes fastest.
Arguments:
- tokens: bfloat16 [16384, 2048], P(('dp', 'tensor')), may hold values from -6 to 6
- positions: int32 [16384], P('dp'), may hold values from 0 to 1023, as said below
- norm_in: float32 [2048], replicated, may hold values from 0.5 to 1.5
- query_weight: bfloat16 [2048, 4096], P('dp', 'tensor'), may hold values from -0.125 to 0.125
- key_weight: bfloat16 [2048, 512], P('dp', 'tensor'), may hold values from -0.125 to 0.125
- value_weight: bfloat16 [2048, 512], P('dp', 'tensor'), may hold values from -0.125 to 0.125
- query_gain: float32 [128], replicated, may hold values from 0.5 to 1.5
- key_gain: float32 [128], replicated, may hold values from 0.5 to 1.5
- out_weight: bfloat16 [4096, 2048], P('tensor', 'dp'), may hold values from -0.5 to 0.5
- norm_mid: float32 [2048], replicated, may hold values from 0.5 to 1.5
- routed_experts: int32 [16384, 8], P(('dp', 'tensor')), may hold values from 0 to 63, all different within a row; in each aligned block of 128 rows (0 to 127, 128 to 255, ...) at most 20 rows name the same one
- route_weight: float32 [16384, 8], P(('dp', 'tensor')), may hold values from 0.05 to 0.5
- gate_weight: bfloat16 [64, 2048, 768], P('dp', None, 'tensor'), may hold values from -0.125 to 0.125
- up_weight: bfloat16 [64, 2048, 768], P('dp', None, 'tensor'), may hold values from -0.125 to 0.125
- down_weight: bfloat16 [64, 768, 2048], P('dp', 'tensor'), may hold values from -0.625 to 0.625
- out_grad: bfloat16 [16384, 2048], P(('dp', 'tensor')), may hold values from -6 to 6
Outputs:
- output: bfloat16 [16384, 2048], P(('dp', 'tensor'))
- grad_tokens: bfloat16 [16384, 2048], P(('dp', 'tensor'))
- grad_norm_in: float32 [2048], replicated
- grad_query: float32 [2048, 4096], P('dp', 'tensor')
- grad_key: float32 [2048, 512], P('dp', 'tensor')
- grad_value: float32 [2048, 512], P('dp', 'tensor')
- grad_query_gain: float32 [128], replicated
- grad_key_gain: float32 [128], replicated
- grad_out_proj: float32 [4096, 2048], P('tensor', 'dp')
- grad_norm_mid: float32 [2048], replicated
- grad_route: float32 [16384, 8], P(('dp', 'tensor'))
- grad_gate: float32 [64, 2048, 768], P('dp', None, 'tensor')
- grad_up: float32 [64, 2048, 768], P('dp', None, 'tensor')
- grad_down: float32 [64, 768, 2048], P('dp', 'tensor')
Inputs may be any that keep to these rules, and one draw needn't show every extreme that they name: Within each sequence of 256 tokens the positions rise, by one or two from each token to the next. `routed_experts`: each row names 8 different experts; in the rows of one device no expert is named by more than 20 rows.
All inputs are finite; a program needn't handle non-finite values.
Results may differ from a plain program's by a relative error of at most 0.02.
Values may be sent and summed in bfloat16 or wider, within the bound.
A program may use at most 320 MiB of HBM per device.

v0:
```python
import math

import jax
import jax.numpy as jnp
from jax import lax
from jax.sharding import PartitionSpec as P

HD = 128
TOP = 8


EPS = 1e-06
THETA = 1000000.0


def rms_scale(values):
    return lax.rsqrt(jnp.mean(values * values, axis=-1, keepdims=True) + EPS)


def norm_back(values, scale, gain, grad):
    scaled = gain * grad
    inner = jnp.mean(scaled * values, axis=-1, keepdims=True)
    d_values = scale * scaled - values * (scale * scale * scale) * inner
    axes = tuple(range(grad.ndim - 1))
    return (d_values, jnp.sum(grad * values * scale, axis=axes))


def rope_tables(positions, head_size):
    half = head_size // 2
    freqs = jnp.exp(jnp.arange(half, dtype=jnp.float32) * (-2.0 * math.log(THETA) / head_size))
    angles = positions.astype(jnp.float32)[:, None] * freqs[None, :]
    return (jnp.cos(angles)[:, None, :], jnp.sin(angles)[:, None, :])


def rotate(values, cosine, sine):
    half = values.shape[-1] // 2
    first = values[..., :half]
    second = values[..., half:]
    return jnp.concatenate(
        [first * cosine - second * sine, second * cosine + first * sine], axis=-1
    )


def rotate_back(grad, cosine, sine):
    half = grad.shape[-1] // 2
    first = grad[..., :half]
    second = grad[..., half:]
    return jnp.concatenate(
        [first * cosine + second * sine, second * cosine - first * sine], axis=-1
    )


def silu_slope(gate):
    sigma = jax.nn.sigmoid(gate)
    return sigma * (1.0 + gate * (1.0 - sigma))


def share_sequence(values):
    return lax.all_gather(values, "tensor", axis=0, tiled=True)


def sum_sequence(term, rows):
    return lax.psum_scatter(
        term(jnp.int32(0), lax.axis_size("tensor") * rows).astype(jnp.bfloat16),
        "tensor",
        scatter_dimension=0,
        tiled=True,
    ).astype(jnp.float32)


def to_owners(buffer):
    return lax.all_to_all(buffer, "dp", split_axis=1, concat_axis=1, tiled=True)


def to_sources(buffer):
    return lax.all_to_all(buffer, "dp", split_axis=1, concat_axis=1, tiled=True)


def per_device(
    tokens,
    positions,
    norm_in,
    query_weight,
    key_weight,
    value_weight,
    query_gain,
    key_gain,
    out_weight,
    norm_mid,
    routed_experts,
    route_weight,
    gate_weight,
    up_weight,
    down_weight,
    out_grad,
):
    rows, width = tokens.shape
    owners = lax.axis_size("dp")
    local_experts = gate_weight.shape[0]
    experts_total = local_experts * owners
    capacity = 5 * rows * TOP // (4 * experts_total)
    column = owners * capacity
    scale = HD ** (-0.5)
    query_full, key_full, value_full, out_full = (
        lax.all_gather(query_weight, "dp", axis=0, tiled=True),
        lax.all_gather(key_weight, "dp", axis=0, tiled=True),
        lax.all_gather(value_weight, "dp", axis=0, tiled=True),
        lax.all_gather(out_weight, "dp", axis=1, tiled=True),
    )
    query_heads = query_full.shape[1] // HD
    key_heads = key_full.shape[1] // HD
    group = query_heads // key_heads
    inputs = tokens.astype(jnp.float32)
    in_scale = rms_scale(inputs)
    normed = (inputs * in_scale * norm_in).astype(jnp.bfloat16)
    whole = share_sequence(normed)
    length = whole.shape[0]
    cosine, sine = rope_tables(positions, HD)
    query_raw = jnp.dot(whole, query_full, preferred_element_type=jnp.float32).reshape(
        length, query_heads, HD
    )
    key_raw = jnp.dot(whole, key_full, preferred_element_type=jnp.float32).reshape(
        length, key_heads, HD
    )
    value_low = (
        jnp.dot(whole, value_full, preferred_element_type=jnp.float32)
        .astype(jnp.bfloat16)
        .reshape(length, key_heads, HD)
    )
    query_scale = rms_scale(query_raw)
    query = (
        rotate(query_raw * query_scale * query_gain, cosine, sine)
        .astype(jnp.bfloat16)
        .reshape(length, key_heads, group, HD)
    )
    key_scale = rms_scale(key_raw)
    key = rotate(key_raw * key_scale * key_gain, cosine, sine).astype(jnp.bfloat16)
    causal = jnp.arange(length)[:, None] >= jnp.arange(length)[None, :]
    scores = jnp.einsum("ahgd,bhd->hgab", query, key, preferred_element_type=jnp.float32) * scale
    scores = jnp.where(causal, scores, -1e30)
    peak = jnp.max(scores, axis=-1, keepdims=True)
    log_total = peak + jnp.log(jnp.sum(jnp.exp(scores - peak), axis=-1, keepdims=True))
    probs_low = jnp.exp(scores - log_total).astype(jnp.bfloat16)
    mixed = (
        jnp.einsum("hgab,bhd->ahgd", probs_low, value_low, preferred_element_type=jnp.float32)
        .astype(jnp.bfloat16)
        .reshape(length, query_heads * HD)
    )

    def out_term(start, count):
        return jnp.dot(mixed, out_full, preferred_element_type=jnp.float32)

    attended = sum_sequence(out_term, rows)
    hidden_in = inputs + attended
    mid_scale = rms_scale(hidden_in)
    normed_mid = (hidden_in * mid_scale * norm_mid).astype(jnp.bfloat16)
    routes = rows * TOP
    flat_experts = routed_experts.reshape(routes)
    onehot = (flat_experts[:, None] == jnp.arange(experts_total, dtype=jnp.int32)[None, :]).astype(
        jnp.int32
    )
    rank = jnp.sum((jnp.cumsum(onehot, axis=0) - onehot) * onehot, axis=1)
    slot = (flat_experts % local_experts * owners + flat_experts // local_experts) * capacity + rank
    slot_count = local_experts * column
    route_of_slot = (
        jnp.full((slot_count,), routes, jnp.int32).at[slot].set(jnp.arange(routes, dtype=jnp.int32))
    )
    padded_mid = jnp.concatenate([normed_mid, jnp.zeros((1, width), jnp.bfloat16)], axis=0)
    send_rows = padded_mid[route_of_slot // TOP].reshape(local_experts, owners, capacity, width)
    expert_rows = to_owners(send_rows)
    gathered = lax.all_gather(expert_rows, "tensor", axis=0, tiled=True)
    rows_all = gathered.reshape(-1, local_experts, column, width)
    weights_gate, weights_up, weights_down = (gate_weight, up_weight, down_weight)
    gate = jnp.einsum("glmd,ldf->glmf", rows_all, weights_gate, preferred_element_type=jnp.float32)
    up = jnp.einsum("glmd,ldf->glmf", rows_all, weights_up, preferred_element_type=jnp.float32)
    activated = jax.nn.silu(gate)
    hidden = (activated * up).astype(jnp.bfloat16)
    units = hidden.shape[-1]
    hidden_flat = hidden.reshape(-1, column, units)
    piece = hidden_flat.reshape(
        lax.axis_size("tensor") * local_experts // local_experts, local_experts, column, units
    )
    result = jnp.einsum("glmf,lfd->glmd", piece, weights_down, preferred_element_type=jnp.float32)
    expert_out = lax.psum_scatter(
        result.reshape(lax.axis_size("tensor") * local_experts, owners, capacity, width).astype(
            jnp.bfloat16
        ),
        "tensor",
        scatter_dimension=0,
        tiled=True,
    )
    returned = to_sources(expert_out)
    route_out = (
        returned.reshape(slot_count, width)[slot].reshape(rows, TOP, width).astype(jnp.float32)
    )
    moe = jnp.sum(route_out * route_weight[:, :, None], axis=1)
    output = (hidden_in + moe).astype(jnp.bfloat16)
    grad = out_grad.astype(jnp.float32)
    grad_route = jnp.sum(route_out * grad[:, None, :], axis=-1)
    route_grads = (
        (route_weight[:, :, None] * grad[:, None, :]).astype(jnp.bfloat16).reshape(routes, width)
    )
    padded_grads = jnp.concatenate([route_grads, jnp.zeros((1, width), jnp.bfloat16)], axis=0)
    expert_grads = to_owners(
        padded_grads[route_of_slot].reshape(local_experts, owners, capacity, width)
    )
    grads_all = lax.all_gather(expert_grads, "tensor", axis=0, tiled=True).reshape(
        -1, local_experts, column, width
    )
    d_hidden = jnp.einsum(
        "glmd,lfd->glmf", grads_all, weights_down, preferred_element_type=jnp.float32
    )
    d_gate = (d_hidden * up * silu_slope(gate)).astype(jnp.bfloat16)
    d_up = (d_hidden * activated).astype(jnp.bfloat16)
    local_down = jnp.einsum("glmf,glmd->lfd", hidden, grads_all, preferred_element_type=jnp.float32)
    local_gate = jnp.einsum("glmd,glmf->ldf", rows_all, d_gate, preferred_element_type=jnp.float32)
    local_up = jnp.einsum("glmd,glmf->ldf", rows_all, d_up, preferred_element_type=jnp.float32)
    grad_gate, grad_up, grad_down = (local_gate, local_up, local_down)
    gate_flat = d_gate.reshape(-1, column, units)
    up_flat = d_up.reshape(-1, column, units)
    gate_piece = gate_flat.reshape(
        lax.axis_size("tensor") * local_experts // local_experts, local_experts, column, units
    )
    up_piece = up_flat.reshape(
        lax.axis_size("tensor") * local_experts // local_experts, local_experts, column, units
    )
    total = jnp.einsum(
        "glmf,ldf->glmd", gate_piece, weights_gate, preferred_element_type=jnp.float32
    )
    total = total + jnp.einsum(
        "glmf,ldf->glmd", up_piece, weights_up, preferred_element_type=jnp.float32
    )
    input_grads = lax.psum_scatter(
        total.reshape(lax.axis_size("tensor") * local_experts, owners, capacity, width).astype(
            jnp.bfloat16
        ),
        "tensor",
        scatter_dimension=0,
        tiled=True,
    )
    back_rows = to_sources(input_grads)
    d_mid = jnp.sum(
        back_rows.reshape(slot_count, width)[slot].reshape(rows, TOP, width).astype(jnp.float32),
        axis=1,
    )
    d_mid_in, grad_norm_mid = norm_back(hidden_in, mid_scale, norm_mid, d_mid)
    d_hidden_in = grad + d_mid_in
    d_attended = d_hidden_in.astype(jnp.bfloat16)
    d_whole = share_sequence(d_attended)
    grad_out_proj = jnp.einsum("ac,ad->cd", mixed, d_whole, preferred_element_type=jnp.float32)
    d_mixed = (
        jnp.einsum("ad,cd->ac", d_whole, out_full, preferred_element_type=jnp.float32)
        .astype(jnp.bfloat16)
        .reshape(length, key_heads, group, HD)
    )
    scores = jnp.einsum("ahgd,bhd->hgab", query, key, preferred_element_type=jnp.float32) * scale
    scores = jnp.where(causal, scores, -1e30)
    probs = jnp.exp(scores - log_total)
    probs_low = probs.astype(jnp.bfloat16)
    d_probs = jnp.einsum("ahgd,bhd->hgab", d_mixed, value_low, preferred_element_type=jnp.float32)
    value_grad = jnp.einsum(
        "hgab,ahgd->bhd", probs_low, d_mixed, preferred_element_type=jnp.float32
    )
    delta = jnp.sum(probs * d_probs, axis=-1, keepdims=True)
    d_scores = (probs * (d_probs - delta)).astype(jnp.bfloat16)
    d_query = (
        jnp.einsum("hgab,bhd->ahgd", d_scores, key, preferred_element_type=jnp.float32).reshape(
            length, query_heads, HD
        )
        * scale
    )
    d_key = (
        jnp.einsum("hgab,ahgd->bhd", d_scores, query, preferred_element_type=jnp.float32) * scale
    )
    d_query_raw, grad_query_gain = norm_back(
        query_raw, query_scale, query_gain, rotate_back(d_query, cosine, sine)
    )
    d_key_raw, grad_key_gain = norm_back(
        key_raw, key_scale, key_gain, rotate_back(d_key, cosine, sine)
    )
    query_low = d_query_raw.astype(jnp.bfloat16).reshape(length, query_heads * HD)
    key_low = d_key_raw.astype(jnp.bfloat16).reshape(length, key_heads * HD)
    value_back = value_grad.astype(jnp.bfloat16).reshape(length, key_heads * HD)
    grad_query = jnp.einsum("ad,ac->dc", whole, query_low, preferred_element_type=jnp.float32)
    grad_key = jnp.einsum("ad,ac->dc", whole, key_low, preferred_element_type=jnp.float32)
    grad_value = jnp.einsum("ad,ac->dc", whole, value_back, preferred_element_type=jnp.float32)

    def normed_term(start, count):
        total = jnp.einsum("ac,dc->ad", query_low, query_full, preferred_element_type=jnp.float32)
        total = total + jnp.einsum(
            "ac,dc->ad", key_low, key_full, preferred_element_type=jnp.float32
        )
        return total + jnp.einsum(
            "ac,dc->ad", value_back, value_full, preferred_element_type=jnp.float32
        )

    d_normed = sum_sequence(normed_term, rows)
    d_inputs, grad_norm_in = norm_back(inputs, in_scale, norm_in, d_normed)
    grad_tokens = (d_hidden_in + d_inputs).astype(jnp.bfloat16)
    grad_query, grad_key, grad_value, grad_out_proj = (
        lax.psum_scatter(grad_query, "dp", scatter_dimension=0, tiled=True),
        lax.psum_scatter(grad_key, "dp", scatter_dimension=0, tiled=True),
        lax.psum_scatter(grad_value, "dp", scatter_dimension=0, tiled=True),
        lax.psum_scatter(grad_out_proj, "dp", scatter_dimension=1, tiled=True),
    )
    grad_norm_in, grad_query_gain, grad_key_gain, grad_norm_mid = lax.psum(
        (grad_norm_in, grad_query_gain, grad_key_gain, grad_norm_mid), ("dp", "tensor")
    )
    return (
        output,
        grad_tokens,
        grad_norm_in,
        grad_query,
        grad_key,
        grad_value,
        grad_query_gain,
        grad_key_gain,
        grad_out_proj,
        grad_norm_mid,
        grad_route,
        grad_gate,
        grad_up,
        grad_down,
    )


def solution(mesh):
    return jax.shard_map(
        per_device,
        mesh=mesh,
        in_specs=(
            P(("dp", "tensor"), None),
            P("dp"),
            P(),
            P("dp", "tensor"),
            P("dp", "tensor"),
            P("dp", "tensor"),
            P(),
            P(),
            P("tensor", "dp"),
            P(),
            P(("dp", "tensor"), None),
            P(("dp", "tensor"), None),
            P("dp", None, "tensor"),
            P("dp", None, "tensor"),
            P("dp", "tensor", None),
            P(("dp", "tensor"), None),
        ),
        out_specs=(
            P(("dp", "tensor"), None),
            P(("dp", "tensor"), None),
            P(),
            P("dp", "tensor"),
            P("dp", "tensor"),
            P("dp", "tensor"),
            P(),
            P(),
            P("tensor", "dp"),
            P(),
            P(("dp", "tensor"), None),
            P("dp", None, "tensor"),
            P("dp", None, "tensor"),
            P("dp", "tensor", None),
        ),
        check_vma=False,
    )
```

profile of v0, /device:TPU:0, one launch (start us, length us, event | category | flops | bytes accessed | tf_op | source)
XLA Modules:
  0.0 2744.3 jit_solution(14364298702669861685)
XLA Ops:
  17.7 18.0 reduce-window.6
  45.7 13.6 gather_fusion.2
  68.2 11.9 all-to-all-start.2
  81.3 79.3 %all-gather.13.cloned.1.call-done = bf16[2048,256]{1,0:T(8,128)(2,1)} async-done(((bf16[32,256]{1,0:T(8,128)(2,1)}), bf16[2048,256]{1,0:T(8,128)(2,1)}) %all-gather.13.cloned.1.call-update) | async-done | bytes 1048592 | tf_op jit(solution)/shard_map/all_gather | solution.py:106
  165.0 68.7 %all-gather.11.cloned.1.call-done = bf16[2048,256]{1,0:T(8,128)(2,1)} async-done(((bf16[32,256]{1,0:T(8,128)(2,1)}), bf16[2048,256]{1,0:T(8,128)(2,1)}) %all-gather.11.cloned.1.call-update) | async-done | bytes 1048592 | tf_op jit(solution)/shard_map/all_gather | solution.py:107
  236.1 79.0 %all-gather.15.cloned.1.call-done = bf16[2048,2048]{1,0:T(8,128)(2,1)} async-done(((bf16[32,2048]{1,0:T(8,128)(2,1)}), bf16[2048,2048]{1,0:T(8,128)(2,1)}) %all-gather.15.cloned.1.call-update) | async-done | bytes 8388624 | tf_op jit(solution)/shard_map/all_gather | solution.py:105
  331.2 67.4 %all-gather.17.cloned.1.call-done = bf16[2048,2048]{0,1:T(8,128)(2,1)} async-done(((bf16[2048,32]{0,1:T(8,128)(2,1)}), bf16[2048,2048]{0,1:T(8,128)(2,1)}) %all-gather.17.cloned.1.call-update) | async-done | bytes 8388624 | tf_op jit(solution)/shard_map/all_gather | solution.py:108
  413.5 13.7 reduce-scatter.9.cloned.1.call-done
  445.6 152.1 %all_to_all.20 = bf16[1,64,20,2048]{3,2,0,1:T(8,128)(2,1)S(1)} all-to-all(bf16[1,64,20,2048]{3,2,0,1:T(8,128)(2,1)} %bitcast.323), channel_id=1, replica_groups=mesh['dp'=64,'tensor'=2] {'dp'}, dimensions={1} | all-to-all | bytes 10485760 | tf_op jit(solution)/shard_map/all_to_all | solution.py:72
  602.9 26.4 all-gather.21.cloned.1.call-done
  629.3 19.5 copy.153
  663.3 100.8 %all-gather.19.cloned.1.call-done = bf16[2,64,20,2048]{3,1,2,0:T(8,128)(2,1)} async-done(((bf16[1,64,20,2048]{3,1,2,0:T(8,128)(2,1)}), bf16[2,64,20,2048]{3,1,2,0:T(8,128)(2,1)}) %all-gather.19.cloned.1.call-update) | async-done | bytes 10485776 | tf_op jit(solution)/shard_map/all_gather | solution.py:171
  764.1 20.2 copy.143
  784.4 26.0 copy.171
  839.6 12.5 fusion.5
  852.0 20.2 copy.155
  872.3 13.6 copy.156
  885.9 125.5 %reduce-scatter.13.cloned.1.call-done = bf16[1,64,20,2048]{3,1,2,0:T(8,128)(2,1)} async-done(((bf16[2,64,20,2048]{3,1,2,0:T(8,128)(2,1)}), bf16[1,64,20,2048]{3,1,2,0:T(8,128)(2,1)}) %reduce-scatter.13.cloned.1.call-update) | async-done | bytes 5242896 | tf_op jit(solution)/shard_map/reduce_scatter | solution.py:233
  1029.9 75.5 %all-to-all-done.3 = bf16[1,64,20,2048]{3,2,0,1:T(8,128)(2,1)} async-done(((bf16[1,64,20,2048]{3,2,0,1:T(8,128)(2,1)}), bf16[1,64,20,2048]{3,2,0,1:T(8,128)(2,1)}, u32[]{:S(2)}, u32[]{:S(2)}) %all-to-all-start.3) | async-done | bytes 5242912 | tf_op jit(solution)/shard_map/all_to_all | solution.py:76
  1114.8 12.0 gather_fusion.3
  1141.2 30.9 %copy.146 = bf16[2,1,1280,2048]{3,0,2,1:T(2,128)(2,1)} copy(bf16[2,1,1280,2048]{3,2,0,1:T(8,128)(2,1)S(1)} %fusion.4) | data formatting | bytes 20971520 | tf_op jit(solution)/shard_map/convert_element_type | solution.py:185
  1172.1 13.7 copy.147
  1255.4 57.2 %reduce-scatter.11.cloned.1.call-done = bf16[1,64,20,2048]{3,1,2,0:T(8,128)(2,1)} async-done(((bf16[2,64,20,2048]{3,1,2,0:T(8,128)(2,1)}), bf16[1,64,20,2048]{3,1,2,0:T(8,128)(2,1)}) %reduce-scatter.11.cloned.1.call-update) | async-done | bytes 5242896 | tf_op jit(solution)/shard_map/reduce_scatter | solution.py:184
  1331.2 14.2 fusion.22
  1345.4 11.4 convolution_bitcast_fusion
  1364.5 45.7 %all-to-all-done.1 = bf16[1,64,20,2048]{3,2,0,1:T(8,128)(2,1)} async-done(((bf16[1,64,20,2048]{3,2,0,1:T(8,128)(2,1)}), bf16[1,64,20,2048]{3,2,0,1:T(8,128)(2,1)}, u32[]{:S(2)}, u32[]{:S(2)}) %all-to-all-start.1) | async-done | bytes 5242912 | tf_op jit(solution)/shard_map/all_to_all | solution.py:76
  1419.2 12.0 gather_fusion.1
  1439.4 68.4 %all-reduce.2 = (f32[2048]{0:T(1024)}, f32[128]{0:T(128)}, f32[128]{0:T(128)}, f32[2048]{0:T(1024)}) all-reduce(f32[2048]{0:T(1024)S(1)} %get-tuple-element.46, f32[128]{0:T(128)S(1)} %bitcast_reduce_fusion, f32[128]{0:T(128)S(1)} %bitcast_reduce_fusion.1, ...), channel_id=1, replica_groups=mesh['dp'=64,'tensor'=2] {'dp','tensor'}, use_global_device_ids=true, to_apply=%region_22.23 | all-reduce | flops 4352 | bytes 34816 | tf_op jit(solution)/shard_map/psum | solution.py:306
  1511.3 180.2 %reduce-scatter.21.cloned.1.call-done = f32[32,256]{1,0:T(8,128)} async-done(((f32[2048,256]{1,0:T(8,128)}), f32[32,256]{1,0:T(8,128)}) %reduce-scatter.21.cloned.1.call-update) | async-done | bytes 32784 | tf_op jit(solution)/shard_map/reduce_scatter | solution.py:303
  1691.4 331.9 %reduce-scatter.19.cloned.1.call-done = f32[32,256]{1,0:T(8,128)} async-done(((f32[2048,256]{1,0:T(8,128)}), f32[32,256]{1,0:T(8,128)}) %reduce-scatter.19.cloned.1.call-update) | async-done | bytes 32784 | tf_op jit(solution)/shard_map/reduce_scatter | solution.py:302
  2023.3 357.4 %reduce-scatter.23.cloned.1.call-done = f32[2048,32]{0,1:T(8,128)} async-done(((f32[2048,2048]{0,1:T(8,128)}), f32[2048,32]{0,1:T(8,128)}) %reduce-scatter.23.cloned.1.call-update) | async-done | bytes 262160 | tf_op jit(solution)/shard_map/reduce_scatter | solution.py:304
  2380.7 356.9 %reduce-scatter.17.cloned.1.call-done = f32[32,2048]{1,0:T(8,128)} async-done(((f32[2048,2048]{1,0:T(8,128)}), f32[32,2048]{1,0:T(8,128)}) %reduce-scatter.17.cloned.1.call-update) | async-done | bytes 262160 | tf_op jit(solution)/shard_map/reduce_scatter | solution.py:301
  (315 shorter events, 293.2 us)
Async XLA Ops:
  7.2 812.2 %copy-start = (bf16[1,2048,384]{2,1,0:T(8,128)(2,1)S(1)}, bf16[1,2048,384]{2,1,0:T(8,128)(2,1)}, u32[]{:S(2)}) copy-start(bf16[1,2048,384]{2,1,0:T(8,128)(2,1)} %param.28) | copy-start | bytes 4718596
  7.2 28.9 %copy-start.27 = (bf16[128,2048]{1,0:T(8,128)(2,1)S(1)}, bf16[128,2048]{1,0:T(8,128)(2,1)}, u32[]{:S(2)}) copy-start(bf16[128,2048]{1,0:T(8,128)(2,1)} %param.31) | copy-start | bytes 1572868
  7.2 74.1 %all-gather.9.cloned.1.call-start = ((), (), s32[]{:S(2)}) async-start(), calls=%async_computation.12 | async-start | bytes 1572864 | tf_op jit(solution)/shard_map/all_gather | solution.py:59
  11.7 148.8 %all-gather.13.cloned.1.call-start = ((), (), s32[]{:S(2)}) async-start(), calls=%async_computation.14 | async-start | bytes 1064960 | tf_op jit(solution)/shard_map/all_gather | solution.py:106
  12.5 221.2 %all-gather.11.cloned.1.call-start = ((), (), s32[]{:S(2)}) async-start(), calls=%async_computation.13 | async-start | bytes 1064960 | tf_op jit(solution)/shard_map/all_gather | solution.py:107
  13.2 301.9 %all-gather.15.cloned.1.call-start = ((), (), s32[]{:S(2)}) async-start(), calls=%async_computation.15 | async-start | bytes 8519680 | tf_op jit(solution)/shard_map/all_gather | solution.py:105
  13.8 384.8 %all-gather.17.cloned.1.call-start = ((), (), s32[]{:S(2)}) async-start(), calls=%async_computation.16 | async-start | bytes 8519680 | tf_op jit(solution)/shard_map/all_gather | solution.py:108
  68.2 95.9 %copy-start.70 = (f32[128]{0:T(128)S(1)}, f32[128]{0:T(128)}, u32[]{:S(2)}) copy-start(f32[128]{0:T(128)} %param.23) | copy-start | bytes 1540
  68.2 337.3 %all-to-all-start.2 = ((bf16[1,64,20,2048]{3,2,0,1:T(8,128)(2,1)}), bf16[1,64,20,2048]{3,2,0,1:T(8,128)(2,1)}, u32[]{:S(2)}, u32[]{:S(2)}) async-start(bf16[1,64,20,2048]{3,2,0,1:T(8,128)(2,1)} %bitcast.322), calls=%async_computation.4 | async-start | bytes 12582912 | tf_op jit(solution)/shard_map/all_to_all | solution.py:72
  80.0 347.1 %reduce-scatter.9.cloned.1.call-start = ((), (), s32[]{:S(2)}) async-start(), calls=%async_computation.17 | async-start | bytes 1572864 | tf_op jit(solution)/shard_map/reduce_scatter | solution.py:63
  80.7 247.7 %copy-start.29 = (pred[256,256]{0,1:T(8,128)(4,1)}, pred[256,256]{0,1:T(8,128)(4,1)S(1)}, u32[]{:S(2)}) copy-start(pred[256,256]{0,1:T(8,128)(4,1)S(1)} %iota_compare_fusion.2) | copy-start | bytes 196612
  81.2 243.4 %copy-start.35 = (f32[256,64]{1,0:T(8,128)}, f32[256,64]{1,0:T(8,128)S(1)}, u32[]{:S(2)}) copy-start(f32[256,64]{1,0:T(8,128)S(1)} %get-tuple-element.81) | copy-start | bytes 196612
  81.2 243.4 %copy-start.37 = (f32[256,64]{1,0:T(8,128)}, f32[256,64]{1,0:T(8,128)S(1)}, u32[]{:S(2)}) copy-start(f32[256,64]{1,0:T(8,128)S(1)} %get-tuple-element.82) | copy-start | bytes 196612
  81.3 152.4 %copy-start.7 = (bf16[256,2048]{1,0:T(8,128)(2,1)S(1)}, bf16[256,2048]{1,0:T(8,128)(2,1)}, u32[]{:S(2)}) copy-start(bf16[256,2048]{1,0:T(8,128)(2,1)} %all-gather.9.cloned.1.call-done) | copy-start | bytes 3145732
  162.7 158.2 %copy-start.41 = (f32[256,256]{0,1:T(8,128)}, f32[256,256]{0,1:T(8,128)S(1)}, u32[]{:S(2)}) copy-start(f32[256,256]{0,1:T(8,128)S(1)} %get-tuple-element.88) | copy-start | bytes 786436
  162.8 158.1 %copy-start.39 = (f32[256,2,128]{2,0,1:T(8,128)}, f32[256,2,128]{2,0,1:T(8,128)S(1)}, u32[]{:S(2)}) copy-start(f32[256,2,128]{2,0,1:T(8,128)S(1)} %copy.132) | copy-start | bytes 786436
  331.2 74.2 %copy-start.31 = (bf16[2,128,8,256]{3,1,2,0:T(8,128)(2,1)}, bf16[2,128,8,256]{3,1,2,0:T(8,128)(2,1)S(1)}, u32[]{:S(2)}) copy-start(bf16[2,128,8,256]{3,1,2,0:T(8,128)(2,1)S(1)} %convolution_convert_fusion.3) | copy-start | bytes 3145732
  405.4 224.0 %all-gather.21.cloned.1.call-start = ((), (), s32[]{:S(2)}) async-start(), calls=%async_computation.20 | async-start | bytes 15728640 | tf_op jit(solution)/shard_map/all_gather | solution.py:207
  413.4 350.7 %all-gather.19.cloned.1.call-start = ((), (), s32[]{:S(2)}) async-start(), calls=%async_computation.18 | async-start | bytes 15728640 | tf_op jit(solution)/shard_map/all_gather | solution.py:171
  602.9 408.6 %reduce-scatter.13.cloned.1.call-start = ((), (), s32[]{:S(2)}) async-start(), calls=%async_computation.21 | async-start | bytes 15728640 | tf_op jit(solution)/shard_map/reduce_scatter | solution.py:233
  1019.5 85.9 %all-to-all-start.3 = ((bf16[1,64,20,2048]{3,2,0,1:T(8,128)(2,1)}), bf16[1,64,20,2048]{3,2,0,1:T(8,128)(2,1)}, u32[]{:S(2)}, u32[]{:S(2)}) async-start(bf16[1,64,20,2048]{3,2,0,1:T(8,128)(2,1)} %copy.157), calls=%async_computation.6 | async-start | bytes 12582912 | tf_op jit(solution)/shard_map/all_to_all | solution.py:76
  1029.8 161.4 %all-gather.23.cloned.1.call-start = ((), (), s32[]{:S(2)}) async-start(), calls=%async_computation.22 | async-start | bytes 1572864 | tf_op jit(solution)/shard_map/all_gather | solution.py:59
  1133.6 179.0 %reduce-scatter.11.cloned.1.call-start = ((), (), s32[]{:S(2)}) async-start(), calls=%async_computation.19 | async-start | bytes 15728640 | tf_op jit(solution)/shard_map/reduce_scatter | solution.py:184
  1185.8 252.2 %reduce-scatter.15.cloned.1.call-start = ((), (), s32[]{:S(2)}) async-start(), calls=%async_computation.23 | async-start | bytes 1572864 | tf_op jit(solution)/shard_map/reduce_scatter | solution.py:63
  1232.1 459.3 %reduce-scatter.21.cloned.1.call-start = ((), (), s32[]{:S(2)}) async-start(), calls=%async_computation.26 | async-start | bytes 2129920 | tf_op jit(solution)/shard_map/reduce_scatter | solution.py:303
  1234.1 789.2 %reduce-scatter.19.cloned.1.call-start = ((), (), s32[]{:S(2)}) async-start(), calls=%async_computation.25 | async-start | bytes 2129920 | tf_op jit(solution)/shard_map/reduce_scatter | solution.py:302
  1235.9 1144.8 %reduce-scatter.23.cloned.1.call-start = ((), (), s32[]{:S(2)}) async-start(), calls=%async_computation.27 | async-start | bytes 17039360 | tf_op jit(solution)/shard_map/reduce_scatter | solution.py:304
  1245.8 1491.7 %reduce-scatter.17.cloned.1.call-start = ((), (), s32[]{:S(2)}) async-start(), calls=%async_computation.24 | async-start | bytes 17039360 | tf_op jit(solution)/shard_map/reduce_scatter | solution.py:301
  1320.8 89.5 %all-to-all-start.1 = ((bf16[1,64,20,2048]{3,2,0,1:T(8,128)(2,1)}), bf16[1,64,20,2048]{3,2,0,1:T(8,128)(2,1)}, u32[]{:S(2)}, u32[]{:S(2)}) async-start(bf16[1,64,20,2048]{3,2,0,1:T(8,128)(2,1)} %copy.148), calls=%async_computation.3 | async-start | bytes 12582912 | tf_op jit(solution)/shard_map/all_to_all | solution.py:76
  1331.2 25.7 slice-start
  1431.2 76.6 %copy-start.73 = (f32[128]{0:T(128)S(1)}, f32[128]{0:T(128)}, u32[]{:S(2)}) copy-start(f32[128]{0:T(128)} %get-tuple-element.83) | copy-start | bytes 1540
  1431.2 1306.3 %copy-start.1 = (bf16[1,2048,384]{2,1,0:T(8,128)(2,1)S(1)}, bf16[1,2048,384]{2,1,0:T(8,128)(2,1)}, u32[]{:S(2)}) copy-start(bf16[1,2048,384]{2,1,0:T(8,128)(2,1)} %param.28) | copy-start | bytes 4718596
  (67 other events, 344.1 us)
Sparse Core Ops, SparseCore 0:
  11.9 26.3 all-gather.8
  41.5 118.9 all-gather.12
  163.9 69.7 all-gather.10
  236.8 78.3 all-gather.14
  318.2 80.3 all-gather.16
  405.5 21.5 reduce-scatter.8
  428.9 200.3 all-gather.20
  631.1 132.9 all-gather.18
  886.0 125.3 reduce-scatter.12
  1133.7 26.0 all-gather.22
  1185.9 126.6 reduce-scatter.10
  1314.9 29.5 reduce-scatter.14
  1347.4 343.9 reduce-scatter.20
  1694.3 328.9 reduce-scatter.18
  2026.1 354.5 reduce-scatter.22
  2383.5 353.9 reduce-scatter.16
where the time goes:
time: 2750 us; the launch traced here: 2740 us
  waiting for transfers between devices  1970 us (72%)
  local copies, waits for them, and re-layouts  294 us (11%)
  blocking collectives  220 us (8%)
  matrix products  150 us (5%)
  other arithmetic  63.1 us (2%)
  starting transfers between devices  33.8 us (1%)
    reduce_scatter x1, waiting for transfers between devices, per_device(): lax.psum_scatter(grad_out_proj, 'dp', scatter_dimension=1, tiled=True)  357 us
    reduce_scatter x1, waiting for transfers between devices, per_device(): lax.psum_scatter(grad_query, 'dp', scatter_dimension=0, tiled=True)  357 us
    reduce_scatter x1, waiting for transfers between devices, per_device(): lax.psum_scatter(grad_key, 'dp', scatter_dimension=0, tiled=True)  332 us
    reduce_scatter x1, waiting for transfers between devices, per_device(): lax.psum_scatter(grad_value, 'dp', scatter_dimension=0, tiled=True)  180 us
    all_to_all x1, blocking collectives, to_owners(): return lax.all_to_all(buffer, 'dp', split_axis=1, concat_axis=1, tiled=True)  152 us
    reduce_scatter x1, waiting for transfers between devices, per_device(): lax.psum_scatter(total.reshape(lax.axis_size('tensor') * local_experts, o...  126 us
    all_to_all x2, waiting for transfers between devices, to_sources(): return lax.all_to_all(buffer, 'dp', split_axis=1, concat_axis=1, tiled=True)  121 us
    all_gather x1, waiting for transfers between devices, per_device(): gathered = lax.all_gather(expert_rows, 'tensor', axis=0, tiled=True)  101 us
  transfers between devices with their start and end apart: 19, of which 15 were waited for; matrix products, arithmetic and copies ran while one was open for 12% of the time, Pallas kernels for 0%

commit v1 on v0

v1 whole, which is shorter than its diff:
```python
import math

import jax
import jax.numpy as jnp
from jax import lax
from jax.sharding import PartitionSpec as P

HD = 128
TOP = 8
EPS = 1e-06
THETA = 1000000.0
BF16 = jnp.bfloat16
F32 = jnp.float32


def dot(left, right, contract):
    return lax.dot_general(left, right, (contract, ((), ())), preferred_element_type=F32)


def rms_scale(values):
    return lax.rsqrt(jnp.mean(values * values, axis=-1, keepdims=True) + EPS)


def norm_back(values, scale, gain, grad):
    scaled = gain * grad
    inner = jnp.mean(scaled * values, axis=-1, keepdims=True)
    d_values = scale * scaled - values * (scale * scale * scale) * inner
    axes = tuple(range(grad.ndim - 1))
    return (d_values, jnp.sum(grad * values * scale, axis=axes))


def rope_tables(positions, head_size):
    half = head_size // 2
    freqs = jnp.exp(jnp.arange(half, dtype=F32) * (-2.0 * math.log(THETA) / head_size))
    angles = positions.astype(F32)[:, None] * freqs[None, :]
    return (jnp.cos(angles)[:, None, :], jnp.sin(angles)[:, None, :])


def rotate(values, cosine, sine):
    half = values.shape[-1] // 2
    first = values[..., :half]
    second = values[..., half:]
    return jnp.concatenate(
        [first * cosine - second * sine, second * cosine + first * sine], axis=-1
    )


def rotate_back(grad, cosine, sine):
    half = grad.shape[-1] // 2
    first = grad[..., :half]
    second = grad[..., half:]
    return jnp.concatenate(
        [first * cosine + second * sine, second * cosine - first * sine], axis=-1
    )


def swap(values):
    return lax.ppermute(values, "tensor", [(0, 1), (1, 0)])


def share_sequence(values):
    other = swap(values)
    first = lax.axis_index("tensor") == 0
    return jnp.concatenate(
        [jnp.where(first, values, other), jnp.where(first, other, values)], axis=0
    )


def sum_sequence(total, rows):
    mine = lax.axis_index("tensor") * rows
    own = lax.dynamic_slice_in_dim(total, mine, rows, 0)
    sent = lax.dynamic_slice_in_dim(total, rows - mine, rows, 0).astype(BF16)
    return own + swap(sent).astype(F32)


def exchange(buffer):
    return lax.all_to_all(buffer, "dp", split_axis=0, concat_axis=0, tiled=True)


def per_device(
    tokens,
    positions,
    norm_in,
    query_weight,
    key_weight,
    value_weight,
    query_gain,
    key_gain,
    out_weight,
    norm_mid,
    routed_experts,
    route_weight,
    gate_weight,
    up_weight,
    down_weight,
    out_grad,
):
    rows, width = tokens.shape
    owners = lax.axis_size("dp")
    experts = owners
    capacity = 5 * rows * TOP // (4 * experts)
    slots = experts * capacity
    scale = HD ** (-0.5)

    shard = jnp.concatenate([query_weight, key_weight, value_weight, out_weight.T], axis=1)
    full = lax.all_gather(shard, "dp", axis=0, tiled=True)
    q_cols, k_cols = query_weight.shape[1], key_weight.shape[1]
    in_cols = q_cols + 2 * k_cols
    in_full, out_full = full[:, :in_cols], full[:, in_cols:]
    query_heads, key_heads = q_cols // HD, k_cols // HD
    group = query_heads // key_heads

    gate_w, up_w, down_w = gate_weight[0], up_weight[0], down_weight[0]
    down_o, gate_o, up_o = swap(down_w), swap(gate_w), swap(up_w)

    names = routed_experts[:, :, None] == jnp.arange(experts, dtype=jnp.int32)
    chosen = jnp.any(names, axis=1)
    weight_of = jnp.sum(jnp.where(names, route_weight[:, :, None], 0.0), axis=1)
    below = jnp.arange(rows)[:, None] > jnp.arange(rows)[None, :]
    rank = dot(below.astype(BF16), chosen.astype(BF16), ((1,), (0,))).astype(jnp.int32)
    rank = jnp.where(chosen, rank, -1)
    place_b = rank.T[:, None, :] == jnp.arange(capacity, dtype=jnp.int32)[None, :, None]
    place = place_b.reshape(slots, rows).astype(BF16)
    slot_weight = jnp.sum(jnp.where(place_b, weight_of.T[:, None, :], 0.0), axis=2).reshape(slots)

    grad = out_grad.astype(F32)
    d_rows = (dot(place, out_grad, ((1,), (0,))) * slot_weight[:, None]).astype(BF16)
    expert_grads = exchange(d_rows.reshape(experts, capacity, width)).reshape(slots, width)

    inputs = tokens.astype(F32)
    in_scale = rms_scale(inputs)
    normed = (inputs * in_scale * norm_in).astype(BF16)
    whole = share_sequence(normed)
    length = whole.shape[0]
    cosine, sine = rope_tables(positions, HD)
    raw = dot(whole, in_full, ((1,), (0,)))
    query_raw = raw[:, :q_cols].reshape(length, query_heads, HD)
    key_raw = raw[:, q_cols : q_cols + k_cols].reshape(length, key_heads, HD)
    value_low = raw[:, q_cols + k_cols :].astype(BF16).reshape(length, key_heads, HD)
    query_scale = rms_scale(query_raw)
    query = (
        rotate(query_raw * query_scale * query_gain, cosine, sine)
        .astype(BF16)
        .reshape(length, key_heads, group, HD)
    )
    key_scale = rms_scale(key_raw)
    key = rotate(key_raw * key_scale * key_gain, cosine, sine).astype(BF16)
    causal = jnp.arange(length)[:, None] >= jnp.arange(length)[None, :]
    scores = jnp.einsum("ahgd,bhd->hgab", query, key, preferred_element_type=F32) * scale
    scores = jnp.where(causal, scores, -1e30)
    peak = jnp.max(scores, axis=-1, keepdims=True)
    log_total = peak + jnp.log(jnp.sum(jnp.exp(scores - peak), axis=-1, keepdims=True))
    probs_low = jnp.exp(scores - log_total).astype(BF16)
    mixed = (
        jnp.einsum("hgab,bhd->ahgd", probs_low, value_low, preferred_element_type=F32)
        .astype(BF16)
        .reshape(length, q_cols)
    )
    attended = sum_sequence(dot(mixed, out_full, ((1,), (1,))), rows)
    hidden_in = inputs + attended
    mid_scale = rms_scale(hidden_in)
    normed_mid = (hidden_in * mid_scale * norm_mid).astype(BF16)

    send_rows = dot(place, normed_mid, ((1,), (0,))).astype(BF16)
    rows_in = exchange(send_rows.reshape(experts, capacity, width)).reshape(slots, width)

    def expert_half(gate_h, up_h, down_h):
        gate = dot(rows_in, gate_h, ((1,), (0,)))
        up = dot(rows_in, up_h, ((1,), (0,)))
        d_hidden = dot(expert_grads, down_h, ((1,), (1,)))
        sigma = jax.nn.sigmoid(gate)
        activated = gate * sigma
        hidden = (activated * up).astype(BF16)
        d_gate = (d_hidden * up * (sigma * (1.0 + gate * (1.0 - sigma)))).astype(BF16)
        d_up = (d_hidden * activated).astype(BF16)
        result = dot(hidden, down_h, ((1,), (0,)))
        d_row = dot(d_gate, gate_h, ((1,), (1,))) + dot(d_up, up_h, ((1,), (1,)))
        return hidden, d_gate, d_up, result, d_row

    hid_m, dg_m, du_m, res_m, dr_m = expert_half(gate_w, up_w, down_w)
    hid_o, dg_o, du_o, res_o, dr_o = expert_half(gate_o, up_o, down_o)
    d_row = (dr_m + dr_o).astype(BF16)
    result = (res_m + res_o).astype(BF16)
    back_rows = exchange(d_row.reshape(experts, capacity, width)).reshape(slots, width)
    returned = exchange(result.reshape(experts, capacity, width)).reshape(slots, width)

    def expert_grad(left_o, right_o, left_m, right_m):
        sent = dot(left_o, right_o, ((0,), (0,))).astype(BF16)
        return (dot(left_m, right_m, ((0,), (0,))) + swap(sent).astype(F32))[None]

    grad_down = expert_grad(hid_o, expert_grads, hid_m, expert_grads)
    grad_gate = expert_grad(rows_in, dg_o, rows_in, dg_m)
    grad_up = expert_grad(rows_in, du_o, rows_in, du_m)

    combine = jnp.where(place_b, weight_of.T[:, None, :], 0.0).reshape(slots, rows)
    combine_high = combine.astype(BF16)
    combine_low = (combine - combine_high.astype(F32)).astype(BF16)
    moe = dot(combine_high, returned, ((0,), (0,))) + dot(combine_low, returned, ((0,), (0,)))
    output = (hidden_in + moe).astype(BF16)
    products = dot(returned, out_grad, ((1,), (1,)))
    of_expert = jnp.sum(
        jnp.where(place_b, products.reshape(experts, capacity, rows), 0.0), axis=1
    ).T
    grad_route = jnp.sum(jnp.where(names, of_expert[:, None, :], 0.0), axis=2)

    d_mid = dot(place, back_rows, ((0,), (0,)))
    d_mid_in, grad_norm_mid = norm_back(hidden_in, mid_scale, norm_mid, d_mid)
    d_hidden_in = grad + d_mid_in
    d_attended = d_hidden_in.astype(BF16)
    d_whole = share_sequence(d_attended)
    d_mixed = (
        dot(d_whole, out_full, ((1,), (0,))).astype(BF16).reshape(length, key_heads, group, HD)
    )
    probs = jnp.exp(scores - log_total)
    d_probs = jnp.einsum("ahgd,bhd->hgab", d_mixed, value_low, preferred_element_type=F32)
    value_grad = jnp.einsum("hgab,ahgd->bhd", probs_low, d_mixed, preferred_element_type=F32)
    delta = jnp.sum(probs * d_probs, axis=-1, keepdims=True)
    d_scores = (probs * (d_probs - delta)).astype(BF16)
    d_query = (
        jnp.einsum("hgab,bhd->ahgd", d_scores, key, preferred_element_type=F32).reshape(
            length, query_heads, HD
        )
        * scale
    )
    d_key = jnp.einsum("hgab,ahgd->bhd", d_scores, query, preferred_element_type=F32) * scale
    d_query_raw, grad_query_gain = norm_back(
        query_raw, query_scale, query_gain, rotate_back(d_query, cosine, sine)
    )
    d_key_raw, grad_key_gain = norm_back(
        key_raw, key_scale, key_gain, rotate_back(d_key, cosine, sine)
    )
    d_raw = jnp.concatenate(
        [
            d_query_raw.astype(BF16).reshape(length, q_cols),
            d_key_raw.astype(BF16).reshape(length, k_cols),
            value_grad.astype(BF16).reshape(length, k_cols),
        ],
        axis=1,
    )
    d_normed = sum_sequence(dot(d_raw, in_full, ((1,), (1,))), rows)
    d_inputs, grad_norm_in = norm_back(inputs, in_scale, norm_in, d_normed)
    grad_tokens = (d_hidden_in + d_inputs).astype(BF16)

    gains = jnp.concatenate([grad_norm_in, grad_norm_mid, grad_query_gain, grad_key_gain])
    gains = lax.psum(gains, ("dp", "tensor"))
    grad_norm_in, grad_norm_mid = gains[:width], gains[width : 2 * width]
    grad_query_gain, grad_key_gain = gains[2 * width : 2 * width + HD], gains[2 * width + HD :]

    in_grads = dot(whole, d_raw, ((0,), (0,))).astype(BF16)
    out_grads = dot(d_whole, mixed, ((0,), (0,))).astype(BF16)
    partial = jnp.concatenate([in_grads, out_grads], axis=1)
    parts = exchange(partial.reshape(owners, -1, partial.shape[1]))
    total = jnp.sum(parts.astype(F32), axis=0)
    return (
        output,
        grad_tokens,
        grad_norm_in,
        total[:, :q_cols],
        total[:, q_cols : q_cols + k_cols],
        total[:, q_cols + k_cols : in_cols],
        grad_query_gain,
        grad_key_gain,
        total[:, in_cols:].T,
        grad_norm_mid,
        grad_route,
        grad_gate,
        grad_up,
        grad_down,
    )


def solution(mesh):
    tokens_spec = P(("dp", "tensor"), None)
    columns, rows = P("dp", None, "tensor"), P("dp", "tensor", None)
    proj = P("dp", "tensor")
    return jax.shard_map(
        per_device,
        mesh=mesh,
        in_specs=(
            tokens_spec,
            P("dp"),
            P(),
            proj,
            proj,
            proj,
            P(),
            P(),
            P("tensor", "dp"),
            P(),
            tokens_spec,
            tokens_spec,
            columns,
            columns,
            rows,
            tokens_spec,
        ),
        out_specs=(
            tokens_spec,
            tokens_spec,
            P(),
            proj,
            proj,
            proj,
            P(),
            P(),
            P("tensor", "dp"),
            P(),
            tokens_spec,
            columns,
            columns,
            rows,
        ),
        check_vma=False,
    )
```

time: 2750 us -> 1280 us (0.47)
  waiting for transfers between devices: 1970 us -> 575 us
  local copies, waits for them, and re-layouts: 294 us -> 86.9 us
  blocking collectives: 220 us -> 323 us
  matrix products: 150 us -> 180 us
    reduce_scatter x8 -> x0, waiting for transfers between devices: 1420 us -> none  [the longest x1 357 us: per_device(): lax.psum_scatter(grad_out_proj, 'dp', scatter_dimension=1, tiled=True)]
    ppermute x0 -> x10, waiting for transfers between devices: none -> 402 us  [swap(): return lax.ppermute(values, 'tensor', [(0, 1), (1, 0)])]
    all_gather x8 -> x1, waiting for transfers between devices: 422 us -> 100 us  [per_device(): full = lax.all_gather(shard, 'dp', axis=0, tiled=True)]
    all_to_all x1 -> x3, blocking collectives: 152 us -> 246 us  [exchange(): return lax.all_to_all(buffer, 'dp', split_axis=0, concat_axis=0, tiled=True)]
    convert_element_type x5 -> x3, local copies, waits for them, and re-layouts: 83.2 us -> 4.47 us  [the longest x1 3.44 us: per_device(): probs_low = jnp.exp(scores - log_total).astype(BF16)]
    all_to_all x3 -> x2, waiting for transfers between devices: 121 us -> 72.7 us  [exchange(): return lax.all_to_all(buffer, 'dp', split_axis=0, concat_axis=0, tiled=True)]
    gather x4 -> x0, local copies, waits for them, and re-layouts: 44.1 us -> none  [the longest x1 13.6 us: per_device(): padded_grads[route_of_slot].reshape(local_experts, owners, capacity, width)]
    all_gather x2 -> x0, local copies, waits for them, and re-layouts: 39.7 us -> none  [the longest x1 20.2 us: per_device(): gathered = lax.all_gather(expert_rows, 'tensor', axis=0, tiled=True)]
  transfers between devices with their start and end apart: 19 -> 13, of which waited for: 15 -> 10; matrix products, arithmetic and copies ran while one was open for 12% -> 8% of each run, Pallas kernels for 0% -> 0%
where the time goes in v1:
time: 1280 us; the launch traced here: 1270 us
  waiting for transfers between devices  575 us (45%)
  blocking collectives  323 us (25%)
  matrix products  180 us (14%)
  local copies, waits for them, and re-layouts  86.9 us (7%)
  other arithmetic  53.3 us (4%)
  starting transfers between devices  35.4 us (3%)
  between operations  15.5 us (1%)
    ppermute x10, waiting for transfers between devices, swap(): return lax.ppermute(values, 'tensor', [(0, 1), (1, 0)])  402 us
    all_to_all x3, blocking collectives, exchange(): return lax.all_to_all(buffer, 'dp', split_axis=0, concat_axis=0, tiled=True)  246 us
    dot_general x31, matrix products, dot(): lax.dot_general(left, right, (contract, ((), ())), preferred_element_type...  174 us
    all_gather x1, waiting for transfers between devices, per_device(): full = lax.all_gather(shard, 'dp', axis=0, tiled=True)  100 us
    psum x1, blocking collectives, per_device(): gains = lax.psum(gains, ('dp', 'tensor'))  77 us
    all_to_all x2, waiting for transfers between devices, exchange(): return lax.all_to_all(buffer, 'dp', split_axis=0, concat_axis=0, tiled=True)  72.7 us
  transfers between devices with their start and end apart: 13, of which 10 were waited for; matrix products, arithmetic and copies ran while one was open for 8% of the time, Pallas kernels for 0%

profile of v1, /device:TPU:0, one launch (start us, length us, event | category | flops | bytes accessed | tf_op | source)
XLA Modules:
  0.0 1269.2 jit_solution(12733780084653871354)
XLA Ops:
  14.5 11.3 collective-permute-done
  26.1 100.2 %all-gather.2.cloned.1.call-done = bf16[2048,4608]{1,0:T(8,128)(2,1)} async-done(((bf16[32,4608]{1,0:T(8,128)(2,1)}), bf16[2048,4608]{1,0:T(8,128)(2,1)}) %all-gather.2.cloned.1.call-update) | async-done | bytes 18874384 | tf_op jit(solution)/shard_map/all_gather | solution.py:106
  153.7 11.8 collective-permute-start.1
  170.1 9.2 collective-permute-done.1
  185.8 8.9 reshape.263
  194.8 6.8 all-to-all-start
  204.9 72.7 %all-to-all-done = bf16[64,20,2048]{2,1,0:T(8,128)(2,1)} async-done(((bf16[64,20,2048]{2,1,0:T(8,128)(2,1)}), bf16[64,20,2048]{2,1,0:T(8,128)(2,1)}, u32[]{:S(2)}, u32[]{:S(2)}) %all-to-all-start) | async-done | bytes 5242912 | tf_op jit(solution)/shard_map/all_to_all | solution.py:77
  277.6 9.0 reshape.264
  299.2 79.1 %collective-permute-done.2 = bf16[2048,384]{1,0:T(8,128)(2,1)} collective-permute-done((bf16[2048,384]{1,0:T(8,128)(2,1)}, bf16[2048,384]{1,0:T(8,128)(2,1)}, u32[]{:S(2)}, u32[]{:S(2)}) %collective-permute-start.2) | collective-permute-done | bytes 1572896 | tf_op jit(solution)/shard_map/ppermute | solution.py:58
  382.6 6.4 multiply_convert_fusion.5
  396.0 8.9 reshape.265
  404.9 84.2 %all_to_all.25 = bf16[64,20,2048]{2,1,0:T(8,128)(2,1)S(1)} all-to-all(bf16[64,20,2048]{2,1,0:T(8,128)(2,1)} %reshape.265), channel_id=1, replica_groups=mesh['dp'=64,'tensor'=2] {'dp'}, dimensions={0} | all-to-all | bytes 10485760 | tf_op jit(solution)/shard_map/all_to_all | solution.py:77
  489.2 6.8 fusion.55
  501.0 8.9 reshape.266
  509.9 80.9 %all_to_all.26 = bf16[64,20,2048]{2,1,0:T(8,128)(2,1)} all-to-all(bf16[64,20,2048]{2,1,0:T(8,128)(2,1)} %reshape.266), channel_id=1, replica_groups=mesh['dp'=64,'tensor'=2] {'dp'}, dimensions={0} | all-to-all | bytes 10485760 | tf_op jit(solution)/shard_map/all_to_all | solution.py:77
  590.9 9.0 reshape.267
  599.9 7.6 multiply_convert_fusion.3
  625.1 7.4 fusion.125
  632.5 16.2 %add_convert_fusion = bf16[1280,2048]{1,0:T(8,128)(2,1)} fusion(f32[1280,2048]{1,0:T(8,128)} %fusion.125, f32[1280,2048]{1,0:T(8,128)} %fusion.112, f32[1280,2048]{1,0:T(8,128)} %fusion.108, bf16[1280,384]{1,0:T(8,128)(2,1)} %get-tuple-element.30, bf16[2048,384]{1,0:T(8,128)(2,1)} %collective-permute-done.2), kind=kOutput, calls=%fused_computation.3 | convolution fusion | flops 2023751680 | bytes 39256064 | tf_op jit(solution)/shard_map/dot_general | solution.py:17
  648.7 8.9 reshape.268
  657.7 80.3 %all_to_all.27 = bf16[64,20,2048]{2,1,0:T(8,128)(2,1)S(1)} all-to-all(bf16[64,20,2048]{2,1,0:T(8,128)(2,1)} %reshape.268), channel_id=1, replica_groups=mesh['dp'=64,'tensor'=2] {'dp'}, dimensions={0} | all-to-all | bytes 10485760 | tf_op jit(solution)/shard_map/all_to_all | solution.py:77
  738.0 6.6 multiply_reduce_fusion.2
  751.8 8.9 collective-permute-done.5
  804.8 13.0 %pad_maximum_fusion = bf16[2048,4608]{1,0:T(8,128)(2,1)} fusion(bf16[2048,2048]{1,0:T(8,128)(2,1)} %convolution_convert_fusion.1, bf16[2048,2560]{1,0:T(8,128)(2,1)S(1)} %convolution_convert_fusion), kind=kLoop, calls=%fused_computation.1 | loop fusion | flops 37748736 | bytes 37748736 | tf_op jit(solution)/shard_map/concatenate | solution.py:251
  824.0 8.8 fusion.23
  846.5 6.8 fusion.38
  856.4 237.6 %collective-permute-done.8 = bf16[2048,384]{1,0:T(8,128)(2,1)S(1)} collective-permute-done((bf16[2048,384]{1,0:T(8,128)(2,1)S(1)}, bf16[2048,384]{1,0:T(8,128)(2,1)S(1)}, u32[]{:S(2)}, u32[]{:S(2)}) %collective-permute-start.8) | collective-permute-done | bytes 1572896 | tf_op jit(solution)/shard_map/ppermute | solution.py:58
  1098.7 29.0 %collective-permute-done.7 = bf16[2048,384]{1,0:T(8,128)(2,1)S(1)} collective-permute-done((bf16[2048,384]{1,0:T(8,128)(2,1)S(1)}, bf16[2048,384]{1,0:T(8,128)(2,1)S(1)}, u32[]{:S(2)}, u32[]{:S(2)}) %collective-permute-start.7) | collective-permute-done | bytes 1572896 | tf_op jit(solution)/shard_map/ppermute | solution.py:58
  1140.8 20.6 %collective-permute-done.9 = bf16[384,2048]{1,0:T(8,128)(2,1)S(1)} collective-permute-done((bf16[384,2048]{1,0:T(8,128)(2,1)S(1)}, bf16[384,2048]{1,0:T(8,128)(2,1)S(1)}, u32[]{:S(2)}, u32[]{:S(2)}) %collective-permute-start.9) | collective-permute-done | bytes 1572896 | tf_op jit(solution)/shard_map/ppermute | solution.py:58
  1165.4 6.6 collective-permute-done.6
  1172.5 77.0 %psum.7 = f32[4352]{0:T(1024)S(1)} all-reduce(f32[4352]{0:T(1024)S(1)} %pad_maximum_fusion.16), channel_id=1, replica_groups=mesh['dp'=64,'tensor'=2] {'dp','tensor'}, use_global_device_ids=true, to_apply=%region_20.21 | all-reduce | flops 4352 | bytes 34816 | tf_op jit(solution)/shard_map/psum | solution.py:245
  1253.1 7.6 convert_reduce_fusion
  (314 shorter events, 196.4 us)
Async XLA Ops:
  7.2 119.1 %all-gather.2.cloned.1.call-start = ((), (), s32[]{:S(2)}) async-start(), calls=%async_computation.5 | async-start | bytes 19169280 | tf_op jit(solution)/shard_map/all_gather | solution.py:106
  10.9 121.0 %copy-start.68 = (f32[128]{0:T(128)}, f32[128]{0:T(128)S(1)}, u32[]{:S(2)}) copy-start(f32[128]{0:T(128)S(1)} %get-tuple-element.67) | copy-start | bytes 1540
  12.2 13.6 %collective-permute-start = (bf16[128,2048]{1,0:T(8,128)(2,1)S(1)}, bf16[128,2048]{1,0:T(8,128)(2,1)S(1)}, u32[]{:S(2)}, u32[]{:S(2)}) collective-permute-start(bf16[128,2048]{1,0:T(8,128)(2,1)S(1)} %fusion.64), channel_id=1, source_target_pairs={{0,1},{1,0},{2,3},{3,2},{4,5},{5,4},{6,7},{7,6},{8,9},{9,8},{10,11... | collective-permute-start | bytes 1572872 | tf_op jit(solution)/shard_map/ppermute | solution.py:58
  14.5 125.4 %copy-start.22 = (f32[256,64]{1,0:T(8,128)}, f32[256,64]{1,0:T(8,128)S(1)}, u32[]{:S(2)}) copy-start(f32[256,64]{1,0:T(8,128)S(1)} %get-tuple-element.64) | copy-start | bytes 196612
  14.5 125.4 %copy-start.24 = (f32[256,64]{1,0:T(8,128)}, f32[256,64]{1,0:T(8,128)S(1)}, u32[]{:S(2)}) copy-start(f32[256,64]{1,0:T(8,128)S(1)} %get-tuple-element.65) | copy-start | bytes 196612
  26.1 105.8 %copy-start.30 = (bf16[128,2048]{1,0:T(8,128)(2,1)}, bf16[128,2048]{1,0:T(8,128)(2,1)S(1)}, u32[]{:S(2)}) copy-start(bf16[128,2048]{1,0:T(8,128)(2,1)S(1)} %get-tuple-element.44) | copy-start | bytes 1572868
  26.1 105.8 %copy-start.32 = (bf16[128,2048]{1,0:T(8,128)(2,1)}, bf16[128,2048]{1,0:T(8,128)(2,1)S(1)}, u32[]{:S(2)}) copy-start(bf16[128,2048]{1,0:T(8,128)(2,1)S(1)} %get-tuple-element.45) | copy-start | bytes 1572868
  153.7 25.6 %collective-permute-start.1 = (bf16[128,2048]{1,0:T(8,128)(2,1)}, bf16[128,2048]{1,0:T(8,128)(2,1)}, u32[]{:S(2)}, u32[]{:S(2)}) collective-permute-start(bf16[128,2048]{1,0:T(8,128)(2,1)} %dynamic-slice_convert_fusion.1), channel_id=1, source_target_pairs={{0,1},{1,0},{2,3},{3,2},{4,5},{5,4},{6,7},{7,6},{8,9},{9,8},{10,11... | collective-permute-start | bytes 1572872 | tf_op jit(solution)/shard_map/ppermute | solution.py:58
  165.6 572.4 %copy-start.59 = (s32[64,128]{1,0:T(8,128)}, s32[64,128]{1,0:T(8,128)S(1)}, u32[]{:S(2)}) copy-start(s32[64,128]{1,0:T(8,128)S(1)} %fusion.61) | copy-start | bytes 98308
  194.8 82.8 %all-to-all-start = ((bf16[64,20,2048]{2,1,0:T(8,128)(2,1)}), bf16[64,20,2048]{2,1,0:T(8,128)(2,1)}, u32[]{:S(2)}, u32[]{:S(2)}) async-start(bf16[64,20,2048]{2,1,0:T(8,128)(2,1)} %reshape.263), calls=%async_computation | async-start | bytes 12582912 | tf_op jit(solution)/shard_map/all_to_all | solution.py:77
  201.6 187.4 %collective-permute-start.4 = (bf16[384,2048]{1,0:T(8,128)(2,1)}, bf16[384,2048]{1,0:T(8,128)(2,1)}, u32[]{:S(2)}, u32[]{:S(2)}) collective-permute-start(bf16[384,2048]{1,0:T(8,128)(2,1)} %bitcast.252), channel_id=1, source_target_pairs={{0,1},{1,0},{2,3},{3,2},{4,5},{5,4},{6,7},{7,6},{8,9},{9,8},{10,11... | collective-permute-start | bytes 4718600 | tf_op jit(solution)/shard_map/ppermute | solution.py:58
  202.8 179.7 %collective-permute-start.3 = (bf16[2048,384]{1,0:T(8,128)(2,1)}, bf16[2048,384]{1,0:T(8,128)(2,1)}, u32[]{:S(2)}, u32[]{:S(2)}) collective-permute-start(bf16[2048,384]{1,0:T(8,128)(2,1)} %bitcast.254), channel_id=1, source_target_pairs={{0,1},{1,0},{2,3},{3,2},{4,5},{5,4},{6,7},{7,6},{8,9},{9,8},{10,11... | collective-permute-start | bytes 4718600 | tf_op jit(solution)/shard_map/ppermute | solution.py:58
  203.7 174.6 %collective-permute-start.2 = (bf16[2048,384]{1,0:T(8,128)(2,1)}, bf16[2048,384]{1,0:T(8,128)(2,1)}, u32[]{:S(2)}, u32[]{:S(2)}) collective-permute-start(bf16[2048,384]{1,0:T(8,128)(2,1)} %bitcast.253), channel_id=1, source_target_pairs={{0,1},{1,0},{2,3},{3,2},{4,5},{5,4},{6,7},{7,6},{8,9},{9,8},{10,11... | collective-permute-start | bytes 4718600 | tf_op jit(solution)/shard_map/ppermute | solution.py:58
  404.9 84.3 %copy-start.34 = (bf16[128,2048]{1,0:T(8,128)(2,1)S(1)}, bf16[128,2048]{1,0:T(8,128)(2,1)}, u32[]{:S(2)}) copy-start(bf16[128,2048]{1,0:T(8,128)(2,1)} %param.31) | copy-start | bytes 1572868
  657.7 80.3 %copy-start.8 = (f32[128,2048]{1,0:T(8,128)S(1)}, f32[128,2048]{1,0:T(8,128)}, u32[]{:S(2)}) copy-start(f32[128,2048]{1,0:T(8,128)} %copy-done.7) | copy-start | bytes 3145732
  657.7 80.3 %copy-start.75 = (f32[128]{0:T(128)S(1)}, f32[128]{0:T(128)}, u32[]{:S(2)}) copy-start(f32[128]{0:T(128)} %copy-done.74) | copy-start | bytes 1540
  746.2 14.5 %collective-permute-start.5 = (bf16[128,2048]{1,0:T(8,128)(2,1)}, bf16[128,2048]{1,0:T(8,128)(2,1)}, u32[]{:S(2)}, u32[]{:S(2)}) collective-permute-start(bf16[128,2048]{1,0:T(8,128)(2,1)} %get-tuple-element.22), channel_id=1, source_target_pairs={{0,1},{1,0},{2,3},{3,2},{4,5},{5,4},{6,7},{7,6},{8,9},{9,8},{10,11... | collective-permute-start | bytes 1572872 | tf_op jit(solution)/shard_map/ppermute | solution.py:58
  817.8 435.3 %all-to-all-start.4 = ((bf16[64,32,4608]{2,1,0:T(8,128)(2,1)}), bf16[64,32,4608]{2,1,0:T(8,128)(2,1)}, u32[]{:S(2)}, u32[]{:S(2)}) async-start(bf16[64,32,4608]{2,1,0:T(8,128)(2,1)} %bitcast.228), calls=%async_computation.4 | async-start | bytes 37748736 | tf_op jit(solution)/shard_map/all_to_all | solution.py:77
  838.5 255.5 %collective-permute-start.8 = (bf16[2048,384]{1,0:T(8,128)(2,1)S(1)}, bf16[2048,384]{1,0:T(8,128)(2,1)S(1)}, u32[]{:S(2)}, u32[]{:S(2)}) collective-permute-start(bf16[2048,384]{1,0:T(8,128)(2,1)S(1)} %convolution_convert_fusion.4), channel_id=1, source_target_pairs={{0,1},{1,0},{2,3},{3,2},{4,5},{5,4},{6,7},{7,6},{8,9},{9,8},{10,11... | collective-permute-start | bytes 4718600 | tf_op jit(solution)/shard_map/ppermute | solution.py:58
  844.5 283.2 %collective-permute-start.7 = (bf16[2048,384]{1,0:T(8,128)(2,1)S(1)}, bf16[2048,384]{1,0:T(8,128)(2,1)S(1)}, u32[]{:S(2)}, u32[]{:S(2)}) collective-permute-start(bf16[2048,384]{1,0:T(8,128)(2,1)S(1)} %convolution_convert_fusion.5), channel_id=1, source_target_pairs={{0,1},{1,0},{2,3},{3,2},{4,5},{5,4},{6,7},{7,6},{8,9},{9,8},{10,11... | collective-permute-start | bytes 4718600 | tf_op jit(solution)/shard_map/ppermute | solution.py:58
  846.5 247.4 %slice-start.6 = ((s8[5242880]{0:T(1024)(128)(4,1)}), s8[1048576]{0:T(1024)(128)(4,1)S(1)}, s32[]{:S(2)}) async-start(s8[5242880]{0:T(1024)(128)(4,1)} %bitcast.248), calls=%async_computation.12 | async-start | bytes 2097152
  853.3 240.6 %slice-start.7 = ((s8[5242880]{0:T(1024)(128)(4,1)}), s8[4194304]{0:T(1024)(128)(4,1)S(1)}, s32[]{:S(2)}) async-start(s8[5242880]{0:T(1024)(128)(4,1)} %bitcast.248), calls=%async_computation.13 | async-start | bytes 8388608
  853.3 240.6 %copy-start.43 = (bf16[1280,384]{1,0:T(8,128)(2,1)S(1)}, bf16[1280,384]{1,0:T(8,128)(2,1)}, u32[]{:S(2)}) copy-start(bf16[1280,384]{1,0:T(8,128)(2,1)} %copy-done.42) | copy-start | bytes 2949124
  855.7 272.0 %copy-start.41 = (bf16[1280,384]{1,0:T(8,128)(2,1)S(1)}, bf16[1280,384]{1,0:T(8,128)(2,1)}, u32[]{:S(2)}) copy-start(bf16[1280,384]{1,0:T(8,128)(2,1)} %copy-done.40) | copy-start | bytes 2949124
  855.7 305.7 %collective-permute-start.9 = (bf16[384,2048]{1,0:T(8,128)(2,1)S(1)}, bf16[384,2048]{1,0:T(8,128)(2,1)S(1)}, u32[]{:S(2)}, u32[]{:S(2)}) collective-permute-start(bf16[384,2048]{1,0:T(8,128)(2,1)S(1)} %convolution_convert_fusion.3), channel_id=1, source_target_pairs={{0,1},{1,0},{2,3},{3,2},{4,5},{5,4},{6,7},{7,6},{8,9},{9,8},{10,11... | collective-permute-start | bytes 4718600 | tf_op jit(solution)/shard_map/ppermute | solution.py:58
  1138.1 33.9 %copy-start.26 = (f32[256,2048]{1,0:T(8,128)}, f32[256,2048]{1,0:T(8,128)S(1)}, u32[]{:S(2)}) copy-start(f32[256,2048]{1,0:T(8,128)S(1)} %fusion) | copy-start | bytes 6291460
  1138.2 33.8 %copy-start.6 = (bf16[128,2048]{1,0:T(8,128)(2,1)S(1)}, bf16[128,2048]{1,0:T(8,128)(2,1)}, u32[]{:S(2)}) copy-start(bf16[128,2048]{1,0:T(8,128)(2,1)} %param.16) | copy-start | bytes 1572868
  1138.2 33.8 %copy-start.64 = (f32[2048]{0:T(1024)S(1)}, f32[2048]{0:T(1024)}, u32[]{:S(2)}) copy-start(f32[2048]{0:T(1024)} %param.18) | copy-start | bytes 24580
  1138.2 33.8 %copy-start.69 = (f32[128]{0:T(128)S(1)}, f32[128]{0:T(128)}, u32[]{:S(2)}) copy-start(f32[128]{0:T(128)} %copy-done.68) | copy-start | bytes 1540
  1138.2 33.8 %collective-permute-start.6 = (bf16[128,2048]{1,0:T(8,128)(2,1)S(1)}, bf16[128,2048]{1,0:T(8,128)(2,1)S(1)}, u32[]{:S(2)}, u32[]{:S(2)}) collective-permute-start(bf16[128,2048]{1,0:T(8,128)(2,1)S(1)} %dynamic-slice_convert_fusion), channel_id=1, source_target_pairs={{0,1},{1,0},{2,3},{3,2},{4,5},{5,4},{6,7},{7,6},{8,9},{9,8},{10,11... | collective-permute-start | bytes 1572872 | tf_op jit(solution)/shard_map/ppermute | solution.py:58
  1165.4 85.2 %copy-start.19 = (f32[128,2048]{1,0:T(8,128)S(1)}, f32[128,2048]{1,0:T(8,128)}, u32[]{:S(2)}) copy-start(f32[128,2048]{1,0:T(8,128)} %get-tuple-element.23) | copy-start | bytes 3145732
  1165.4 85.2 %copy-start.78 = (f32[128]{0:T(128)S(1)}, f32[128]{0:T(128)}, u32[]{:S(2)}) copy-start(f32[128]{0:T(128)} %get-tuple-element.66) | copy-start | bytes 1540
  (73 other events, 398.6 us)
Sparse Core Ops, SparseCore 0:
  11.8 114.4 all-gather.1

commit v2 on v1

--- a/solution.py
+++ b/solution.py
@@ -3,6 +3,8 @@
 import jax
 import jax.numpy as jnp
 from jax import lax
+from jax.experimental import pallas as pl
+from jax.experimental.pallas import tpu as pltpu
 from jax.sharding import PartitionSpec as P
 
 HD = 128
@@ -11,6 +13,403 @@
 THETA = 1000000.0
 BF16 = jnp.bfloat16
 F32 = jnp.float32
+MESH_ID = pl.DeviceIdType.MESH
+ANY_SPEC = pl.BlockSpec(memory_space=pl.ANY)
+VMEM_SPEC = pl.BlockSpec(memory_space=pltpu.VMEM)
+
+
+def coordinates():
+    dp = lax.axis_index("dp")
+    return lax.div(dp, 16), lax.rem(lax.div(dp, 8), 2), lax.rem(lax.div(dp, 2), 4), lax.rem(dp, 2)
+
+
+def device(z, x, y, core, tensor):
+    return (((z * 2 + x) * 4 + y) * 2 + core, tensor)
+
+
+def turn(at, step):
+    return lax.rem(at + step, 4)
+
+
+def send(src, dst, send_sem, recv_sem, to):
+    copy = pltpu.make_async_remote_copy(
+        src_ref=src,
+        dst_ref=dst,
+        send_sem=send_sem,
+        recv_sem=recv_sem,
+        device_id=to,
+        device_id_type=MESH_ID,
+    )
+    copy.start()
+    return copy
+
+
+def greet(peers):
+    barrier = pltpu.get_barrier_semaphore()
+    for peer in peers:
+        pl.semaphore_signal(barrier, inc=1, device_id=peer, device_id_type=MESH_ID)
+    pl.semaphore_wait(barrier, len(peers))
+
+
+STEPS = (1, 3, 2)
+
+
+def reduce_kernel(
+    ga, gb, gain, d_own, d_sent, x_hat, down, gate, up,
+    oa, ob, og, d_came, down_c, gate_c, up_c,
+    own_a, got_a, one_a, two_a, sum_a, three_a,
+    own_b, got_b, one_b, two_b, sum_b, three_b,
+    vec, vecs,
+    load_sem, core_send, core_recv, one_send, one_recv, two_send, two_recv,
+    three_send, three_recv, vec_send, vec_recv, pair_send, pair_recv,
+):
+    z, x, y, core = coordinates()
+    tensor = lax.axis_index("tensor")
+    sibling = device(z, x, y, 1 - core, tensor)
+    along_z = [device(turn(z, s), x, y, core, tensor) for s in STEPS]
+    along_y = [device(z, x, turn(y, s), core, tensor) for s in STEPS]
+    across = device(z, 1 - x, y, core, tensor)
+    near = [
+        device(z, x, y, 1 - core, tensor),
+        device(z, x, y, core, 1 - tensor),
+        device(z, x, y, 1 - core, 1 - tensor),
+    ]
+    greet(along_z + along_y + [across] + near)
+
+    vec_groups = (
+        (near, core * 2 + tensor, 4),
+        (along_z, z, 4),
+        (along_y, y, 4),
+        ([across], x, 2),
+    )
+    vec_copies = {}
+
+    def vec_start(stage):
+        peers, mine, _ = vec_groups[stage]
+        if stage == 0:
+            vec[0] = gain[...]
+            vec[0, 0:1] = jnp.sum(
+                (d_own[...] + d_came[...].astype(F32)) * x_hat[...], axis=0, keepdims=True
+            )
+        vecs[stage, mine] = vec[stage]
+        vec_copies[stage] = [
+            send(vec.at[stage], vecs.at[stage, mine], vec_send.at[stage, i], vec_recv.at[stage, i], peer)
+            for i, peer in enumerate(peers)
+        ]
+
+    def vec_finish(stage):
+        for copy in vec_copies[stage]:
+            copy.wait()
+        count = vec_groups[stage][2]
+        total = vecs[stage, 0]
+        for i in range(1, count):
+            total = total + vecs[stage, i]
+        if stage == 3:
+            og[...] = total
+        else:
+            vec[stage + 1] = total
+
+    partner = near[1]
+    d_copy = send(d_sent, d_came, pair_send.at[0], pair_recv.at[0], partner)
+
+    loads, swaps = {}, {}
+    order = STEPS + (0,)
+    for i, s in enumerate(order):
+        to = turn(z, s)
+        swaps["a", s] = send(ga.at[to, :, :, 1 - core], got_a.at[to], core_send.at[0, i], core_recv.at[0, i], sibling)
+        loads["a", s] = pltpu.make_async_copy(ga.at[to, :, :, core], own_a.at[to], load_sem.at[0, i])
+        loads["a", s].start()
+        to = turn(y, s)
+        swaps["b", s] = send(gb.at[:, :, to, 1 - core], got_b.at[to], core_send.at[1, i], core_recv.at[1, i], sibling)
+        loads["b", s] = pltpu.make_async_copy(gb.at[:, :, to, core], own_b.at[to], load_sem.at[1, i])
+        loads["b", s].start()
+
+    def add_cores(own, got, to):
+        shape = own.shape
+
+        @pl.loop(0, shape[1])
+        def _(i):
+            @pl.loop(0, shape[2])
+            def _(j):
+                own[to, i, j] = (own[to, i, j].astype(F32) + got[to, i, j].astype(F32)).astype(BF16)
+
+    d_copy.wait_recv()
+    vec_start(0)
+    expert = [
+        send(down, down_c, pair_send.at[1], pair_recv.at[1], partner),
+        send(gate, gate_c, pair_send.at[2], pair_recv.at[2], partner),
+    ]
+
+    ones = []
+    for i, s in enumerate(order):
+        loads["a", s].wait()
+        swaps["a", s].wait_recv()
+        add_cores(own_a, got_a, turn(z, s))
+        if s:
+            ones.append(send(own_a.at[turn(z, s)], one_a.at[i], one_send.at[0, i], one_recv.at[0, i], along_z[i]))
+        loads["b", s].wait()
+        swaps["b", s].wait_recv()
+        add_cores(own_b, got_b, turn(y, s))
+        if s:
+            ones.append(send(own_b.at[turn(y, s)], one_b.at[i], one_send.at[1, i], one_recv.at[1, i], along_y[i]))
+    vec_finish(0)
+    vec_start(1)
+
+    for copy in ones:
+        copy.wait_recv()
+    vec_finish(1)
+    vec_start(2)
+    twos = []
+    for i, s in enumerate(order):
+        to = turn(y, s)
+        for k in range(2):
+            sum_a[to, k] = (
+                own_a[z, k, to].astype(F32) + one_a[0, k, to].astype(F32)
+                + one_a[1, k, to].astype(F32) + one_a[2, k, to].astype(F32)
+            ).astype(BF16)
+        if s:
+            twos.append(send(sum_a.at[to], two_a.at[i], two_send.at[0, i], two_recv.at[0, i], along_y[i]))
+        to = turn(z, s)
+        for k in range(2):
+            sum_b[to, k] = (
+                own_b[y, to, k].astype(F32) + one_b[0, to, k].astype(F32)
+                + one_b[1, to, k].astype(F32) + one_b[2, to, k].astype(F32)
+            ).astype(BF16)
+        if s:
+            twos.append(send(sum_b.at[to], two_b.at[i], two_send.at[1, i], two_recv.at[1, i], along_z[i]))
+
+    for copy in twos:
+        copy.wait_recv()
+    vec_finish(2)
+    vec_start(3)
+
+    def last(sums, two, at, k):
+        return (
+            sums[at, k].astype(F32) + two[0, k].astype(F32) + two[1, k].astype(F32) + two[2, k].astype(F32)
+        )
+
+    three_a[0] = last(sum_a, two_a, y, 1 - x).astype(BF16)
+    final_a = send(three_a.at[0], three_a.at[1], three_send.at[0], three_recv.at[0], across)
+    three_b[0] = last(sum_b, two_b, z, 1 - x).astype(BF16)
+    final_b = send(three_b.at[0], three_b.at[1], three_send.at[1], three_recv.at[1], across)
+    expert.append(send(up, up_c, pair_send.at[3], pair_recv.at[3], partner))
+    mine_a = last(sum_a, two_a, y, x)
+    final_a.wait_recv()
+    oa[...] = mine_a + three_a[1].astype(F32)
+    mine_b = last(sum_b, two_b, z, x)
+    final_b.wait_recv()
+    ob[...] = mine_b + three_b[1].astype(F32)
+    vec_finish(3)
+    for copy in expert:
+        copy.wait_recv()
+    for copy in list(swaps.values()) + ones + twos + [final_a, final_b, d_copy] + expert:
+        copy.wait_send()
+
+
+def reduce_grads(in_grads, out_grads, gains, d_own, d_sent, x_hat, expert):
+    owners = lax.axis_size("dp")
+    rows = in_grads.shape[0] // owners
+    a_cols, b_cols = in_grads.shape[1], out_grads.shape[1]
+    dma = pltpu.SemaphoreType.DMA
+    vmem = pltpu.VMEM
+
+    def scratch(cols, inner):
+        return [
+            vmem((4,) + inner + (rows, cols), BF16),
+            vmem((4,) + inner + (rows, cols), BF16),
+            vmem((3,) + inner + (rows, cols), BF16),
+            vmem((3, 2, rows, cols), BF16),
+            vmem((4, 2, rows, cols), BF16),
+            vmem((2, rows, cols), BF16),
+        ]
+
+    return pl.pallas_call(
+        reduce_kernel,
+        out_shape=(
+            jax.ShapeDtypeStruct((rows, a_cols), F32),
+            jax.ShapeDtypeStruct((rows, b_cols), F32),
+            jax.ShapeDtypeStruct(gains.shape, F32),
+            jax.ShapeDtypeStruct(d_sent.shape, BF16),
+            *[jax.ShapeDtypeStruct(half.shape, BF16) for half in expert],
+        ),
+        in_specs=[ANY_SPEC] * 2 + [VMEM_SPEC] * 4 + [ANY_SPEC] * 3,
+        out_specs=[VMEM_SPEC] * 4 + [ANY_SPEC] * 3,
+        scratch_shapes=scratch(a_cols, (2, 4))
+        + scratch(b_cols, (4, 2))
+        + [
+            vmem((4,) + gains.shape, F32),
+            vmem((4, 4) + gains.shape, F32),
+            dma((2, 4)),
+            dma((2, 4)),
+            dma((2, 4)),
+            dma((2, 3)),
+            dma((2, 3)),
+            dma((2, 3)),
+            dma((2, 3)),
+            dma((2,)),
+            dma((2,)),
+            dma((4, 3)),
+            dma((4, 3)),
+            dma((4,)),
+            dma((4,)),
+        ],
+        compiler_params=pltpu.CompilerParams(
+            collective_id=1, has_side_effects=True, vmem_limit_bytes=56 * 1024 * 1024
+        ),
+        cost_estimate=pl.CostEstimate(flops=10_000_000, bytes_accessed=300_000_000, transcendentals=0),
+    )(
+        in_grads.reshape(4, 2, 4, 2, rows, a_cols),
+        out_grads.reshape(4, 2, 4, 2, rows, b_cols),
+        gains,
+        d_own,
+        d_sent,
+        x_hat,
+        *expert,
+    )
+
+
+def ring(view, at, up, down, sends, recvs, arrived):
+    both = pl.ds(0, 2)
+
+    def start(place, half, i, to):
+        block = view(place, half)
+        return send(block, block, sends.at[i], recvs.at[i], to)
+
+    copies = [start(at, both, 0, up), start(at, both, 1, down)]
+    yield copies
+    copies[0].wait_recv()
+    copies.append(start(turn(at, 3), 0, 2, up))
+    arrived(turn(at, 3))
+    yield
+    copies[1].wait_recv()
+    copies.append(start(turn(at, 1), 1, 3, down))
+    arrived(turn(at, 1))
+    yield
+    copies[2].wait_recv()
+    copies[3].wait_recv()
+    arrived(turn(at, 2))
+    yield
+
+
+def together(*rings):
+    copies = [next(r) for r in rings]
+    for _ in range(3):
+        for r in rings:
+            next(r)
+    return [c for group in copies for c in group]
+
+
+def gather_kernel(
+    sa, sb, part, down, gate, up, fa, fb, whole, down_o, gate_o, up_o,
+    keep_sem, x_send, x_recv, one_send, one_recv, two_send, two_recv, core_send, core_recv, pair_send, pair_recv,
+):
+    z, x, y, core = coordinates()
+    tensor = lax.axis_index("tensor")
+    sibling = device(z, x, y, 1 - core, tensor)
+    across = device(z, 1 - x, y, core, tensor)
+    partner = device(z, x, y, core, 1 - tensor)
+    around_z = device(turn(z, 1), x, y, core, tensor), device(turn(z, 3), x, y, core, tensor)
+    around_y = device(z, x, turn(y, 1), core, tensor), device(z, x, turn(y, 3), core, tensor)
+    greet([sibling, across, partner, *around_z, *around_y])
+
+    pair = send(part, whole.at[tensor], pair_send.at[0], pair_recv.at[0], partner)
+    a_own, b_own = fa.at[z, x, y, core], fb.at[z, x, y, core]
+    over = [
+        send(sa, a_own, x_send.at[0], x_recv.at[0], across),
+        send(sb, b_own, x_send.at[1], x_recv.at[1], across),
+    ]
+    expert = [
+        send(src, dst, pair_send.at[i], pair_recv.at[i], partner)
+        for i, (src, dst) in enumerate(((down, down_o), (gate, gate_o), (up, up_o)), 1)
+    ]
+    keep = [
+        pltpu.make_async_copy(part, whole.at[tensor], keep_sem.at[0]),
+        pltpu.make_async_copy(sa, a_own, keep_sem.at[1]),
+        pltpu.make_async_copy(sb, b_own, keep_sem.at[2]),
+    ]
+    for copy in keep:
+        copy.start()
+    keep[1].wait()
+    keep[2].wait()
+    over[0].wait_recv()
+    over[1].wait_recv()
+
+    def skip(place):
+        return None
+
+    small = together(
+        ring(lambda i, h: fa.at[z, h, i, core], y, *around_y, one_send.at[0], one_recv.at[0], skip),
+        ring(lambda i, h: fb.at[i, h, y, core], z, *around_z, one_send.at[1], one_recv.at[1], skip),
+    )
+    cores = []
+
+    def hand_on(view):
+        def arrived(place):
+            block, k = view(place, pl.ds(0, 2)), len(cores)
+            cores.append(send(block, block, core_send.at[k], core_recv.at[k], sibling))
+
+        return arrived
+
+    def view_a(i, h):
+        return fa.at[i, h, :, core]
+
+    def view_b(i, h):
+        return fb.at[:, h, i, core]
+
+    large = [
+        ring(view_a, z, *around_z, two_send.at[0], two_recv.at[0], hand_on(view_a)),
+        ring(view_b, y, *around_y, two_send.at[1], two_recv.at[1], hand_on(view_b)),
+    ]
+    copies = [next(r) for r in large]
+    hand_on(view_a)(z)
+    hand_on(view_b)(y)
+    for _ in range(3):
+        for r in large:
+            next(r)
+    keep[0].wait()
+    pair.wait_recv()
+    for copy in cores + expert:
+        copy.wait_recv()
+    for copy in expert + [pair] + over + small + copies[0] + copies[1] + cores:
+        copy.wait_send()
+
+
+def gather_weights(in_shard, out_shard, part, expert):
+    owners = lax.axis_size("dp")
+    (rows, a_cols), b_cols = in_shard.shape, out_shard.shape[1]
+    dma = pltpu.SemaphoreType.DMA
+    in_full, out_full, whole, *other = pl.pallas_call(
+        gather_kernel,
+        out_shape=(
+            jax.ShapeDtypeStruct((4, 2, 4, 2, rows, a_cols), BF16),
+            jax.ShapeDtypeStruct((4, 2, 4, 2, rows, b_cols), BF16),
+            jax.ShapeDtypeStruct((2,) + part.shape, BF16),
+            *[jax.ShapeDtypeStruct(w.shape, BF16) for w in expert],
+        ),
+        in_specs=[ANY_SPEC] * 6,
+        out_specs=[ANY_SPEC] * 6,
+        scratch_shapes=[
+            dma((3,)),
+            dma((2,)),
+            dma((2,)),
+            dma((2, 4)),
+            dma((2, 4)),
+            dma((2, 4)),
+            dma((2, 4)),
+            dma((8,)),
+            dma((8,)),
+            dma((4,)),
+            dma((4,)),
+        ],
+        compiler_params=pltpu.CompilerParams(collective_id=2, has_side_effects=True),
+        cost_estimate=pl.CostEstimate(flops=0, bytes_accessed=250_000_000, transcendentals=0),
+    )(in_shard, out_shard, part, *expert)
+    return (
+        in_full.reshape(owners * rows, a_cols),
+        out_full.reshape(owners * rows, b_cols),
+        whole.reshape(-1, part.shape[1]),
+        other,
+    )
 
 
 def dot(left, right, contract):
@@ -66,11 +465,17 @@
     )
 
 
+def halves_of(total, rows):
+    mine = lax.axis_index("tensor") * rows
+    return (
+        lax.dynamic_slice_in_dim(total, mine, rows, 0),
+        lax.dynamic_slice_in_dim(total, rows - mine, rows, 0),
+    )
+
+
 def sum_sequence(total, rows):
-    mine = lax.axis_index("tensor") * rows
-    own = lax.dynamic_slice_in_dim(total, mine, rows, 0)
-    sent = lax.dynamic_slice_in_dim(total, rows - mine, rows, 0).astype(BF16)
-    return own + swap(sent).astype(F32)
+    own, sent = halves_of(total, rows)
+    return own + swap(sent.astype(BF16)).astype(F32)
 
 
 def exchange(buffer):
@@ -102,16 +507,19 @@
     slots = experts * capacity
     scale = HD ** (-0.5)
 
-    shard = jnp.concatenate([query_weight, key_weight, value_weight, out_weight.T], axis=1)
-    full = lax.all_gather(shard, "dp", axis=0, tiled=True)
+    inputs = tokens.astype(F32)
+    in_scale = rms_scale(inputs)
+    normed = (inputs * in_scale * norm_in).astype(BF16)
+    gate_w, up_w, down_w = gate_weight[0], up_weight[0], down_weight[0]
+    in_full, out_full, whole, (down_o, gate_o, up_o) = gather_weights(
+        jnp.concatenate([query_weight, key_weight, value_weight], axis=1),
+        out_weight.T,
+        normed,
+        (down_w, gate_w, up_w),
+    )
     q_cols, k_cols = query_weight.shape[1], key_weight.shape[1]
-    in_cols = q_cols + 2 * k_cols
-    in_full, out_full = full[:, :in_cols], full[:, in_cols:]
     query_heads, key_heads = q_cols // HD, k_cols // HD
     group = query_heads // key_heads
-
-    gate_w, up_w, down_w = gate_weight[0], up_weight[0], down_weight[0]
-    down_o, gate_o, up_o = swap(down_w), swap(gate_w), swap(up_w)
 
     names = routed_experts[:, :, None] == jnp.arange(experts, dtype=jnp.int32)
     chosen = jnp.any(names, axis=1)
@@ -125,12 +533,9 @@
 
     grad = out_grad.astype(F32)
     d_rows = (dot(place, out_grad, ((1,), (0,))) * slot_weight[:, None]).astype(BF16)
+    d_rows, whole = lax.optimization_barrier((d_rows, whole))
     expert_grads = exchange(d_rows.reshape(experts, capacity, width)).reshape(slots, width)
 
-    inputs = tokens.astype(F32)
-    in_scale = rms_scale(inputs)
-    normed = (inputs * in_scale * norm_in).astype(BF16)
-    whole = share_sequence(normed)
     length = whole.shape[0]
     cosine, sine = rope_tables(positions, HD)
     raw = dot(whole, in_full, ((1,), (0,)))
@@ -162,6 +567,7 @@
     normed_mid = (hidden_in * mid_scale * norm_mid).astype(BF16)
 
     send_rows = dot(place, normed_mid, ((1,), (0,))).astype(BF16)
+    send_rows, expert_grads = lax.optimization_barrier((send_rows, expert_grads))
     rows_in = exchange(send_rows.reshape(experts, capacity, width)).reshape(slots, width)
 
     def expert_half(gate_h, up_h, down_h):
@@ -182,16 +588,51 @@
     d_row = (dr_m + dr_o).astype(BF16)
     result = (res_m + res_o).astype(BF16)
     back_rows = exchange(d_row.reshape(experts, capacity, width)).reshape(slots, width)
+    halves = ((hid_m, expert_grads), (rows_in, dg_m), (rows_in, du_m))
+    sent = [
+        dot(left, right, ((0,), (0,))).astype(BF16)
+        for left, right in ((hid_o, expert_grads), (rows_in, dg_o), (rows_in, du_o))
+    ]
+
+    d_mid = dot(place, back_rows, ((0,), (0,)))
+    d_mid_in, grad_norm_mid = norm_back(hidden_in, mid_scale, norm_mid, d_mid)
+    d_hidden_in = grad + d_mid_in
+    d_attended = d_hidden_in.astype(BF16)
+    d_whole = share_sequence(d_attended)
+    d_whole, result = lax.optimization_barrier((d_whole, result))
+    d_mixed = (
+        dot(d_whole, out_full, ((1,), (0,))).astype(BF16).reshape(length, key_heads, group, HD)
+    )
+    probs = jnp.exp(scores - log_total)
+    d_probs = jnp.einsum("ahgd,bhd->hgab", d_mixed, value_low, preferred_element_type=F32)
+    value_grad = jnp.einsum("hgab,ahgd->bhd", probs_low, d_mixed, preferred_element_type=F32)
+    delta = jnp.sum(probs * d_probs, axis=-1, keepdims=True)
+    d_scores = (probs * (d_probs - delta)).astype(BF16)
+    d_query = (
+        jnp.einsum("hgab,bhd->ahgd", d_scores, key, preferred_element_type=F32).reshape(
+            length, query_heads, HD
+        )
+        * scale
+    )
+    d_key = jnp.einsum("hgab,ahgd->bhd", d_scores, query, preferred_element_type=F32) * scale
+    d_query_raw, grad_query_gain = norm_back(
+        query_raw, query_scale, query_gain, rotate_back(d_query, cosine, sine)
+    )
+    d_key_raw, grad_key_gain = norm_back(
+        key_raw, key_scale, key_gain, rotate_back(d_key, cosine, sine)
+    )
+    d_raw = jnp.concatenate(
+        [
+            d_query_raw.astype(BF16).reshape(length, q_cols),
+            d_key_raw.astype(BF16).reshape(length, k_cols),
+            value_grad.astype(BF16).reshape(length, k_cols),
+        ],
+        axis=1,
+    )
+    d_total = dot(d_raw, in_full, ((1,), (1,)))
+    d_own, d_sent = halves_of(d_total, rows)
+
     returned = exchange(result.reshape(experts, capacity, width)).reshape(slots, width)
-
-    def expert_grad(left_o, right_o, left_m, right_m):
-        sent = dot(left_o, right_o, ((0,), (0,))).astype(BF16)
-        return (dot(left_m, right_m, ((0,), (0,))) + swap(sent).astype(F32))[None]
-
-    grad_down = expert_grad(hid_o, expert_grads, hid_m, expert_grads)
-    grad_gate = expert_grad(rows_in, dg_o, rows_in, dg_m)
-    grad_up = expert_grad(rows_in, du_o, rows_in, du_m)
-
     combine = jnp.where(place_b, weight_of.T[:, None, :], 0.0).reshape(slots, rows)
     combine_high = combine.astype(BF16)
     combine_low = (combine - combine_high.astype(F32)).astype(BF16)
@@ -203,64 +644,34 @@
     ).T
     grad_route = jnp.sum(jnp.where(names, of_expert[:, None, :], 0.0), axis=2)
 
-    d_mid = dot(place, back_rows, ((0,), (0,)))
-    d_mid_in, grad_norm_mid = norm_back(hidden_in, mid_scale, norm_mid, d_mid)
-    d_hidden_in = grad + d_mid_in
-    d_attended = d_hidden_in.astype(BF16)
-    d_whole = share_sequence(d_attended)
-    d_mixed = (
-        dot(d_whole, out_full, ((1,), (0,))).astype(BF16).reshape(length, key_heads, group, HD)
-    )
-    probs = jnp.exp(scores - log_total)
-    d_probs = jnp.einsum("ahgd,bhd->hgab", d_mixed, value_low, preferred_element_type=F32)
-    value_grad = jnp.einsum("hgab,ahgd->bhd", probs_low, d_mixed, preferred_element_type=F32)
-    delta = jnp.sum(probs * d_probs, axis=-1, keepdims=True)
-    d_scores = (probs * (d_probs - delta)).astype(BF16)
-    d_query = (
-        jnp.einsum("hgab,bhd->ahgd", d_scores, key, preferred_element_type=F32).reshape(
-            length, query_heads, HD
-        )
-        * scale
-    )
-    d_key = jnp.einsum("hgab,ahgd->bhd", d_scores, query, preferred_element_type=F32) * scale
-    d_query_raw, grad_query_gain = norm_back(
-        query_raw, query_scale, query_gain, rotate_back(d_query, cosine, sine)
-    )
-    d_key_raw, grad_key_gain = norm_back(
-        key_raw, key_scale, key_gain, rotate_back(d_key, cosine, sine)
-    )
-    d_raw = jnp.concatenate(
-        [
-            d_query_raw.astype(BF16).reshape(length, q_cols),
-            d_key_raw.astype(BF16).reshape(length, k_cols),
-            value_grad.astype(BF16).reshape(length, k_cols),
-        ],
-        axis=1,
-    )
-    d_normed = sum_sequence(dot(d_raw, in_full, ((1,), (1,))), rows)
-    d_inputs, grad_norm_in = norm_back(inputs, in_scale, norm_in, d_normed)
-    grad_tokens = (d_hidden_in + d_inputs).astype(BF16)
-
-    gains = jnp.concatenate([grad_norm_in, grad_norm_mid, grad_query_gain, grad_key_gain])
-    gains = lax.psum(gains, ("dp", "tensor"))
-    grad_norm_in, grad_norm_mid = gains[:width], gains[width : 2 * width]
-    grad_query_gain, grad_key_gain = gains[2 * width : 2 * width + HD], gains[2 * width + HD :]
-
     in_grads = dot(whole, d_raw, ((0,), (0,))).astype(BF16)
     out_grads = dot(d_whole, mixed, ((0,), (0,))).astype(BF16)
-    partial = jnp.concatenate([in_grads, out_grads], axis=1)
-    parts = exchange(partial.reshape(owners, -1, partial.shape[1]))
-    total = jnp.sum(parts.astype(F32), axis=0)
+    gains = jnp.pad(
+        jnp.stack([grad_norm_mid, jnp.pad(jnp.concatenate([grad_query_gain, grad_key_gain]), (0, width - 2 * HD))]),
+        ((1, 5), (0, 0)),
+    )
+    in_total, out_total, gains, d_came, *came = reduce_grads(
+        in_grads, out_grads, gains, d_own, d_sent.astype(BF16), inputs * in_scale, sent
+    )
+    d_normed = d_own + d_came.astype(F32)
+    d_inputs, _ = norm_back(inputs, in_scale, norm_in, d_normed)
+    grad_tokens = (d_hidden_in + d_inputs).astype(BF16)
+    grad_down, grad_gate, grad_up = [
+        (dot(left, right, ((0,), (0,))) + half.astype(F32))[None]
+        for (left, right), half in zip(halves, came)
+    ]
+    grad_norm_in, grad_norm_mid = gains[0], gains[1]
+    grad_query_gain, grad_key_gain = gains[2, :HD], gains[2, HD : 2 * HD]
     return (
         output,
         grad_tokens,
         grad_norm_in,
-        total[:, :q_cols],
-        total[:, q_cols : q_cols + k_cols],
-        total[:, q_cols + k_cols : in_cols],
+        in_total[:, :q_cols],
+        in_total[:, q_cols : q_cols + k_cols],
+        in_total[:, q_cols + k_cols :],
         grad_query_gain,
         grad_key_gain,
-        total[:, in_cols:].T,
+        out_total.T,
         grad_norm_mid,
         grad_route,
         grad_gate,

time: 1280 us -> 835 us (0.65)
  waiting for transfers between devices: 575 us -> 185 us
  blocking collectives: 323 us -> 0 us
  Pallas kernels: 0 us -> 291 us
  other arithmetic: 53.3 us -> 30.9 us
  between operations: 15.5 us -> 2.19 us
    ppermute x10 -> x2, waiting for transfers between devices: 402 us -> 68.6 us  [swap(): return lax.ppermute(values, 'tensor', [(0, 1), (1, 0)])]
    pallas_call x0 -> x2, Pallas kernels: none -> 291 us  [the longest x1 166 us: reduce_grads(): pl.pallas_call(reduce_kernel, out_shape=(jax.ShapeDtypeStruct((rows, a_co...]
    all_to_all x3 -> x0, blocking collectives: 246 us -> none  [exchange(): return lax.all_to_all(buffer, 'dp', split_axis=0, concat_axis=0, tiled=True)]
    all_gather x1 -> x0, waiting for transfers between devices: 100 us -> none  [per_device(): full = lax.all_gather(shard, 'dp', axis=0, tiled=True)]
    psum x1 -> x0, blocking collectives: 77 us -> none  [per_device(): gains = lax.psum(gains, ('dp', 'tensor'))]
    all_to_all x2 -> x4, waiting for transfers between devices: 72.7 us -> 117 us  [exchange(): return lax.all_to_all(buffer, 'dp', split_axis=0, concat_axis=0, tiled=True)]
    all_to_all x2 -> x4, starting transfers between devices: 13 us -> 40.1 us  [exchange(): return lax.all_to_all(buffer, 'dp', split_axis=0, concat_axis=0, tiled=True)]
    ppermute x10 -> x2, starting transfers between devices: 22.4 us -> 0.76 us  [swap(): return lax.ppermute(values, 'tensor', [(0, 1), (1, 0)])]
  transfers between devices with their start and end apart: 13 -> 6, of which waited for: 10 -> 4; matrix products, arithmetic and copies ran while one was open for 8% -> 16% of each run, Pallas kernels for 0% -> 20%
where the time goes in v2:
time: 835 us; the launch traced here: 825 us
  Pallas kernels  291 us (35%)
  waiting for transfers between devices  185 us (22%)
  matrix products  181 us (22%)
  local copies, waits for them, and re-layouts  93 us (11%)
  starting transfers between devices  40.8 us (5%)
  other arithmetic  30.9 us (4%)
    dot_general x31, matrix products, dot(): lax.dot_general(left, right, (contract, ((), ())), preferred_element_type...  171 us
    pallas_call x1, Pallas kernels, reduce_grads(): pl.pallas_call(reduce_kernel, out_shape=(jax.ShapeDtypeStruct((rows, a_co...  166 us
    pallas_call x1, Pallas kernels, gather_weights(): pl.pallas_call(gather_kernel, out_shape=(jax.ShapeDtypeStruct((4, 2, 4, 2...  126 us
    all_to_all x4, waiting for transfers between devices, exchange(): return lax.all_to_all(buffer, 'dp', split_axis=0, concat_axis=0, tiled=True)  117 us
    ppermute x2, waiting for transfers between devices, swap(): return lax.ppermute(values, 'tensor', [(0, 1), (1, 0)])  68.6 us
    all_to_all x4, starting transfers between devices, exchange(): return lax.all_to_all(buffer, 'dp', split_axis=0, concat_axis=0, tiled=True)  40.1 us
  transfers between devices with their start and end apart: 6, of which 4 were waited for; matrix products, arithmetic and copies ran while one was open for 16% of the time, Pallas kernels for 20%

profile of v2, /device:TPU:0, one launch (start us, length us, event | category | flops | bytes accessed | tf_op | source)
XLA Modules:
  0.0 824.5 jit_solution(11441573759744869724)
XLA Ops:
  9.5 125.6 %shard_map.263 = (bf16[4,2,4,2,32,2560]{5,4,3,2,1,0:T(8,128)(2,1)}, bf16[4,2,4,2,32,2048]{5,4,3,2,1,0:T(8,128)(2,1)}, bf16[2,128,2048]{2,1,0:T(8,128)(2,1)}, bf1...) custom-call(bf16[32,2560]{1,0:T(8,128)(2,1)} %pad_maximum_fusion.7.sa, ...), custom_call_target="tpu_custom_call" | custom-call | bytes 250000000 | tf_op jit(solution)/shard_map/pallas_call | solution.py:381
  135.1 8.9 %reshape.278 = bf16[64,20,2048]{2,1,0:T(8,128)(2,1)} reshape(bf16[1280,2048]{1,0:T(8,128)(2,1)} %multiply_convert_fusion) | data formatting | bytes 10485760 | tf_op jit(solution)/shard_map/reshape | solution.py:537
  144.0 9.4 %all-to-all-start = ((bf16[64,20,2048]{2,1,0:T(8,128)(2,1)}), bf16[64,20,2048]{2,1,0:T(8,128)(2,1)}, u32[]{:S(2)}, u32[]{:S(2)}) async-start(bf16[64,20,2048]{2,1,0:T(8,128)(2,1)} %reshape.278), calls=%async_computation | async-start | bytes 12582912 | tf_op jit(solution)/shard_map/all_to_all | solution.py:482
  153.5 5.6 fusion.105
  179.0 61.3 %collective-permute-done = bf16[128,2048]{1,0:T(8,128)(2,1)} collective-permute-done((bf16[128,2048]{1,0:T(8,128)(2,1)}, bf16[128,2048]{1,0:T(8,128)(2,1)}, u32[]{:S(2)}, u32[]{:S(2)}) %collective-permute-start) | collective-permute-done | bytes 524320 | tf_op jit(solution)/shard_map/ppermute | solution.py:457
  247.0 9.0 %reshape.279 = bf16[1280,2048]{1,0:T(8,128)(2,1)} reshape(bf16[64,20,2048]{2,1,0:T(8,128)(2,1)} %all-to-all-done) | data formatting | bytes 10485760 | tf_op jit(solution)/shard_map/reshape | solution.py:537
  256.0 8.9 %reshape.280 = bf16[64,20,2048]{2,1,0:T(8,128)(2,1)} reshape(bf16[1280,2048]{1,0:T(8,128)(2,1)} %convolution_convert_fusion.2) | data formatting | bytes 10485760 | tf_op jit(solution)/shard_map/reshape | solution.py:571
  264.9 8.3 %all-to-all-start.1 = ((bf16[64,20,2048]{2,1,0:T(8,128)(2,1)}), bf16[64,20,2048]{2,1,0:T(8,128)(2,1)}, u32[]{:S(2)}, u32[]{:S(2)}) async-start(bf16[64,20,2048]{2,1,0:T(8,128)(2,1)} %reshape.280), calls=%async_computation.1 | async-start | bytes 12582912 | tf_op jit(solution)/shard_map/all_to_all | solution.py:482
  273.3 7.3 fusion.96
  284.8 64.0 %all-to-all-done.1 = bf16[64,20,2048]{2,1,0:T(8,128)(2,1)} async-done(((bf16[64,20,2048]{2,1,0:T(8,128)(2,1)}), bf16[64,20,2048]{2,1,0:T(8,128)(2,1)}, u32[]{:S(2)}, u32[]{:S(2)}) %all-to-all-start.1) | async-done | bytes 5242912 | tf_op jit(solution)/shard_map/all_to_all | solution.py:482
  348.8 9.0 %reshape.281 = bf16[1280,2048]{1,0:T(8,128)(2,1)} reshape(bf16[64,20,2048]{2,1,0:T(8,128)(2,1)} %all-to-all-done.1) | data formatting | bytes 10485760 | tf_op jit(solution)/shard_map/reshape | solution.py:571
  357.8 5.4 fusion.92
  371.7 5.8 fusion.109
  382.1 5.4 fusion.90
  387.5 5.4 fusion.86
  393.0 14.5 %add_convert_fusion.1 = bf16[1280,2048]{1,0:T(8,128)(2,1)} fusion(f32[1280,2048]{1,0:T(8,128)} %fusion.109, f32[1280,2048]{1,0:T(8,128)} %fusion.90, f32[1280,2048]{1,0:T(8,128)} %fusion.86, bf16[1280,384]{1,0:T(8,128)(2,1)S(1)} %get-tuple-element.66, bf16[2048,384]{1,0:T(8,128)(2,1)} %get-tuple-element.41), kind=kOutput, calls=%fused_computation.2 | convolution fusion | flops 2023751680 | bytes 39256064 | tf_op jit(solution)/shard_map/dot_general | solution.py:416
  407.5 8.9 %reshape.282 = bf16[64,20,2048]{2,1,0:T(8,128)(2,1)} reshape(bf16[1280,2048]{1,0:T(8,128)(2,1)} %add_convert_fusion.1) | data formatting | bytes 10485760 | tf_op jit(solution)/shard_map/reshape | solution.py:590
  416.4 11.7 %all-to-all-start.2 = ((bf16[64,20,2048]{2,1,0:T(8,128)(2,1)}), bf16[64,20,2048]{2,1,0:T(8,128)(2,1)}, u32[]{:S(2)}, u32[]{:S(2)}) async-start(bf16[64,20,2048]{2,1,0:T(8,128)(2,1)} %reshape.282), calls=%async_computation.2 | async-start | bytes 12582912 | tf_op jit(solution)/shard_map/all_to_all | solution.py:482
  450.8 52.9 %all-to-all-done.2 = bf16[64,20,2048]{2,1,0:T(8,128)(2,1)} async-done(((bf16[64,20,2048]{2,1,0:T(8,128)(2,1)}), bf16[64,20,2048]{2,1,0:T(8,128)(2,1)}, u32[]{:S(2)}, u32[]{:S(2)}) %all-to-all-start.2) | async-done | bytes 5242912 | tf_op jit(solution)/shard_map/all_to_all | solution.py:482
  503.7 8.9 %multiply_reduce_fusion.2 = (f32[2048]{0:T(1024)S(1)}, f32[128]{0:T(128)S(1)}, f32[128,2048]{1,0:T(8,128)S(1)}) fusion(f32[128,2048]{1,0:T(8,128)S(1)} %copy-done.5, f32[128]{0:T(128)} %copy-done.77, f32[2048]{0:T(1024)S(1)} %copy-done.69, bf16[64,20,2048]{2,1,0:T(8,128)(2,1)} %all-to-all-done.2, s32[64,128]{1,0:T(8,128)S(1)} %fusion.48), kind=kOutput, calls=%fused_computation.98 | convolution fusion | flops 672823168 | bytes 7390208 | tf_op jit(solution)/shard_map/dot_general | solution.py:416
  514.4 6.1 convolution_convert_fusion.5.down
  520.5 7.3 collective-permute-done.1
  537.9 5.7 convolution_convert_fusion.1
  543.6 8.9 %reshape.283 = bf16[64,20,2048]{2,1,0:T(8,128)(2,1)} reshape(bf16[1280,2048]{1,0:T(8,128)(2,1)} %add_convert_fusion) | data formatting | bytes 10485760 | tf_op jit(solution)/shard_map/reshape | solution.py:635
  552.5 10.6 %all-to-all-start.3 = ((bf16[64,20,2048]{2,1,0:T(8,128)(2,1)}), bf16[64,20,2048]{2,1,0:T(8,128)(2,1)}, u32[]{:S(2)}, u32[]{:S(2)}) async-start(bf16[64,20,2048]{2,1,0:T(8,128)(2,1)} %reshape.283), calls=%async_computation.3 | async-start | bytes 12582912 | tf_op jit(solution)/shard_map/all_to_all | solution.py:482
  590.2 5.6 fusion.58
  598.4 5.9 convolution_convert_fusion
  604.3 165.6 %shard_map.264 = (f32[32,2560]{1,0:T(8,128)}, f32[32,2048]{1,0:T(8,128)}, f32[8,2048]{1,0:T(8,128)}, bf16[128,2048]{1,0:T(8,128)(2,1)}, bf16[384,2048]{1,0:T(8,1...) custom-call(bf16[4,2,4,2,32,2560]{5,4,3,2,1,0:T(8,128)(2,1)} %bitcast.245, ...), custom_call_target="tpu_custom_call" | custom-call | flops 10000000 | bytes 300000000 | tf_op jit(solution)/shard_map/pallas_call | solution.py:226
  779.3 7.3 add_bitcast_fusion.2
  795.5 9.0 %fusion.42 = f32[64,128]{1,0:T(8,128)S(1)} fusion(bf16[64,20,2048]{2,1,0:T(8,128)(2,1)} %all-to-all-done.3, bf16[128,2048]{1,0:T(8,128)(2,1)S(1)} %copy-done.25, s32[64,128]{1,0:T(8,128)S(1)} %fusion.48), kind=kOutput, calls=%fused_computation.75 | convolution fusion | flops 671571968 | bytes 5832704 | tf_op jit(solution)/shard_map/dot_general | solution.py:416
  805.1 8.7 %fusion.12 = f32[128,2048]{1,0:T(8,128)S(1)} fusion(bf16[64,20,2048]{2,1,0:T(8,128)(2,1)} %all-to-all-done.3, f32[64,128]{1,0:T(8,128)S(1)} %bitcast.282, s32[64,128]{1,0:T(8,128)S(1)} %fusion.48), kind=kOutput, calls=%fused_computation.30 | convolution fusion | flops 671416320 | bytes 6356992 | tf_op jit(solution)/shard_map/dot_general | solution.py:416
  813.8 9.8 %fusion.27 = bf16[128,2048]{1,0:T(8,128)(2,1)} fusion(f32[128,2048]{1,0:T(8,128)S(1)} %copy-done.5, f32[128,2048]{1,0:T(8,128)S(1)} %fusion.12, bf16[64,20,2048]{2,1,0:T(8,128)(2,1)} %all-to-all-done.3, f32[64,128]{1,0:T(8,128)S(1)} %bitcast.283, s32[64,128]{1,0:T(8,128)S(1)} %fusion.48), kind=kOutput, calls=%fused_computation.35 | convolution fusion | flops 672858112 | bytes 7929856 | tf_op jit(solution)/shard_map/dot_general | solution.py:416
  (315 shorter events, 135.5 us)
Async XLA Ops:
  144.0 9.5 %copy-start.40 = (bf16[2,128,2048]{2,1,0:T(8,128)(2,1)S(1)}, bf16[2,128,2048]{2,1,0:T(8,128)(2,1)}, u32[]{:S(2)}) copy-start(bf16[2,128,2048]{2,1,0:T(8,128)(2,1)} %get-tuple-element.33) | copy-start | bytes 3145732
  144.0 102.9 %all-to-all-start = ((bf16[64,20,2048]{2,1,0:T(8,128)(2,1)}), bf16[64,20,2048]{2,1,0:T(8,128)(2,1)}, u32[]{:S(2)}, u32[]{:S(2)}) async-start(bf16[64,20,2048]{2,1,0:T(8,128)(2,1)} %reshape.278), calls=%async_computation | async-start | bytes 12582912 | tf_op jit(solution)/shard_map/all_to_all | solution.py:482
  177.2 65.9 %copy-start.33 = (pred[1280,128]{1,0:T(32,128)(4,1)S(1)}, pred[1280,128]{1,0:T(32,128)(4,1)}, u32[]{:S(2)}) copy-start(pred[1280,128]{1,0:T(32,128)(4,1)} %copy-done.32) | copy-start | bytes 491524
  177.2 65.9 %copy-start.69 = (f32[2048]{0:T(1024)S(1)}, f32[2048]{0:T(1024)}, u32[]{:S(2)}) copy-start(f32[2048]{0:T(1024)} %param.25) | copy-start | bytes 24580
  178.6 61.7 %collective-permute-start = (bf16[128,2048]{1,0:T(8,128)(2,1)}, bf16[128,2048]{1,0:T(8,128)(2,1)}, u32[]{:S(2)}, u32[]{:S(2)}) collective-permute-start(bf16[128,2048]{1,0:T(8,128)(2,1)} %dynamic-slice_convert_fusion.1), channel_id=1, source_target_pairs={{0,1},{1,0},{2,3},{3,2},{4,5},{5,4},{6,7},{7,6},{8,9},{9,8},{10,11... | collective-permute-start | bytes 1572872 | tf_op jit(solution)/shard_map/ppermute | solution.py:457
  264.9 15.7 %slice-start = ((s8[5242880]{0:T(1024)(128)(4,1)}), s8[1048576]{0:T(1024)(128)(4,1)S(1)}, s32[]{:S(2)}) async-start(s8[5242880]{0:T(1024)(128)(4,1)} %bitcast.249), calls=%async_computation.4 | async-start | bytes 2097152
  264.9 83.9 %all-to-all-start.1 = ((bf16[64,20,2048]{2,1,0:T(8,128)(2,1)}), bf16[64,20,2048]{2,1,0:T(8,128)(2,1)}, u32[]{:S(2)}, u32[]{:S(2)}) async-start(bf16[64,20,2048]{2,1,0:T(8,128)(2,1)} %reshape.280), calls=%async_computation.1 | async-start | bytes 12582912 | tf_op jit(solution)/shard_map/all_to_all | solution.py:482
  370.7 22.3 %copy-start.54 = (bf16[1280,384]{1,0:T(8,128)(2,1)}, bf16[1280,384]{1,0:T(8,128)(2,1)S(1)}, u32[]{:S(2)}) copy-start(bf16[1280,384]{1,0:T(8,128)(2,1)S(1)} %get-tuple-element.66) | copy-start | bytes 2949124
  416.4 87.3 %all-to-all-start.2 = ((bf16[64,20,2048]{2,1,0:T(8,128)(2,1)}), bf16[64,20,2048]{2,1,0:T(8,128)(2,1)}, u32[]{:S(2)}, u32[]{:S(2)}) async-start(bf16[64,20,2048]{2,1,0:T(8,128)(2,1)} %reshape.282), calls=%async_computation.2 | async-start | bytes 12582912 | tf_op jit(solution)/shard_map/all_to_all | solution.py:482
  428.1 10.0 %slice-start.4 = ((s8[5242880]{0:T(1024)(128)(4,1)}), s8[1048576]{0:T(1024)(128)(4,1)S(1)}, s32[]{:S(2)}) async-start(s8[5242880]{0:T(1024)(128)(4,1)} %bitcast.267), calls=%async_computation.8 | async-start | bytes 2097152
  446.2 57.5 %copy-start.5 = (f32[128,2048]{1,0:T(8,128)S(1)}, f32[128,2048]{1,0:T(8,128)}, u32[]{:S(2)}) copy-start(f32[128,2048]{1,0:T(8,128)} %copy-done.4) | copy-start | bytes 3145732
  450.8 61.7 %copy-start.24 = (bf16[128,2048]{1,0:T(8,128)(2,1)S(1)}, bf16[128,2048]{1,0:T(8,128)(2,1)}, u32[]{:S(2)}) copy-start(bf16[128,2048]{1,0:T(8,128)(2,1)} %param.31) | copy-start | bytes 1572868
  503.7 8.9 %copy-start.78 = (f32[128]{0:T(128)S(1)}, f32[128]{0:T(128)}, u32[]{:S(2)}) copy-start(f32[128]{0:T(128)} %copy-done.77) | copy-start | bytes 1540
  503.7 8.9 %copy-start.82 = (f32[128]{0:T(128)S(1)}, f32[128]{0:T(128)}, u32[]{:S(2)}) copy-start(f32[128]{0:T(128)} %get-tuple-element.102) | copy-start | bytes 1540
  514.0 14.0 %slice-start.10 = ((s8[8388608]{0:T(1024)(128)(4,1)}), s8[4194304]{0:T(1024)(128)(4,1)S(1)}, s32[]{:S(2)}) async-start(s8[8388608]{0:T(1024)(128)(4,1)} %bitcast.296), calls=%async_computation.14 | async-start | bytes 8388608
  514.0 14.0 %slice-start.11 = ((s8[8388608]{0:T(1024)(128)(4,1)}), s8[4194304]{0:T(1024)(128)(4,1)S(1)}, s32[]{:S(2)}) async-start(s8[8388608]{0:T(1024)(128)(4,1)} %bitcast.296), calls=%async_computation.15 | async-start | bytes 8388608
  514.0 13.9 %collective-permute-start.1 = (bf16[128,2048]{1,0:T(8,128)(2,1)S(1)}, bf16[128,2048]{1,0:T(8,128)(2,1)S(1)}, u32[]{:S(2)}, u32[]{:S(2)}) collective-permute-start(bf16[128,2048]{1,0:T(8,128)(2,1)S(1)} %get-tuple-element.56), channel_id=1, source_target_pairs={{0,1},{1,0},{2,3},{3,2},{4,5},{5,4},{6,7},{7,6},{8,9},{9,8},{10,11... | collective-permute-start | bytes 1572872 | tf_op jit(solution)/shard_map/ppermute | solution.py:457
  552.5 242.9 %all-to-all-start.3 = ((bf16[64,20,2048]{2,1,0:T(8,128)(2,1)}), bf16[64,20,2048]{2,1,0:T(8,128)(2,1)}, u32[]{:S(2)}, u32[]{:S(2)}) async-start(bf16[64,20,2048]{2,1,0:T(8,128)(2,1)} %reshape.283), calls=%async_computation.3 | async-start | bytes 12582912 | tf_op jit(solution)/shard_map/all_to_all | solution.py:482
  604.3 167.5 %copy-start.7 = (bf16[128,2048]{1,0:T(8,128)(2,1)S(1)}, bf16[128,2048]{1,0:T(8,128)(2,1)}, u32[]{:S(2)}) copy-start(bf16[128,2048]{1,0:T(8,128)(2,1)} %param.16) | copy-start | bytes 1572868
  604.3 167.5 %copy-start.66 = (f32[2048]{0:T(1024)S(1)}, f32[2048]{0:T(1024)}, u32[]{:S(2)}) copy-start(f32[2048]{0:T(1024)} %param.18) | copy-start | bytes 24580
  769.9 8.1 copy-start.19
  769.9 8.1 copy-start.26
  769.9 8.1 copy-start.76
  770.0 8.1 copy-start.81
  771.7 7.6 copy-start.37
  771.7 7.6 copy-start.84
  771.8 14.9 %slice-start.6 = ((s8[5242880]{0:T(1024)(128)(4,1)}), s8[4194304]{0:T(1024)(128)(4,1)S(1)}, s32[]{:S(2)}) async-start(s8[5242880]{0:T(1024)(128)(4,1)} %bitcast.269), calls=%async_computation.10 | async-start | bytes 8388608
  779.3 7.3 copy-start.35
  779.3 12.1 %slice-start.2 = ((s8[5242880]{0:T(1024)(128)(4,1)}), s8[4194304]{0:T(1024)(128)(4,1)S(1)}, s32[]{:S(2)}) async-start(s8[5242880]{0:T(1024)(128)(4,1)} %bitcast.251), calls=%async_computation.6 | async-start | bytes 8388608
  795.4 9.0 %copy-start.68 = (s32[128,8]{0,1:T(8,128)S(1)}, s32[128,8]{0,1:T(8,128)}, u32[]{:S(2)}) copy-start(s32[128,8]{0,1:T(8,128)} %param.26) | copy-start | bytes 12292
  795.4 9.6 %copy-start.62 = (f32[128,64]{0,1:T(8,128)S(1)}, f32[128,64]{0,1:T(8,128)}, u32[]{:S(2)}) copy-start(f32[128,64]{0,1:T(8,128)} %copy-done.61) | copy-start | bytes 98308
  813.8 9.8 %copy-start.63 = (f32[32,2048]{1,0:T(8,128)S(1)}, f32[32,2048]{1,0:T(8,128)}, u32[]{:S(2)}) copy-start(f32[32,2048]{1,0:T(8,128)} %get-tuple-element.48) | copy-start | bytes 786436
  (73 other events, 242.2 us)

commit v3 on v2

--- a/solution.py
+++ b/solution.py
@@ -1,3 +1,4 @@
+import functools
 import math
 
 import jax
@@ -55,8 +56,8 @@
 
 
 def reduce_kernel(
-    ga, gb, gain, d_own, d_sent, x_hat, down, gate, up,
-    oa, ob, og, d_came, down_c, gate_c, up_c,
+    ga, gb, gain, d_own, d_sent, x_hat, down, gate,
+    oa, ob, og, d_came, down_c, gate_c,
     own_a, got_a, one_a, two_a, sum_a, three_a,
     own_b, got_b, one_b, two_b, sum_b, three_b,
     vec, vecs,
@@ -133,15 +134,14 @@
             def _(j):
                 own[to, i, j] = (own[to, i, j].astype(F32) + got[to, i, j].astype(F32)).astype(BF16)
 
-    d_copy.wait_recv()
-    vec_start(0)
-    expert = [
-        send(down, down_c, pair_send.at[1], pair_recv.at[1], partner),
-        send(gate, gate_c, pair_send.at[2], pair_recv.at[2], partner),
-    ]
-
     ones = []
+    expert = []
     for i, s in enumerate(order):
+        if i == 1:
+            d_copy.wait_recv()
+            vec_start(0)
+            expert.append(send(down, down_c, pair_send.at[1], pair_recv.at[1], partner))
+            expert.append(send(gate, gate_c, pair_send.at[2], pair_recv.at[2], partner))
         loads["a", s].wait()
         swaps["a", s].wait_recv()
         add_cores(own_a, got_a, turn(z, s))
@@ -192,7 +192,6 @@
     final_a = send(three_a.at[0], three_a.at[1], three_send.at[0], three_recv.at[0], across)
     three_b[0] = last(sum_b, two_b, z, 1 - x).astype(BF16)
     final_b = send(three_b.at[0], three_b.at[1], three_send.at[1], three_recv.at[1], across)
-    expert.append(send(up, up_c, pair_send.at[3], pair_recv.at[3], partner))
     mine_a = last(sum_a, two_a, y, x)
     final_a.wait_recv()
     oa[...] = mine_a + three_a[1].astype(F32)
@@ -232,8 +231,8 @@
             jax.ShapeDtypeStruct(d_sent.shape, BF16),
             *[jax.ShapeDtypeStruct(half.shape, BF16) for half in expert],
         ),
-        in_specs=[ANY_SPEC] * 2 + [VMEM_SPEC] * 4 + [ANY_SPEC] * 3,
-        out_specs=[VMEM_SPEC] * 4 + [ANY_SPEC] * 3,
+        in_specs=[ANY_SPEC] * 2 + [VMEM_SPEC] * 4 + [ANY_SPEC] * 2,
+        out_specs=[VMEM_SPEC] * 4 + [ANY_SPEC] * 2,
         scratch_shapes=scratch(a_cols, (2, 4))
         + scratch(b_cols, (4, 2))
         + [
@@ -250,8 +249,8 @@
             dma((2,)),
             dma((4, 3)),
             dma((4, 3)),
-            dma((4,)),
-            dma((4,)),
+            dma((3,)),
+            dma((3,)),
         ],
         compiler_params=pltpu.CompilerParams(
             collective_id=1, has_side_effects=True, vmem_limit_bytes=56 * 1024 * 1024
@@ -300,7 +299,7 @@
 
 
 def gather_kernel(
-    sa, sb, part, down, gate, up, fa, fb, whole, down_o, gate_o, up_o,
+    sa, sb, part, down, gate, fa, fb, whole, down_o, gate_o,
     keep_sem, x_send, x_recv, one_send, one_recv, two_send, two_recv, core_send, core_recv, pair_send, pair_recv,
 ):
     z, x, y, core = coordinates()
@@ -320,7 +319,7 @@
     ]
     expert = [
         send(src, dst, pair_send.at[i], pair_recv.at[i], partner)
-        for i, (src, dst) in enumerate(((down, down_o), (gate, gate_o), (up, up_o)), 1)
+        for i, (src, dst) in enumerate(((down, down_o), (gate, gate_o)), 1)
     ]
     keep = [
         pltpu.make_async_copy(part, whole.at[tensor], keep_sem.at[0]),
@@ -386,8 +385,8 @@
             jax.ShapeDtypeStruct((2,) + part.shape, BF16),
             *[jax.ShapeDtypeStruct(w.shape, BF16) for w in expert],
         ),
-        in_specs=[ANY_SPEC] * 6,
-        out_specs=[ANY_SPEC] * 6,
+        in_specs=[ANY_SPEC] * 5,
+        out_specs=[ANY_SPEC] * 5,
         scratch_shapes=[
             dma((3,)),
             dma((2,)),
@@ -412,6 +411,151 @@
     )
 
 
+ROWS_FULL, ROWS_PART, CHUNKS = 16, 4, 4
+
+
+def pack_kernel(weighted, values, place, part, *refs):
+    out = refs[-1]
+    width = values.shape[1]
+    step = width // CHUNKS
+    tokens = values.shape[0]
+    main = jnp.dot(place[...], values[...], preferred_element_type=F32)
+    rest = jnp.zeros((place.shape[0], step), F32)
+    for j in range(CHUNKS):
+        rest += jnp.dot(
+            part[:, j * tokens : (j + 1) * tokens],
+            values[:, j * step : (j + 1) * step],
+            preferred_element_type=F32,
+        )
+    if weighted:
+        main, rest = main * refs[0][...], rest * refs[1][...]
+    out[:, :width] = main.astype(BF16)
+    out[:, width:] = rest.astype(BF16)
+
+
+def pack(values, place, part, weights=()):
+    total, tokens = place.shape
+    width = values.shape[1]
+    block = total // 4
+    return pl.pallas_call(
+        functools.partial(pack_kernel, bool(weights)),
+        grid=(4,),
+        out_shape=jax.ShapeDtypeStruct((total, width + width // CHUNKS), BF16),
+        in_specs=[
+            pl.BlockSpec((tokens, width), lambda g: (0, 0)),
+            pl.BlockSpec((block, tokens), lambda g: (g, 0)),
+            pl.BlockSpec((block, CHUNKS * tokens), lambda g: (g, 0)),
+        ]
+        + [pl.BlockSpec((block, 1), lambda g: (g, 0))] * len(weights),
+        out_specs=pl.BlockSpec((block, width + width // CHUNKS), lambda g: (g, 0)),
+        cost_estimate=pl.CostEstimate(flops=1_000_000_000, bytes_accessed=8_000_000, transcendentals=0),
+    )(values, place, part, *weights)
+
+
+def expert_kernel(
+    rows, grads, gate_m, gate_o, up_m, up_o, down_m, down_o,
+    result, d_row, rows_out, grads_out, hidden, d_gate, d_up,
+    gate_w, up_w, down_w,
+):
+    units = down_m.shape[0]
+
+    @pl.when(pl.program_id(0) == 0)
+    def _():
+        gate_w[:, :units] = gate_m[...]
+        gate_w[:, units:] = gate_o[...]
+        up_w[:, :units] = up_m[...]
+        up_w[:, units:] = up_o[...]
+        down_w[:units] = down_m[...]
+        down_w[units:] = down_o[...]
+
+    block = rows.shape[0]
+    width = down_w.shape[1]
+    step = width // CHUNKS
+    more = block // ROWS_FULL * ROWS_PART
+
+    def picks(shape, axis, j):
+        extra = lax.broadcasted_iota(jnp.int32, shape, axis)
+        packed = lax.broadcasted_iota(jnp.int32, shape, 1 - axis)
+        return (packed == (extra >> 2) * 16 + j * 4 + (extra & 3)).astype(F32).astype(BF16)
+
+    def spread(src, dst):
+        dst[:block] = src[:, :width]
+        for j in range(CHUNKS):
+            dst[block:, j * step : (j + 1) * step] = jnp.dot(
+                picks((more, block), 0, j), src[:, width:], preferred_element_type=F32
+            ).astype(BF16)
+
+    def repack(dst, parts):
+        rest = jnp.zeros((block, step), F32)
+        for j in range(CHUNKS):
+            full = parts(j).astype(BF16)
+            dst[:, j * step : (j + 1) * step] = full[:block]
+            rest += jnp.dot(picks((block, more), 1, j), full[block:], preferred_element_type=F32)
+        dst[:, width:] = rest.astype(BF16)
+
+    spread(rows, rows_out)
+    gate = jnp.dot(rows_out[...], gate_w[...], preferred_element_type=F32)
+    up = jnp.dot(rows_out[...], up_w[...], preferred_element_type=F32)
+    sigma = jax.nn.sigmoid(gate)
+    activated = gate * sigma
+    hidden[...] = (activated * up).astype(BF16)
+    spread(grads, grads_out)
+    d_hidden = dot(grads_out[...], down_w[...], ((1,), (1,)))
+    d_gate[...] = (d_hidden * up * (sigma * (1.0 + gate * (1.0 - sigma)))).astype(BF16)
+    d_up[...] = (d_hidden * activated).astype(BF16)
+    repack(
+        d_row,
+        lambda j: dot(d_gate[...], gate_w[j * step : (j + 1) * step], ((1,), (1,)))
+        + dot(d_up[...], up_w[j * step : (j + 1) * step], ((1,), (1,))),
+    )
+    repack(
+        result,
+        lambda j: jnp.dot(hidden[...], down_w[:, j * step : (j + 1) * step], preferred_element_type=F32),
+    )
+
+
+def run_expert(rows, grads, gate_w, up_w, down_w):
+    total, packed = rows.shape
+    units, width = 2 * down_w[0].shape[0], down_w[0].shape[1]
+    groups = 4
+    block = total // groups
+    full = block // ROWS_FULL * (ROWS_FULL + ROWS_PART)
+
+    def whole_of(w):
+        return pl.BlockSpec(w.shape, lambda g: (0, 0), pipeline_mode=pl.Buffered(1))
+
+    def cut(rows, cols):
+        return pl.BlockSpec((rows, cols), lambda g: (g, 0))
+
+    def shape(cols):
+        return jax.ShapeDtypeStruct((full * groups, cols), BF16)
+
+    return pl.pallas_call(
+        expert_kernel,
+        grid=(groups,),
+        out_shape=(
+            jax.ShapeDtypeStruct((total, packed), BF16),
+            jax.ShapeDtypeStruct((total, packed), BF16),
+            shape(width),
+            shape(width),
+            shape(units),
+            shape(units),
+            shape(units),
+        ),
+        in_specs=[cut(block, packed)] * 2 + [whole_of(w) for w in (*gate_w, *up_w, *down_w)],
+        out_specs=[cut(block, packed)] * 2 + [cut(full, width)] * 2 + [cut(full, units)] * 3,
+        scratch_shapes=[
+            pltpu.VMEM((width, units), BF16),
+            pltpu.VMEM((width, units), BF16),
+            pltpu.VMEM((units, width), BF16),
+        ],
+        compiler_params=pltpu.CompilerParams(vmem_limit_bytes=56 * 1024 * 1024),
+        cost_estimate=pl.CostEstimate(
+            flops=12 * full * groups * width * units, bytes_accessed=45_000_000, transcendentals=full * groups * units
+        ),
+    )(rows, grads, *gate_w, *up_w, *down_w)
+
+
 def dot(left, right, contract):
     return lax.dot_general(left, right, (contract, ((), ())), preferred_element_type=F32)
 
@@ -479,7 +623,10 @@
 
 
 def exchange(buffer):
-    return lax.all_to_all(buffer, "dp", split_axis=0, concat_axis=0, tiled=True)
+    groups = [[dp * 2 + (dp // 8 % 2 ^ g) for dp in range(64)] for g in range(2)]
+    return lax.all_to_all(
+        buffer, ("dp", "tensor"), split_axis=0, concat_axis=0, tiled=True, axis_index_groups=groups
+    )
 
 
 def per_device(
@@ -503,19 +650,17 @@
     rows, width = tokens.shape
     owners = lax.axis_size("dp")
     experts = owners
-    capacity = 5 * rows * TOP // (4 * experts)
-    slots = experts * capacity
     scale = HD ** (-0.5)
 
     inputs = tokens.astype(F32)
     in_scale = rms_scale(inputs)
     normed = (inputs * in_scale * norm_in).astype(BF16)
     gate_w, up_w, down_w = gate_weight[0], up_weight[0], down_weight[0]
-    in_full, out_full, whole, (down_o, gate_o, up_o) = gather_weights(
+    in_full, out_full, whole, (down_o, gate_o) = gather_weights(
         jnp.concatenate([query_weight, key_weight, value_weight], axis=1),
         out_weight.T,
         normed,
-        (down_w, gate_w, up_w),
+        (down_w, gate_w),
     )
     q_cols, k_cols = query_weight.shape[1], key_weight.shape[1]
     query_heads, key_heads = q_cols // HD, k_cols // HD
@@ -526,15 +671,36 @@
     weight_of = jnp.sum(jnp.where(names, route_weight[:, :, None], 0.0), axis=1)
     below = jnp.arange(rows)[:, None] > jnp.arange(rows)[None, :]
     rank = dot(below.astype(BF16), chosen.astype(BF16), ((1,), (0,))).astype(jnp.int32)
-    rank = jnp.where(chosen, rank, -1)
-    place_b = rank.T[:, None, :] == jnp.arange(capacity, dtype=jnp.int32)[None, :, None]
-    place = place_b.reshape(slots, rows).astype(BF16)
-    slot_weight = jnp.sum(jnp.where(place_b, weight_of.T[:, None, :], 0.0), axis=2).reshape(slots)
+    rank = jnp.where(chosen, rank, -1).T
+    spot = jnp.arange(ROWS_FULL, dtype=jnp.int32)
+    in_place = rank[:, None, :] == spot[None, :, None]
+    extra = rank[:, None, :] == ROWS_FULL + (spot % ROWS_PART)[None, :, None]
+    quarter = jnp.arange(CHUNKS, dtype=jnp.int32)
+    in_part = extra[:, :, None, :] & (
+        (spot // ROWS_PART)[None, :, None, None] == quarter[None, None, :, None]
+    )
+    packed_rows = experts * ROWS_FULL
+    place = in_place.reshape(packed_rows, rows).astype(BF16)
+    part = in_part.reshape(packed_rows, CHUNKS * rows).astype(BF16)
+    weight_t = weight_of.T
+    place_weight = jnp.sum(jnp.where(in_place, weight_t[:, None, :], 0.0), axis=2).reshape(packed_rows, 1)
+    part_weight = jnp.sum(jnp.where(extra, weight_t[:, None, :], 0.0), axis=2).reshape(packed_rows, 1)
+
+    def to_experts(packed):
+        return exchange(packed.reshape(experts, ROWS_FULL, -1)).reshape(packed_rows, -1)
+
+    def quarters(values):
+        return values.reshape(rows, CHUNKS, -1).transpose(1, 0, 2).reshape(CHUNKS * rows, -1)
+
+    def to_tokens(packed, place, part):
+        first = dot(place, packed[:, :width], ((0,), (0,)))
+        rest = dot(part, packed[:, width:], ((0,), (0,)))
+        return first + rest.reshape(CHUNKS, rows, -1).transpose(1, 0, 2).reshape(rows, width)
 
     grad = out_grad.astype(F32)
-    d_rows = (dot(place, out_grad, ((1,), (0,))) * slot_weight[:, None]).astype(BF16)
+    d_rows = pack(out_grad, place, part, (place_weight, part_weight))
     d_rows, whole = lax.optimization_barrier((d_rows, whole))
-    expert_grads = exchange(d_rows.reshape(experts, capacity, width)).reshape(slots, width)
+    expert_grads = to_experts(d_rows)
 
     length = whole.shape[0]
     cosine, sine = rope_tables(positions, HD)
@@ -566,40 +732,27 @@
     mid_scale = rms_scale(hidden_in)
     normed_mid = (hidden_in * mid_scale * norm_mid).astype(BF16)
 
-    send_rows = dot(place, normed_mid, ((1,), (0,))).astype(BF16)
-    send_rows, expert_grads = lax.optimization_barrier((send_rows, expert_grads))
-    rows_in = exchange(send_rows.reshape(experts, capacity, width)).reshape(slots, width)
-
-    def expert_half(gate_h, up_h, down_h):
-        gate = dot(rows_in, gate_h, ((1,), (0,)))
-        up = dot(rows_in, up_h, ((1,), (0,)))
-        d_hidden = dot(expert_grads, down_h, ((1,), (1,)))
-        sigma = jax.nn.sigmoid(gate)
-        activated = gate * sigma
-        hidden = (activated * up).astype(BF16)
-        d_gate = (d_hidden * up * (sigma * (1.0 + gate * (1.0 - sigma)))).astype(BF16)
-        d_up = (d_hidden * activated).astype(BF16)
-        result = dot(hidden, down_h, ((1,), (0,)))
-        d_row = dot(d_gate, gate_h, ((1,), (1,))) + dot(d_up, up_h, ((1,), (1,)))
-        return hidden, d_gate, d_up, result, d_row
-
-    hid_m, dg_m, du_m, res_m, dr_m = expert_half(gate_w, up_w, down_w)
-    hid_o, dg_o, du_o, res_o, dr_o = expert_half(gate_o, up_o, down_o)
-    d_row = (dr_m + dr_o).astype(BF16)
-    result = (res_m + res_o).astype(BF16)
-    back_rows = exchange(d_row.reshape(experts, capacity, width)).reshape(slots, width)
-    halves = ((hid_m, expert_grads), (rows_in, dg_m), (rows_in, du_m))
-    sent = [
-        dot(left, right, ((0,), (0,))).astype(BF16)
-        for left, right in ((hid_o, expert_grads), (rows_in, dg_o), (rows_in, du_o))
+    send_rows = pack(normed_mid, place, part)
+    send_rows, expert_grads, up_s = lax.optimization_barrier((send_rows, expert_grads, up_w))
+    up_o = swap(up_s)
+    result, d_row, rows_in, grads_in, hidden, d_gate, d_up = run_expert(
+        to_experts(send_rows), expert_grads, (gate_w, gate_o), (up_w, up_o), (down_w, down_o)
+    )
+    back_rows = to_experts(d_row)
+    units = down_w.shape[0]
+    halves, others = [
+        ((hidden[:, of], grads_in), (rows_in, d_gate[:, of]), (rows_in, d_up[:, of]))
+        for of in (slice(0, units), slice(units, 2 * units))
     ]
-
-    d_mid = dot(place, back_rows, ((0,), (0,)))
+    sent = [dot(left, right, ((0,), (0,))).astype(BF16) for left, right in others]
+
+    d_mid = to_tokens(back_rows, place, part)
     d_mid_in, grad_norm_mid = norm_back(hidden_in, mid_scale, norm_mid, d_mid)
     d_hidden_in = grad + d_mid_in
     d_attended = d_hidden_in.astype(BF16)
     d_whole = share_sequence(d_attended)
-    d_whole, result = lax.optimization_barrier((d_whole, result))
+    d_whole, result, up_sent = lax.optimization_barrier((d_whole, result, sent[2]))
+    up_came = swap(up_sent)
     d_mixed = (
         dot(d_whole, out_full, ((1,), (0,))).astype(BF16).reshape(length, key_heads, group, HD)
     )
@@ -632,33 +785,34 @@
     d_total = dot(d_raw, in_full, ((1,), (1,)))
     d_own, d_sent = halves_of(d_total, rows)
 
-    returned = exchange(result.reshape(experts, capacity, width)).reshape(slots, width)
-    combine = jnp.where(place_b, weight_of.T[:, None, :], 0.0).reshape(slots, rows)
-    combine_high = combine.astype(BF16)
-    combine_low = (combine - combine_high.astype(F32)).astype(BF16)
-    moe = dot(combine_high, returned, ((0,), (0,))) + dot(combine_low, returned, ((0,), (0,)))
-    output = (hidden_in + moe).astype(BF16)
-    products = dot(returned, out_grad, ((1,), (1,)))
-    of_expert = jnp.sum(
-        jnp.where(place_b, products.reshape(experts, capacity, rows), 0.0), axis=1
-    ).T
-    grad_route = jnp.sum(jnp.where(names, of_expert[:, None, :], 0.0), axis=2)
-
+    returned = to_experts(result)
     in_grads = dot(whole, d_raw, ((0,), (0,))).astype(BF16)
     out_grads = dot(d_whole, mixed, ((0,), (0,))).astype(BF16)
     gains = jnp.pad(
         jnp.stack([grad_norm_mid, jnp.pad(jnp.concatenate([grad_query_gain, grad_key_gain]), (0, width - 2 * HD))]),
         ((1, 5), (0, 0)),
     )
+    in_grads, returned, up_came = lax.optimization_barrier((in_grads, returned, up_came))
     in_total, out_total, gains, d_came, *came = reduce_grads(
-        in_grads, out_grads, gains, d_own, d_sent.astype(BF16), inputs * in_scale, sent
-    )
+        in_grads, out_grads, gains, d_own, d_sent.astype(BF16), inputs * in_scale, sent[:2]
+    )
+    place_high = (place * place_weight).astype(BF16)
+    part_high = (part * part_weight).astype(BF16)
+    place_low = (place * place_weight - place_high.astype(F32)).astype(BF16)
+    part_low = (part * part_weight - part_high.astype(F32)).astype(BF16)
+    moe = to_tokens(returned, place_high, part_high) + to_tokens(returned, place_low, part_low)
+    output = (hidden_in + moe).astype(BF16)
+    products = dot(returned[:, :width], out_grad, ((1,), (1,))) * place
+    rest = dot(returned[:, width:], quarters(out_grad), ((1,), (1,))) * part
+    of_row = products + jnp.sum(rest.reshape(packed_rows, CHUNKS, rows), axis=1)
+    of_expert = jnp.sum(of_row.reshape(experts, ROWS_FULL, rows), axis=1).T
+    grad_route = jnp.sum(jnp.where(names, of_expert[:, None, :], 0.0), axis=2)
     d_normed = d_own + d_came.astype(F32)
     d_inputs, _ = norm_back(inputs, in_scale, norm_in, d_normed)
     grad_tokens = (d_hidden_in + d_inputs).astype(BF16)
     grad_down, grad_gate, grad_up = [
         (dot(left, right, ((0,), (0,))) + half.astype(F32))[None]
-        for (left, right), half in zip(halves, came)
+        for (left, right), half in zip(halves, (*came, up_came))
     ]
     grad_norm_in, grad_norm_mid = gains[0], gains[1]
     grad_query_gain, grad_key_gain = gains[2, :HD], gains[2, HD : 2 * HD]

time: 835 us -> 653 us (0.78)
  matrix products: 181 us -> 94.2 us
  waiting for transfers between devices: 185 us -> 150 us
  Pallas kernels: 291 us -> 257 us
  local copies, waits for them, and re-layouts: 93 us -> 64.8 us
  other arithmetic: 30.9 us -> 42.7 us
    dot_general x31 -> x21, matrix products: 171 us -> 85.5 us  [dot(): lax.dot_general(left, right, (contract, ((), ())), preferred_element_type...]
    pallas_call x1, Pallas kernels: 166 us -> 111 us  [reduce_grads(): pl.pallas_call(reduce_kernel, out_shape=(jax.ShapeDtypeStruct((rows, a_co...]
    pallas_call x0 -> x3, Pallas kernels: none -> 51.4 us  [the longest x1 39.5 us: run_expert(): pl.pallas_call(expert_kernel, grid=(groups,), out_shape=(jax.ShapeDtypeSt...]
    reshape x6, local copies, waits for them, and re-layouts: 53.7 us -> 4.59 us  [the longest x1 2.14 us: per_device(): of_row = products + jnp.sum(rest.reshape(packed_rows, CHUNKS, rows), axis=1)]
    pallas_call x1, Pallas kernels: 126 us -> 94.9 us  [gather_weights(): pl.pallas_call(gather_kernel, out_shape=(jax.ShapeDtypeStruct((4, 2, 4, 2...]
    all_to_all x4, waiting for transfers between devices: 117 us -> 89.4 us  [exchange(): lax.all_to_all(buffer, ('dp', 'tensor'), split_axis=0, concat_axis=0, til...]
    ppermute x2 -> x4, waiting for transfers between devices: 68.6 us -> 61.1 us  [swap(): return lax.ppermute(values, 'tensor', [(0, 1), (1, 0)])]
    unnamed x205 -> x174, local copies, waits for them, and re-layouts: 14 us -> 19.8 us
  transfers between devices with their start and end apart: 6 -> 8, of which waited for: 4 -> 7; matrix products, arithmetic and copies ran while one was open for 16% -> 16% of each run, Pallas kernels for 20% -> 1%
where the time goes in v3:
time: 653 us; the launch traced here: 647 us
  Pallas kernels  257 us (39%)
  waiting for transfers between devices  150 us (23%)
  matrix products  94.2 us (14%)
  local copies, waits for them, and re-layouts  64.8 us (10%)
  other arithmetic  42.7 us (7%)
  starting transfers between devices  35.7 us (5%)
    pallas_call x1, Pallas kernels, reduce_grads(): pl.pallas_call(reduce_kernel, out_shape=(jax.ShapeDtypeStruct((rows, a_co...  111 us
    pallas_call x1, Pallas kernels, gather_weights(): pl.pallas_call(gather_kernel, out_shape=(jax.ShapeDtypeStruct((4, 2, 4, 2...  94.9 us
    all_to_all x4, waiting for transfers between devices, exchange(): lax.all_to_all(buffer, ('dp', 'tensor'), split_axis=0, concat_axis=0, til...  89.4 us
    dot_general x21, matrix products, dot(): lax.dot_general(left, right, (contract, ((), ())), preferred_element_type...  85.5 us
    ppermute x4, waiting for transfers between devices, swap(): return lax.ppermute(values, 'tensor', [(0, 1), (1, 0)])  61.1 us
    pallas_call x1, Pallas kernels, run_expert(): pl.pallas_call(expert_kernel, grid=(groups,), out_shape=(jax.ShapeDtypeSt...  39.5 us
    all_to_all x4, starting transfers between devices, exchange(): lax.all_to_all(buffer, ('dp', 'tensor'), split_axis=0, concat_axis=0, til...  34.4 us
    unnamed x174, local copies, waits for them, and re-layouts  19.8 us
  transfers between devices with their start and end apart: 8, of which 7 were waited for; matrix products, arithmetic and copies ran while one was open for 16% of the time, Pallas kernels for 1%

profile of v3, /device:TPU:0, one launch (start us, length us, event | category | flops | bytes accessed | tf_op | source)
XLA Modules:
  0.0 646.9 jit_solution(10507705410542005838)
XLA Ops:
  10.6 6.2 shard_map.263
  16.7 94.9 %shard_map.264 = (bf16[4,2,4,2,32,2560]{5,4,3,2,1,0:T(8,128)(2,1)}, bf16[4,2,4,2,32,2048]{5,4,3,2,1,0:T(8,128)(2,1)}, bf16[2,128,2048]{2,1,0:T(8,128)(2,1)}, bf16[384,2048]{1,0:T(8,128)(2,1)}, bf16[2048,384]{1,0:T(8,128)(2,1)}) custom-call(bf16[32,2560]{1,0:T(8,128)(2,1)} %pad_maximum_fusion.7.sa, bf16[32,2048]{1,0:T(8,128)(2,1)} %bitcast.300, ...), custom_call_target="tpu_custom_call" | custom-call | bytes 250000000 | tf_op jit(solution)/shard_map/pallas_call | solution.py:380
  111.7 7.6 %all-to-all-start = ((bf16[64,16,2560]{2,1,0:T(8,128)(2,1)}), bf16[64,16,2560]{2,1,0:T(8,128)(2,1)}, u32[]{:S(2)}, u32[]{:S(2)}) async-start(bf16[64,16,2560]{2,1,0:T(8,128)(2,1)} %bitcast.257), calls=%async_computation | async-start | bytes 10485760 | tf_op jit(solution)/shard_map/all_to_all | solution.py:627
  119.4 5.6 fusion.106
  150.0 14.1 %collective-permute-done = bf16[128,2048]{1,0:T(8,128)(2,1)} collective-permute-done((bf16[128,2048]{1,0:T(8,128)(2,1)}, bf16[128,2048]{1,0:T(8,128)(2,1)}, u32[]{:S(2)}, u32[]{:S(2)}) %collective-permute-start) | collective-permute-done | bytes 524320 | tf_op jit(solution)/shard_map/ppermute | solution.py:601
  168.6 5.8 shard_map.265
  174.4 7.6 %all-to-all-done = bf16[64,16,2560]{2,1,0:T(8,128)(2,1)} async-done(((bf16[64,16,2560]{2,1,0:T(8,128)(2,1)}), bf16[64,16,2560]{2,1,0:T(8,128)(2,1)}, u32[]{:S(2)}, u32[]{:S(2)}) %all-to-all-start) | async-done | bytes 5242912 | tf_op jit(solution)/shard_map/all_to_all | solution.py:627
  182.0 9.3 %all-to-all-start.1 = ((bf16[64,16,2560]{2,1,0:T(8,128)(2,1)}), bf16[64,16,2560]{2,1,0:T(8,128)(2,1)}, u32[]{:S(2)}, u32[]{:S(2)}) async-start(bf16[64,16,2560]{2,1,0:T(8,128)(2,1)} %bitcast.258), calls=%async_computation.1 | async-start | bytes 10485760 | tf_op jit(solution)/shard_map/all_to_all | solution.py:627
  191.4 36.6 %collective-permute-done.1.up_o = bf16[2048,384]{1,0:T(8,128)(2,1)} collective-permute-done((bf16[2048,384]{1,0:T(8,128)(2,1)}, bf16[2048,384]{1,0:T(8,128)(2,1)}, u32[]{:S(2)}, u32[]{:S(2)}) %collective-permute-start.1) | collective-permute-done | bytes 1572896 | tf_op jit(solution)/shard_map/ppermute | solution.py:601
  228.0 26.0 %all-to-all-done.1 = bf16[64,16,2560]{2,1,0:T(8,128)(2,1)} async-done(((bf16[64,16,2560]{2,1,0:T(8,128)(2,1)}), bf16[64,16,2560]{2,1,0:T(8,128)(2,1)}, u32[]{:S(2)}, u32[]{:S(2)}) %all-to-all-start.1) | async-done | bytes 5242912 | tf_op jit(solution)/shard_map/all_to_all | solution.py:627
  253.9 39.5 %shard_map.266 = (bf16[1024,2560]{1,0:T(8,128)(2,1)}, bf16[1024,2560]{1,0:T(8,128)(2,1)}, bf16[1280,2048]{1,0:T(8,128)(2,1)}, bf16[1280,2048]{1,0:T(8,128)(2,1)}...) custom-call(bf16[1024,2560]{1,0:T(8,128)(2,1)} %bitcast.24.rows, ...), custom_call_target="tpu_custom_call" | custom-call | flops 24159191040 | bytes 45000000 | tf_op jit(solution)/shard_map/pallas_call | solution.py:533
  293.4 9.7 %all-to-all-start.2 = ((bf16[64,16,2560]{2,1,0:T(8,128)(2,1)}), bf16[64,16,2560]{2,1,0:T(8,128)(2,1)}, u32[]{:S(2)}, u32[]{:S(2)}) async-start(bf16[64,16,2560]{2,1,0:T(8,128)(2,1)} %bitcast.273), calls=%async_computation.2 | async-start | bytes 10485760 | tf_op jit(solution)/shard_map/all_to_all | solution.py:627
  304.6 4.5 copy.255
  325.3 7.0 %convolution_convert_fusion.2.gate = bf16[2048,384]{1,0:T(8,128)(2,1)} fusion(bf16[1280,2048]{1,0:T(8,128)(2,1)} %get-tuple-element.55, bf16[1280,768]{1,0:T(8,128)(2,1)} %get-tuple-element.64), kind=kOutput, calls=%fused_computation.22 | convolution fusion | flops 2014052352 | bytes 7798784 | tf_op jit(solution)/shard_map/dot_general | solution.py:560
  332.3 6.6 %convolution_convert_fusion.4 = bf16[2048,384]{1,0:T(8,128)(2,1)} fusion(bf16[1280,2048]{1,0:T(8,128)(2,1)} %get-tuple-element.55, bf16[1280,768]{1,0:T(8,128)(2,1)S(1)} %copy-done.70), kind=kOutput, calls=%fused_computation.24 | convolution fusion | flops 2014052352 | bytes 7798784 | tf_op jit(solution)/shard_map/dot_general | solution.py:560
  338.8 26.9 %all-to-all-done.2 = bf16[64,16,2560]{2,1,0:T(8,128)(2,1)} async-done(((bf16[64,16,2560]{2,1,0:T(8,128)(2,1)}), bf16[64,16,2560]{2,1,0:T(8,128)(2,1)}, u32[]{:S(2)}, u32[]{:S(2)}) %all-to-all-start.2) | async-done | bytes 5242912 | tf_op jit(solution)/shard_map/all_to_all | solution.py:627
  368.1 3.4 multiply_reduce_fusion.2
  373.6 3.5 convolution_convert_fusion.3.down
  377.1 10.4 %collective-permute-done.2 = bf16[128,2048]{1,0:T(8,128)(2,1)S(1)} collective-permute-done((bf16[128,2048]{1,0:T(8,128)(2,1)S(1)}, bf16[128,2048]{1,0:T(8,128)(2,1)S(1)}, u32[]{:S(2)}, u32[]{:S(2)}) %collective-permute-start.2) | collective-permute-done | bytes 524320 | tf_op jit(solution)/shard_map/ppermute | solution.py:601
  398.5 3.8 copy.285
  402.3 3.7 copy.286
  414.7 7.7 %all-to-all-start.3 = ((bf16[64,16,2560]{2,1,0:T(8,128)(2,1)}), bf16[64,16,2560]{2,1,0:T(8,128)(2,1)}, u32[]{:S(2)}, u32[]{:S(2)}) async-start(bf16[64,16,2560]{2,1,0:T(8,128)(2,1)} %bitcast.272), calls=%async_computation.3 | async-start | bytes 10485760 | tf_op jit(solution)/shard_map/all_to_all | solution.py:627
  433.6 4.4 fusion.38
  443.9 5.9 convolution_convert_fusion.1
  449.8 6.0 convolution_convert_fusion
  455.7 28.9 %all-to-all-done.3 = bf16[64,16,2560]{2,1,0:T(8,128)(2,1)} async-done(((bf16[64,16,2560]{2,1,0:T(8,128)(2,1)}), bf16[64,16,2560]{2,1,0:T(8,128)(2,1)}, u32[]{:S(2)}, u32[]{:S(2)}) %all-to-all-start.3) | async-done | bytes 5242912 | tf_op jit(solution)/shard_map/all_to_all | solution.py:627
  484.7 110.6 %shard_map.267 = (f32[32,2560]{1,0:T(8,128)}, f32[32,2048]{1,0:T(8,128)}, f32[8,2048]{1,0:T(8,128)}, bf16[128,2048]{1,0:T(8,128)(2,1)}, bf16[384,2048]{1,0:T(8,128)(2,1)}, /*index=5*/bf16[2048,384]{1,0:T(8,128)(2,1)}) custom-call(bf16[4,2,4,2,32,2560]{5,4,3,2,1,0:T(8,128)(2,1)} %bitcast.253, bf16[4,2,4,2,32,2048]{5,4,3,2,1,0:T(8,128)(2,1)} %bitcast.254, ...), custom_call_target="tpu_custom_call" | custom-call | flops 10000000 | bytes 300000000 | tf_op jit(solution)/shard_map/pallas_call | solution.py:225
  601.1 7.0 %add_bitcast_fusion = f32[1,384,2048]{2,1,0:T(8,128)} fusion(bf16[384,2048]{1,0:T(8,128)(2,1)} %get-tuple-element.71, bf16[1280,2048]{1,0:T(8,128)(2,1)} %get-tuple-element.63, bf16[1280,768]{1,0:T(8,128)(2,1)S(1)} %copy-done.41), kind=kOutput, calls=%fused_computation.19 | convolution fusion | flops 2014838784 | bytes 10944512 | tf_op jit(solution)/shard_map/dot_general | solution.py:560
  608.1 7.7 %add_bitcast_fusion.1 = f32[1,2048,384]{2,1,0:T(8,128)} fusion(bf16[2048,384]{1,0:T(8,128)(2,1)} %collective-permute-done.3, bf16[1280,2048]{1,0:T(8,128)(2,1)} %get-tuple-element.55, bf16[1280,768]{1,0:T(8,128)(2,1)S(1)} %copy-done.71), kind=kOutput, calls=%fused_computation.20 | convolution fusion | flops 2014838784 | bytes 10944512 | tf_op jit(solution)/shard_map/dot_general | solution.py:560
  615.9 4.7 add_bitcast_fusion.2
  628.3 3.9 bitcast_reduce_fusion
  640.6 4.0 fusion.29
  (290 shorter events, 121.3 us)
Async XLA Ops:
  2.5 6.0 copy-start.47
  8.5 8.2 %copy-start.63 = (f32[128]{0:T(128)}, f32[128]{0:T(128)S(1)}, u32[]{:S(2)}) copy-start(f32[128]{0:T(128)S(1)} %get-tuple-element.123) | copy-start | bytes 1540
  111.7 7.7 %copy-start.65 = (s32[256]{0:T(256)S(1)}, s32[256]{0:T(256)}, u32[]{:S(2)}) copy-start(s32[256]{0:T(256)} %param.17) | copy-start | bytes 3076
  111.7 7.7 %copy-start.27 = (bf16[2,128,2048]{2,1,0:T(8,128)(2,1)S(1)}, bf16[2,128,2048]{2,1,0:T(8,128)(2,1)}, u32[]{:S(2)}) copy-start(bf16[2,128,2048]{2,1,0:T(8,128)(2,1)} %get-tuple-element.43) | copy-start | bytes 3145732
  111.7 70.3 %all-to-all-start = ((bf16[64,16,2560]{2,1,0:T(8,128)(2,1)}), bf16[64,16,2560]{2,1,0:T(8,128)(2,1)}, u32[]{:S(2)}, u32[]{:S(2)}) async-start(bf16[64,16,2560]{2,1,0:T(8,128)(2,1)} %bitcast.257), calls=%async_computation | async-start | bytes 10485760 | tf_op jit(solution)/shard_map/all_to_all | solution.py:627
  125.0 6.1 copy-start.10
  132.4 5.8 copy-start.61
  134.0 6.8 %copy-start.5 = (bf16[256,16,64]{2,0,1:T(8,128)(2,1)}, bf16[256,16,64]{2,0,1:T(8,128)(2,1)S(1)}, u32[]{:S(2)}) copy-start(bf16[256,16,64]{2,0,1:T(8,128)(2,1)S(1)} %copy.235) | copy-start | bytes 1572868
  139.4 6.2 slice-start.5
  149.6 14.5 %collective-permute-start = (bf16[128,2048]{1,0:T(8,128)(2,1)}, bf16[128,2048]{1,0:T(8,128)(2,1)}, u32[]{:S(2)}, u32[]{:S(2)}) collective-permute-start(bf16[128,2048]{1,0:T(8,128)(2,1)} %dynamic-slice_convert_fusion.1), channel_id=1, source_target_pairs={{0,1},{1,0},{2,3},{3,2},{4,5},{5,4},{6,7},{7,6},{8,9},{9,8},{10,11... | collective-permute-start | bytes 1572872 | tf_op jit(solution)/shard_map/ppermute | solution.py:601
  182.0 72.0 %all-to-all-start.1 = ((bf16[64,16,2560]{2,1,0:T(8,128)(2,1)}), bf16[64,16,2560]{2,1,0:T(8,128)(2,1)}, u32[]{:S(2)}, u32[]{:S(2)}) async-start(bf16[64,16,2560]{2,1,0:T(8,128)(2,1)} %bitcast.258), calls=%async_computation.1 | async-start | bytes 10485760 | tf_op jit(solution)/shard_map/all_to_all | solution.py:627
  191.3 36.7 %collective-permute-start.1 = (bf16[2048,384]{1,0:T(8,128)(2,1)}, bf16[2048,384]{1,0:T(8,128)(2,1)}, u32[]{:S(2)}, u32[]{:S(2)}) collective-permute-start(bf16[2048,384]{1,0:T(8,128)(2,1)} %bitcast.317), channel_id=1, source_target_pairs={{0,1},{1,0},{2,3},{3,2},{4,5},{5,4},{6,7},{7,6},{8,9},{9,8},{10,11... | collective-permute-start | bytes 4718600 | tf_op jit(solution)/shard_map/ppermute | solution.py:601
  293.4 72.3 %all-to-all-start.2 = ((bf16[64,16,2560]{2,1,0:T(8,128)(2,1)}), bf16[64,16,2560]{2,1,0:T(8,128)(2,1)}, u32[]{:S(2)}, u32[]{:S(2)}) async-start(bf16[64,16,2560]{2,1,0:T(8,128)(2,1)} %bitcast.273), calls=%async_computation.2 | async-start | bytes 10485760 | tf_op jit(solution)/shard_map/all_to_all | solution.py:627
  311.8 6.1 copy-start.53
  325.2 7.0 %copy-start.70 = (bf16[1280,768]{1,0:T(8,128)(2,1)S(1)}, bf16[1280,768]{1,0:T(8,128)(2,1)}, u32[]{:S(2)}) copy-start(bf16[1280,768]{1,0:T(8,128)(2,1)} %get-tuple-element.56) | copy-start | bytes 5898244
  367.9 5.7 slice-start
  372.9 14.7 %collective-permute-start.2 = (bf16[128,2048]{1,0:T(8,128)(2,1)S(1)}, bf16[128,2048]{1,0:T(8,128)(2,1)S(1)}, u32[]{:S(2)}, u32[]{:S(2)}) collective-permute-start(bf16[128,2048]{1,0:T(8,128)(2,1)S(1)} %get-tuple-element.78), channel_id=1, source_target_pairs={{0,1},{1,0},{2,3},{3,2},{4,5},{5,4},{6,7},{7,6},{8,9},{9,8},{10,11... | collective-permute-start | bytes 1572872 | tf_op jit(solution)/shard_map/ppermute | solution.py:601
  373.6 14.1 %slice-start.7 = ((s8[8388608]{0:T(1024)(128)(4,1)}), s8[4194304]{0:T(1024)(128)(4,1)S(1)}, s32[]{:S(2)}) async-start(s8[8388608]{0:T(1024)(128)(4,1)} %bitcast.314), calls=%async_computation.11 | async-start | bytes 8388608
  373.6 14.1 %slice-start.8 = ((s8[8388608]{0:T(1024)(128)(4,1)}), s8[4194304]{0:T(1024)(128)(4,1)S(1)}, s32[]{:S(2)}) async-start(s8[8388608]{0:T(1024)(128)(4,1)} %bitcast.314), calls=%async_computation.12 | async-start | bytes 8388608
  414.6 41.1 %collective-permute-start.3 = (bf16[2048,384]{1,0:T(8,128)(2,1)}, bf16[2048,384]{1,0:T(8,128)(2,1)}, u32[]{:S(2)}, u32[]{:S(2)}) collective-permute-start(bf16[2048,384]{1,0:T(8,128)(2,1)} %convolution_convert_fusion.4), channel_id=1, source_target_pairs={{0,1},{1,0},{2,3},{3,2},{4,5},{5,4},{6,7},{7,6},{8,9},{9,8},{10,11... | collective-permute-start | bytes 4718600 | tf_op jit(solution)/shard_map/ppermute | solution.py:601
  414.7 70.0 %all-to-all-start.3 = ((bf16[64,16,2560]{2,1,0:T(8,128)(2,1)}), bf16[64,16,2560]{2,1,0:T(8,128)(2,1)}, u32[]{:S(2)}, u32[]{:S(2)}) async-start(bf16[64,16,2560]{2,1,0:T(8,128)(2,1)} %bitcast.272), calls=%async_computation.3 | async-start | bytes 10485760 | tf_op jit(solution)/shard_map/all_to_all | solution.py:627
  427.5 10.5 %slice-start.2 = ((s8[10485760]{0:T(1024)(128)(4,1)}), s8[4194304]{0:T(1024)(128)(4,1)S(1)}, s32[]{:S(2)}) async-start(s8[10485760]{0:T(1024)(128)(4,1)} %bitcast.308), calls=%async_computation.6 | async-start | bytes 8388608
  429.7 8.3 %slice-start.3 = ((s8[10485760]{0:T(1024)(128)(4,1)}), s8[4194304]{0:T(1024)(128)(4,1)S(1)}, s32[]{:S(2)}) async-start(s8[10485760]{0:T(1024)(128)(4,1)} %bitcast.308), calls=%async_computation.7 | async-start | bytes 8388608
  432.4 5.6 slice-start.4
  441.0 8.8 %copy-start.13 = (f32[256,2048]{1,0:T(8,128)}, f32[256,2048]{1,0:T(8,128)S(1)}, u32[]{:S(2)}) copy-start(f32[256,2048]{1,0:T(8,128)S(1)} %fusion.73) | copy-start | bytes 6291460
  443.9 5.9 copy-start.28
  484.7 116.4 %copy-start.41 = (bf16[1280,768]{1,0:T(8,128)(2,1)S(1)}, bf16[1280,768]{1,0:T(8,128)(2,1)}, u32[]{:S(2)}) copy-start(bf16[1280,768]{1,0:T(8,128)(2,1)} %get-tuple-element.62) | copy-start | bytes 5898244
  601.1 7.0 %copy-start.71 = (bf16[1280,768]{1,0:T(8,128)(2,1)S(1)}, bf16[1280,768]{1,0:T(8,128)(2,1)}, u32[]{:S(2)}) copy-start(bf16[1280,768]{1,0:T(8,128)(2,1)} %get-tuple-element.56) | copy-start | bytes 5898244
  601.1 14.8 %slice-start.9 = ((s8[5242880]{0:T(1024)(128)(4,1)}), s8[4194304]{0:T(1024)(128)(4,1)S(1)}, s32[]{:S(2)}) async-start(s8[5242880]{0:T(1024)(128)(4,1)} %bitcast.319), calls=%async_computation.13 | async-start | bytes 8388608
  608.1 7.7 %copy-start.68 = (bf16[2048,384]{1,0:T(8,128)(2,1)S(1)}, bf16[2048,384]{1,0:T(8,128)(2,1)}, u32[]{:S(2)}) copy-start(bf16[2048,384]{1,0:T(8,128)(2,1)} %get-tuple-element.69) | copy-start | bytes 4718596
  608.1 7.7 %slice-start.10 = ((s8[5242880]{0:T(1024)(128)(4,1)}), s8[1048576]{0:T(1024)(128)(4,1)S(1)}, s32[]{:S(2)}) async-start(s8[5242880]{0:T(1024)(128)(4,1)} %bitcast.319), calls=%async_computation.14 | async-start | bytes 2097152
  608.1 7.7 %copy-start.69 = (bf16[1280,768]{1,0:T(8,128)(2,1)S(1)}, bf16[1280,768]{1,0:T(8,128)(2,1)}, u32[]{:S(2)}) copy-start(bf16[1280,768]{1,0:T(8,128)(2,1)} %get-tuple-element.64) | copy-start | bytes 5898244
  (59 other events, 172.9 us)

commit v4 on v3

--- a/solution.py
+++ b/solution.py
@@ -58,8 +58,8 @@
 def reduce_kernel(
     ga, gb, gain, d_own, d_sent, x_hat, down, gate,
     oa, ob, og, d_came, down_c, gate_c,
-    own_a, got_a, one_a, two_a, sum_a, three_a,
-    own_b, got_b, one_b, two_b, sum_b, three_b,
+    own_a, got_a, one_a, via_a, two_a, sum_a, three_a,
+    own_b, got_b, one_b, via_b, two_b, sum_b, three_b,
     vec, vecs,
     load_sem, core_send, core_recv, one_send, one_recv, two_send, two_recv,
     three_send, three_recv, vec_send, vec_recv, pair_send, pair_recv,
@@ -114,7 +114,7 @@
     d_copy = send(d_sent, d_came, pair_send.at[0], pair_recv.at[0], partner)
 
     loads, swaps = {}, {}
-    order = STEPS + (0,)
+    order = (2, 1, 3, 0)
     for i, s in enumerate(order):
         to = turn(z, s)
         swaps["a", s] = send(ga.at[to, :, :, 1 - core], got_a.at[to], core_send.at[0, i], core_recv.at[0, i], sibling)
@@ -134,46 +134,85 @@
             def _(j):
                 own[to, i, j] = (own[to, i, j].astype(F32) + got[to, i, j].astype(F32)).astype(BF16)
 
-    ones = []
-    expert = []
-    for i, s in enumerate(order):
-        if i == 1:
-            d_copy.wait_recv()
-            vec_start(0)
-            expert.append(send(down, down_c, pair_send.at[1], pair_recv.at[1], partner))
-            expert.append(send(gate, gate_c, pair_send.at[2], pair_recv.at[2], partner))
-        loads["a", s].wait()
-        swaps["a", s].wait_recv()
-        add_cores(own_a, got_a, turn(z, s))
-        if s:
-            ones.append(send(own_a.at[turn(z, s)], one_a.at[i], one_send.at[0, i], one_recv.at[0, i], along_z[i]))
-        loads["b", s].wait()
-        swaps["b", s].wait_recv()
-        add_cores(own_b, got_b, turn(y, s))
-        if s:
-            ones.append(send(own_b.at[turn(y, s)], one_b.at[i], one_send.at[1, i], one_recv.at[1, i], along_y[i]))
+    def round_ring(own, got, via, one, at, up, down, name, row):
+        n = own.shape[1] // 2
+        halves = pl.ds(0, n), pl.ds(n, n)
+        above, far, below = turn(at, 1), turn(at, 2), turn(at, 3)
+
+        def step(src, dst, i, to):
+            return send(src, dst, one_send.at[row, i], one_recv.at[row, i], to)
+
+        def ready(s):
+            loads[name, s].wait()
+            swaps[name, s].wait_recv()
+            add_cores(own, got, turn(at, s))
+
+        def pass_on(k, to):
+            first = k * n
+
+            @pl.loop(0, n)
+            def _(i):
+                @pl.loop(0, own.shape[2])
+                def _(j):
+                    own[to, first + i, j] = (
+                        own[to, first + i, j].astype(F32) + via[k, i, j].astype(F32)
+                    ).astype(BF16)
+
+        ready(2)
+        copies = [step(own.at[far, halves[0]], via.at[0], 0, up), step(own.at[far, halves[1]], via.at[1], 1, down)]
+        yield copies
+        ready(1)
+        copies.append(step(own.at[above, halves[1]], one.at[0, halves[1]], 2, up))
+        yield
+        ready(3)
+        copies.append(step(own.at[below, halves[0]], one.at[1, halves[0]], 3, down))
+        yield
+        copies[0].wait_recv()
+        pass_on(0, above)
+        copies.append(step(own.at[above, halves[0]], one.at[0, halves[0]], 4, up))
+        yield
+        copies[1].wait_recv()
+        pass_on(1, below)
+        copies.append(step(own.at[below, halves[1]], one.at[1, halves[1]], 5, down))
+        yield
+        ready(0)
+        yield
+
+    rings = [
+        round_ring(own_a, got_a, via_a, one_a, z, along_z[0], along_z[1], "a", 0),
+        round_ring(own_b, got_b, via_b, one_b, y, along_y[0], along_y[1], "b", 1),
+    ]
+    firsts = [next(r) for r in rings]
+    d_copy.wait_recv()
+    vec_start(0)
+    expert = [
+        send(down, down_c, pair_send.at[1], pair_recv.at[1], partner),
+        send(gate, gate_c, pair_send.at[2], pair_recv.at[2], partner),
+    ]
+    for _ in range(5):
+        for r in rings:
+            next(r)
+    ones = firsts[0] + firsts[1]
     vec_finish(0)
     vec_start(1)
 
-    for copy in ones:
+    for copy in firsts[0][2:] + firsts[1][2:]:
         copy.wait_recv()
     vec_finish(1)
     vec_start(2)
     twos = []
-    for i, s in enumerate(order):
+    for i, s in enumerate(STEPS + (0,)):
         to = turn(y, s)
         for k in range(2):
             sum_a[to, k] = (
-                own_a[z, k, to].astype(F32) + one_a[0, k, to].astype(F32)
-                + one_a[1, k, to].astype(F32) + one_a[2, k, to].astype(F32)
+                own_a[z, k, to].astype(F32) + one_a[0, k, to].astype(F32) + one_a[1, k, to].astype(F32)
             ).astype(BF16)
         if s:
             twos.append(send(sum_a.at[to], two_a.at[i], two_send.at[0, i], two_recv.at[0, i], along_y[i]))
         to = turn(z, s)
         for k in range(2):
             sum_b[to, k] = (
-                own_b[y, to, k].astype(F32) + one_b[0, to, k].astype(F32)
-                + one_b[1, to, k].astype(F32) + one_b[2, to, k].astype(F32)
+                own_b[y, to, k].astype(F32) + one_b[0, to, k].astype(F32) + one_b[1, to, k].astype(F32)
             ).astype(BF16)
         if s:
             twos.append(send(sum_b.at[to], two_b.at[i], two_send.at[1, i], two_recv.at[1, i], along_z[i]))
@@ -216,7 +255,8 @@
         return [
             vmem((4,) + inner + (rows, cols), BF16),
             vmem((4,) + inner + (rows, cols), BF16),
-            vmem((3,) + inner + (rows, cols), BF16),
+            vmem((2,) + inner + (rows, cols), BF16),
+            vmem((2, inner[0] // 2, inner[1], rows, cols), BF16),
             vmem((3, 2, rows, cols), BF16),
             vmem((4, 2, rows, cols), BF16),
             vmem((2, rows, cols), BF16),
@@ -241,8 +281,8 @@
             dma((2, 4)),
             dma((2, 4)),
             dma((2, 4)),
-            dma((2, 3)),
-            dma((2, 3)),
+            dma((2, 6)),
+            dma((2, 6)),
             dma((2, 3)),
             dma((2, 3)),
             dma((2,)),
@@ -572,29 +612,170 @@
     return (d_values, jnp.sum(grad * values * scale, axis=axes))
 
 
+def head_columns(at):
+    return pl.ds(pl.multiple_of(at * HD, HD), HD)
+
+
+def head_probs(query, key):
+    scores = dot(query, key, ((1,), (1,))) * HD ** (-0.5)
+    shape = scores.shape
+    causal = lax.broadcasted_iota(jnp.int32, shape, 0) >= lax.broadcasted_iota(jnp.int32, shape, 1)
+    scores = jnp.where(causal, scores, -1e30)
+    powers = jnp.exp(scores - jnp.max(scores, axis=-1, keepdims=True))
+    return powers / jnp.sum(powers, axis=-1, keepdims=True)
+
+
+def attend_kernel(query_heads, key_heads, raw, cosine, sine, query_gain, key_gain, query, key, value, mixed):
+    group = query_heads // key_heads
+
+    def turned(values, gain):
+        values = values * rms_scale(values) * gain[...]
+        return (values * cosine[...] - pltpu.roll(values, HD // 2, 1) * sine[...]).astype(BF16)
+
+    for g in range(key_heads):
+        own = head_columns(g)
+        key[:, own] = turned(raw[:, head_columns(query_heads + g)], key_gain)
+        value[:, own] = raw[:, head_columns(query_heads + key_heads + g)].astype(BF16)
+
+        @pl.loop(g * group, (g + 1) * group)
+        def _(h):
+            at = head_columns(h)
+            query[:, at] = turned(raw[:, at], query_gain)
+            probs = head_probs(query[:, at], key[:, own])
+            mixed[:, at] = dot(probs.astype(BF16), value[:, own], ((1,), (0,))).astype(BF16)
+
+
+def attend(raw, cosine, sine, query_gain, key_gain, query_heads, key_heads):
+    length = raw.shape[0]
+    cols = [query_heads * HD, key_heads * HD, key_heads * HD, query_heads * HD]
+    return pl.pallas_call(
+        functools.partial(attend_kernel, query_heads, key_heads),
+        out_shape=[jax.ShapeDtypeStruct((length, c), BF16) for c in cols],
+        in_specs=[VMEM_SPEC] * 5,
+        out_specs=[VMEM_SPEC] * 4,
+        compiler_params=pltpu.CompilerParams(vmem_limit_bytes=48 * 1024 * 1024),
+        cost_estimate=pl.CostEstimate(flops=600_000_000, bytes_accessed=6_000_000, transcendentals=1_100_000),
+    )(raw, cosine, sine, query_gain[None], key_gain[None])
+
+
+def attend_back_kernel(
+    query_heads, key_heads, raw, cosine, sine, query_gain, key_gain, query, key, value, d_mixed,
+    d_raw, gain_sums, d_key, d_value,
+):
+    group = query_heads // key_heads
+    scale = HD ** (-0.5)
+
+    def through_norm(values, gain, d_turned, row):
+        d_out = d_turned * cosine[...] + pltpu.roll(d_turned, HD // 2, 1) * sine[...]
+        norm = rms_scale(values)
+        scaled = gain[...] * d_out
+        inner = jnp.mean(scaled * values, axis=-1, keepdims=True)
+        gain_sums[row : row + 1] += jnp.sum(d_out * values * norm, axis=0, keepdims=True)
+        return (norm * scaled - values * (norm * norm * norm) * inner).astype(BF16)
+
+    gain_sums[...] = jnp.zeros_like(gain_sums)
+    for g in range(key_heads):
+        own = head_columns(g)
+        d_key[...] = jnp.zeros_like(d_key)
+        d_value[...] = jnp.zeros_like(d_value)
+
+        @pl.loop(g * group, (g + 1) * group)
+        def _(h):
+            at = head_columns(h)
+            probs = head_probs(query[:, at], key[:, own])
+            d_probs = dot(d_mixed[:, at], value[:, own], ((1,), (1,)))
+            d_value[...] += dot(probs.astype(BF16), d_mixed[:, at], ((0,), (0,)))
+            delta = jnp.sum(probs * d_probs, axis=-1, keepdims=True)
+            d_scores = (probs * (d_probs - delta)).astype(BF16)
+            d_key[...] += dot(d_scores, query[:, at], ((0,), (0,)))
+            d_query = dot(d_scores, key[:, own], ((1,), (0,))) * scale
+            d_raw[:, at] = through_norm(raw[:, at], query_gain, d_query, 0)
+
+        at = head_columns(query_heads + g)
+        d_raw[:, at] = through_norm(raw[:, at], key_gain, d_key[...] * scale, 1)
+        d_raw[:, head_columns(query_heads + key_heads + g)] = d_value[...].astype(BF16)
+
+
+def attend_back(raw, cosine, sine, query_gain, key_gain, query, key, value, d_mixed):
+    length = raw.shape[0]
+    query_heads, key_heads = query.shape[1] // HD, key.shape[1] // HD
+    return pl.pallas_call(
+        functools.partial(attend_back_kernel, query_heads, key_heads),
+        out_shape=(
+            jax.ShapeDtypeStruct(raw.shape, BF16),
+            jax.ShapeDtypeStruct((8, HD), F32),
+        ),
+        in_specs=[VMEM_SPEC] * 9,
+        out_specs=[VMEM_SPEC] * 2,
+        scratch_shapes=[pltpu.VMEM((length, HD), F32), pltpu.VMEM((length, HD), F32)],
+        compiler_params=pltpu.CompilerParams(vmem_limit_bytes=48 * 1024 * 1024),
+        cost_estimate=pl.CostEstimate(flops=1_000_000, bytes_accessed=1_000_000, transcendentals=0),
+    )(raw, cosine, sine, query_gain[None], key_gain[None], query, key, value, d_mixed)
+
+
+def output_kernel(returned, place, part, place_weight, part_weight, grad, base, out, of_expert, total):
+    step = pl.program_id(0)
+    width = grad.shape[1]
+    tokens = grad.shape[0]
+    cut = width // CHUNKS
+
+    @pl.when(step == 0)
+    def _():
+        total[...] = base[...]
+
+    def combine(weights, values):
+        high = weights.astype(BF16)
+        low = (weights - high.astype(F32)).astype(BF16)
+        return dot(high, values, ((0,), (0,))) + dot(low, values, ((0,), (0,)))
+
+    main, rest = returned[:, :width], returned[:, width:]
+    total[...] += combine(place[...].astype(F32) * place_weight[...], main)
+    products = dot(main, grad[...], ((1,), (1,))) * place[...].astype(F32)
+    for j in range(CHUNKS):
+        chosen = part[:, j * tokens : (j + 1) * tokens].astype(F32)
+        at = slice(j * cut, (j + 1) * cut)
+        total[:, at] += combine(chosen * part_weight[...], rest)
+        products += dot(rest, grad[:, at], ((1,), (1,))) * chosen
+    of_expert[...] = jnp.sum(products.reshape(-1, ROWS_FULL, tokens), axis=1)
+
+    @pl.when(step == pl.num_programs(0) - 1)
+    def _():
+        out[...] = total[...].astype(BF16)
+
+
+def finish_output(returned, place, part, place_weight, part_weight, grad, base):
+    total, packed = returned.shape
+    tokens, width = grad.shape
+    groups = 4
+    block = total // groups
+
+    def cut(rows, cols):
+        return pl.BlockSpec((rows, cols), lambda g: (g, 0))
+
+    def fixed(cols):
+        return pl.BlockSpec((tokens, cols), lambda g: (0, 0))
+
+    return pl.pallas_call(
+        output_kernel,
+        grid=(groups,),
+        out_shape=(
+            jax.ShapeDtypeStruct((tokens, width), BF16),
+            jax.ShapeDtypeStruct((total // ROWS_FULL, tokens), F32),
+        ),
+        in_specs=[cut(block, packed), cut(block, tokens), cut(block, CHUNKS * tokens), cut(block, 1), cut(block, 1)]
+        + [fixed(width), fixed(width)],
+        out_specs=[fixed(width), cut(block // ROWS_FULL, tokens)],
+        scratch_shapes=[pltpu.VMEM((tokens, width), F32)],
+        cost_estimate=pl.CostEstimate(flops=3_000_000_000, bytes_accessed=10_000_000, transcendentals=0),
+    )(returned, place, part, place_weight, part_weight, grad, base)
+
+
 def rope_tables(positions, head_size):
     half = head_size // 2
     freqs = jnp.exp(jnp.arange(half, dtype=F32) * (-2.0 * math.log(THETA) / head_size))
     angles = positions.astype(F32)[:, None] * freqs[None, :]
-    return (jnp.cos(angles)[:, None, :], jnp.sin(angles)[:, None, :])
-
-
-def rotate(values, cosine, sine):
-    half = values.shape[-1] // 2
-    first = values[..., :half]
-    second = values[..., half:]
-    return jnp.concatenate(
-        [first * cosine - second * sine, second * cosine + first * sine], axis=-1
-    )
-
-
-def rotate_back(grad, cosine, sine):
-    half = grad.shape[-1] // 2
-    first = grad[..., :half]
-    second = grad[..., half:]
-    return jnp.concatenate(
-        [first * cosine + second * sine, second * cosine - first * sine], axis=-1
-    )
+    cosine, sine = jnp.cos(angles), jnp.sin(angles)
+    return jnp.concatenate([cosine, cosine], axis=1), jnp.concatenate([sine, -sine], axis=1)
 
 
 def swap(values):
@@ -664,7 +845,6 @@
     )
     q_cols, k_cols = query_weight.shape[1], key_weight.shape[1]
     query_heads, key_heads = q_cols // HD, k_cols // HD
-    group = query_heads // key_heads
 
     names = routed_experts[:, :, None] == jnp.arange(experts, dtype=jnp.int32)
     chosen = jnp.any(names, axis=1)
@@ -689,9 +869,6 @@
     def to_experts(packed):
         return exchange(packed.reshape(experts, ROWS_FULL, -1)).reshape(packed_rows, -1)
 
-    def quarters(values):
-        return values.reshape(rows, CHUNKS, -1).transpose(1, 0, 2).reshape(CHUNKS * rows, -1)
-
     def to_tokens(packed, place, part):
         first = dot(place, packed[:, :width], ((0,), (0,)))
         rest = dot(part, packed[:, width:], ((0,), (0,)))
@@ -702,30 +879,10 @@
     d_rows, whole = lax.optimization_barrier((d_rows, whole))
     expert_grads = to_experts(d_rows)
 
-    length = whole.shape[0]
     cosine, sine = rope_tables(positions, HD)
     raw = dot(whole, in_full, ((1,), (0,)))
-    query_raw = raw[:, :q_cols].reshape(length, query_heads, HD)
-    key_raw = raw[:, q_cols : q_cols + k_cols].reshape(length, key_heads, HD)
-    value_low = raw[:, q_cols + k_cols :].astype(BF16).reshape(length, key_heads, HD)
-    query_scale = rms_scale(query_raw)
-    query = (
-        rotate(query_raw * query_scale * query_gain, cosine, sine)
-        .astype(BF16)
-        .reshape(length, key_heads, group, HD)
-    )
-    key_scale = rms_scale(key_raw)
-    key = rotate(key_raw * key_scale * key_gain, cosine, sine).astype(BF16)
-    causal = jnp.arange(length)[:, None] >= jnp.arange(length)[None, :]
-    scores = jnp.einsum("ahgd,bhd->hgab", query, key, preferred_element_type=F32) * scale
-    scores = jnp.where(causal, scores, -1e30)
-    peak = jnp.max(scores, axis=-1, keepdims=True)
-    log_total = peak + jnp.log(jnp.sum(jnp.exp(scores - peak), axis=-1, keepdims=True))
-    probs_low = jnp.exp(scores - log_total).astype(BF16)
-    mixed = (
-        jnp.einsum("hgab,bhd->ahgd", probs_low, value_low, preferred_element_type=F32)
-        .astype(BF16)
-        .reshape(length, q_cols)
+    query, key, value, mixed = attend(
+        raw, cosine, sine, query_gain, key_gain, query_heads, key_heads
     )
     attended = sum_sequence(dot(mixed, out_full, ((1,), (1,))), rows)
     hidden_in = inputs + attended
@@ -745,42 +902,18 @@
         for of in (slice(0, units), slice(units, 2 * units))
     ]
     sent = [dot(left, right, ((0,), (0,))).astype(BF16) for left, right in others]
-
+    kept = [dot(left, right, ((0,), (0,))) for left, right in halves]
+    gate_came = swap(sent[1])
+
+    back_rows, result, gate_came, *kept = lax.optimization_barrier((back_rows, result, gate_came, *kept))
     d_mid = to_tokens(back_rows, place, part)
     d_mid_in, grad_norm_mid = norm_back(hidden_in, mid_scale, norm_mid, d_mid)
     d_hidden_in = grad + d_mid_in
     d_attended = d_hidden_in.astype(BF16)
     d_whole = share_sequence(d_attended)
-    d_whole, result, up_sent = lax.optimization_barrier((d_whole, result, sent[2]))
-    up_came = swap(up_sent)
-    d_mixed = (
-        dot(d_whole, out_full, ((1,), (0,))).astype(BF16).reshape(length, key_heads, group, HD)
-    )
-    probs = jnp.exp(scores - log_total)
-    d_probs = jnp.einsum("ahgd,bhd->hgab", d_mixed, value_low, preferred_element_type=F32)
-    value_grad = jnp.einsum("hgab,ahgd->bhd", probs_low, d_mixed, preferred_element_type=F32)
-    delta = jnp.sum(probs * d_probs, axis=-1, keepdims=True)
-    d_scores = (probs * (d_probs - delta)).astype(BF16)
-    d_query = (
-        jnp.einsum("hgab,bhd->ahgd", d_scores, key, preferred_element_type=F32).reshape(
-            length, query_heads, HD
-        )
-        * scale
-    )
-    d_key = jnp.einsum("hgab,ahgd->bhd", d_scores, query, preferred_element_type=F32) * scale
-    d_query_raw, grad_query_gain = norm_back(
-        query_raw, query_scale, query_gain, rotate_back(d_query, cosine, sine)
-    )
-    d_key_raw, grad_key_gain = norm_back(
-        key_raw, key_scale, key_gain, rotate_back(d_key, cosine, sine)
-    )
-    d_raw = jnp.concatenate(
-        [
-            d_query_raw.astype(BF16).reshape(length, q_cols),
-            d_key_raw.astype(BF16).reshape(length, k_cols),
-            value_grad.astype(BF16).reshape(length, k_cols),
-        ],
-        axis=1,
+    d_mixed = dot(d_whole, out_full, ((1,), (0,))).astype(BF16)
+    d_raw, gain_sums = attend_back(
+        raw, cosine, sine, query_gain, key_gain, query, key, value, d_mixed
     )
     d_total = dot(d_raw, in_full, ((1,), (1,)))
     d_own, d_sent = halves_of(d_total, rows)
@@ -788,31 +921,22 @@
     returned = to_experts(result)
     in_grads = dot(whole, d_raw, ((0,), (0,))).astype(BF16)
     out_grads = dot(d_whole, mixed, ((0,), (0,))).astype(BF16)
-    gains = jnp.pad(
-        jnp.stack([grad_norm_mid, jnp.pad(jnp.concatenate([grad_query_gain, grad_key_gain]), (0, width - 2 * HD))]),
-        ((1, 5), (0, 0)),
-    )
-    in_grads, returned, up_came = lax.optimization_barrier((in_grads, returned, up_came))
-    in_total, out_total, gains, d_came, *came = reduce_grads(
-        in_grads, out_grads, gains, d_own, d_sent.astype(BF16), inputs * in_scale, sent[:2]
-    )
-    place_high = (place * place_weight).astype(BF16)
-    part_high = (part * part_weight).astype(BF16)
-    place_low = (place * place_weight - place_high.astype(F32)).astype(BF16)
-    part_low = (part * part_weight - part_high.astype(F32)).astype(BF16)
-    moe = to_tokens(returned, place_high, part_high) + to_tokens(returned, place_low, part_low)
-    output = (hidden_in + moe).astype(BF16)
-    products = dot(returned[:, :width], out_grad, ((1,), (1,))) * place
-    rest = dot(returned[:, width:], quarters(out_grad), ((1,), (1,))) * part
-    of_row = products + jnp.sum(rest.reshape(packed_rows, CHUNKS, rows), axis=1)
-    of_expert = jnp.sum(of_row.reshape(experts, ROWS_FULL, rows), axis=1).T
+    gain_row = jnp.pad(gain_sums[:2].reshape(1, -1), ((0, 0), (0, width - 2 * HD)))
+    gains = jnp.pad(jnp.concatenate([grad_norm_mid[None], gain_row]), ((1, 5), (0, 0)))
+    in_grads, returned = lax.optimization_barrier((in_grads, returned))
+    in_total, out_total, gains, d_came, down_came, up_came = reduce_grads(
+        in_grads, out_grads, gains, d_own, d_sent.astype(BF16), inputs * in_scale, (sent[0], sent[2])
+    )
+    output, of_expert = finish_output(
+        returned, place, part, place_weight, part_weight, out_grad, hidden_in
+    )
+    of_expert = of_expert.T
     grad_route = jnp.sum(jnp.where(names, of_expert[:, None, :], 0.0), axis=2)
     d_normed = d_own + d_came.astype(F32)
     d_inputs, _ = norm_back(inputs, in_scale, norm_in, d_normed)
     grad_tokens = (d_hidden_in + d_inputs).astype(BF16)
     grad_down, grad_gate, grad_up = [
-        (dot(left, right, ((0,), (0,))) + half.astype(F32))[None]
-        for (left, right), half in zip(halves, (*came, up_came))
+        (own + half.astype(F32))[None] for own, half in zip(kept, (down_came, gate_came, up_came))
     ]
     grad_norm_in, grad_norm_mid = gains[0], gains[1]
     grad_query_gain, grad_key_gain = gains[2, :HD], gains[2, HD : 2 * HD]

time: 653 us -> 574 us (0.88)
  local copies, waits for them, and re-layouts: 64.8 us -> 15.1 us
  matrix products: 94.2 us -> 64.3 us
  Pallas kernels: 257 us -> 284 us
  other arithmetic: 42.7 us -> 26.5 us
  waiting for transfers between devices: 150 us -> 137 us
    pallas_call x0 -> x3, Pallas kernels: none -> 35.8 us  [the longest x1 15.2 us: attend_back(): pl.pallas_call(functools.partial(attend_back_kernel, query_heads, key_hea...]
    all_to_all x4, waiting for transfers between devices: 89.4 us -> 62.2 us  [exchange(): lax.all_to_all(buffer, ('dp', 'tensor'), split_axis=0, concat_axis=0, til...]
    dot_general x21 -> x15, matrix products: 85.5 us -> 64.3 us  [dot(): lax.dot_general(left, right, (contract, ((), ())), preferred_element_type...]
    unnamed x174 -> x75, local copies, waits for them, and re-layouts: 19.8 us -> 2.93 us
    ppermute x4, waiting for transfers between devices: 61.1 us -> 75.3 us  [swap(): return lax.ppermute(values, 'tensor', [(0, 1), (1, 0)])]
    broadcast_in_dim x0 -> x3, other arithmetic: none -> 9.95 us  [per_device(): (own + half.astype(F32))[None]]
    pallas_call x1, Pallas kernels: 111 us -> 102 us  [reduce_grads(): pl.pallas_call(reduce_kernel, out_shape=(jax.ShapeDtypeStruct((rows, a_co...]
    dot_general x6 -> x0, matrix products: 8.66 us -> none  [the longest x1 3.13 us: per_device(): jnp.einsum('hgab,ahgd->bhd', probs_low, d_mixed, preferred_element_type=F32)]
  transfers between devices with their start and end apart: 8 -> 8, of which waited for: 7 -> 8; matrix products, arithmetic and copies ran while one was open for 16% -> 14% of each run, Pallas kernels for 1% -> 6%
where the time goes in v4:
time: 574 us; the launch traced here: 565 us
  Pallas kernels  284 us (49%)
  waiting for transfers between devices  137 us (24%)
  matrix products  64.3 us (11%)
  starting transfers between devices  36.4 us (6%)
  other arithmetic  26.5 us (5%)
  local copies, waits for them, and re-layouts  15.1 us (3%)
    pallas_call x1, Pallas kernels, reduce_grads(): pl.pallas_call(reduce_kernel, out_shape=(jax.ShapeDtypeStruct((rows, a_co...  102 us
    pallas_call x1, Pallas kernels, gather_weights(): pl.pallas_call(gather_kernel, out_shape=(jax.ShapeDtypeStruct((4, 2, 4, 2...  94.9 us
    ppermute x4, waiting for transfers between devices, swap(): return lax.ppermute(values, 'tensor', [(0, 1), (1, 0)])  75.3 us
    dot_general x15, matrix products, dot(): lax.dot_general(left, right, (contract, ((), ())), preferred_element_type...  64.3 us
    all_to_all x4, waiting for transfers between devices, exchange(): lax.all_to_all(buffer, ('dp', 'tensor'), split_axis=0, concat_axis=0, til...  62.2 us
    pallas_call x1, Pallas kernels, run_expert(): pl.pallas_call(expert_kernel, grid=(groups,), out_shape=(jax.ShapeDtypeSt...  39.3 us
    all_to_all x4, starting transfers between devices, exchange(): lax.all_to_all(buffer, ('dp', 'tensor'), split_axis=0, concat_axis=0, til...  35.6 us
    pallas_call x1, Pallas kernels, attend_back(): pl.pallas_call(functools.partial(attend_back_kernel, query_heads, key_hea...  15.2 us
  transfers between devices with their start and end apart: 8, of which 8 were waited for; matrix products, arithmetic and copies ran while one was open for 14% of the time, Pallas kernels for 6%

profile of v4, /device:TPU:0, one launch (start us, length us, event | category | flops | bytes accessed | tf_op | source)
XLA Modules:
  0.0 564.8 jit_solution(7429122326324211213)
XLA Ops:
  11.6 6.2 %shard_map.263 = bf16[1024,2560]{1,0:T(8,128)(2,1)} custom-call(bf16[128,2048]{1,0:T(8,128)(2,1)} %grad.1, bf16[1024,128]{1,0:T(8,128)(2,1)} %get-tuple-element.113.place, bf16[1024,512]{1,0:T(8,128)(2,1)} %get-tuple-element.105.part, f32[1024,1]{1,0:T(8,128)} %reshape.207.refs_0_.place_weight, f32[1024,1]{1,0:T(8,128)} %reshape.208.refs_1_.part_weight), custom_call_target="tpu_custom_call" | custom-call | flops 1000000000 | bytes 8000000 | tf_op jit(solution)/shard_map/pallas_call | solution.py:480
  17.8 94.9 %shard_map.264 = (bf16[4,2,4,2,32,2560]{5,4,3,2,1,0:T(8,128)(2,1)}, bf16[4,2,4,2,32,2048]{5,4,3,2,1,0:T(8,128)(2,1)}, bf16[2,128,2048]{2,1,0:T(8,128)(2,1)}, bf16[384,2048]{1,0:T(8,128)(2,1)}, bf16[2048,384]{1,0:T(8,128)(2,1)}) custom-call(bf16[32,2560]{1,0:T(8,128)(2,1)} %pad_maximum_fusion.3.sa, bf16[32,2048]{1,0:T(8,128)(2,1)} %bitcast.98, ...), custom_call_target="tpu_custom_call" | custom-call | bytes 250000000 | tf_op jit(solution)/shard_map/pallas_call | solution.py:420
  112.8 7.4 %all-to-all-start = ((bf16[64,16,2560]{2,1,0:T(8,128)(2,1)}), bf16[64,16,2560]{2,1,0:T(8,128)(2,1)}, u32[]{:S(2)}, u32[]{:S(2)}) async-start(bf16[64,16,2560]{2,1,0:T(8,128)(2,1)} %bitcast.82), calls=%async_computation | async-start | bytes 10485760 | tf_op jit(solution)/shard_map/all_to_all | solution.py:808
  120.9 5.7 %fusion.33.raw = f32[256,2560]{1,0:T(8,128)S(1)} fusion(bf16[256,2048]{1,0:T(8,128)(2,1)S(1)} %bitcast.90, bf16[2048,2560]{1,0:T(8,128)(2,1)} %bitcast.105), kind=kOutput, calls=%fused_computation.93 | convolution fusion | flops 2684354560 | bytes 14155776 | tf_op jit(solution)/shard_map/dot_general | solution.py:600
  126.7 11.9 %shard_map.265 = (bf16[256,2048]{1,0:T(8,128)(2,1)S(1)}, bf16[256,256]{1,0:T(8,128)(2,1)S(1)}, bf16[256,256]{1,0:T(8,128)(2,1)S(1)}, bf16[256,2048]{1,0:T(8,128)(2,1)S(1)}) custom-call(f32[256,2560]{1,0:T(8,128)S(1)} %fusion.33.raw, f32[256,128]{1,0:T(8,128)S(1)} %get-tuple-element.124.cosine, f32[256,128]{1,0:T(8,128)S(1)} %get-tuple-element.125.sine, ...), custom_call_target="tpu_custom_call" | custom-call | flops 600000000 | bytes 6000000 | tf_op jit(solution)/shard_map/pallas_call | solution.py:651
  138.6 6.5 %fusion.34 = f32[256,2048]{1,0:T(8,128)S(1)} fusion(bf16[256,2048]{1,0:T(8,128)(2,1)S(1)} %get-tuple-element.59, bf16[2048,2048]{1,0:T(8,128)(2,1)} %bitcast.107), kind=kOutput, calls=%fused_computation.94 | convolution fusion | flops 2147483648 | bytes 11534336 | tf_op jit(solution)/shard_map/dot_general | solution.py:600
  146.7 13.7 %collective-permute-done = bf16[128,2048]{1,0:T(8,128)(2,1)} collective-permute-done((bf16[128,2048]{1,0:T(8,128)(2,1)S(1)}, bf16[128,2048]{1,0:T(8,128)(2,1)}, u32[]{:S(2)}, u32[]{:S(2)}) %collective-permute-start) | collective-permute-done | bytes 524320 | tf_op jit(solution)/shard_map/ppermute | solution.py:782
  163.2 5.8 %shard_map.266 = bf16[1024,2560]{1,0:T(8,128)(2,1)} custom-call(bf16[128,2048]{1,0:T(8,128)(2,1)} %multiply_convert_fusion.values, bf16[1024,128]{1,0:T(8,128)(2,1)} %get-tuple-element.113.place, bf16[1024,512]{1,0:T(8,128)(2,1)} %get-tuple-element.105.part), custom_call_target="tpu_custom_call" | custom-call | flops 1000000000 | bytes 8000000 | tf_op jit(solution)/shard_map/pallas_call | solution.py:480
  168.9 13.9 %all-to-all-done = bf16[64,16,2560]{2,1,0:T(8,128)(2,1)} async-done(((bf16[64,16,2560]{2,1,0:T(8,128)(2,1)}), bf16[64,16,2560]{2,1,0:T(8,128)(2,1)}, u32[]{:S(2)}, u32[]{:S(2)}) %all-to-all-start) | async-done | bytes 5242912 | tf_op jit(solution)/shard_map/all_to_all | solution.py:808
  182.8 9.3 %all-to-all-start.1 = ((bf16[64,16,2560]{2,1,0:T(8,128)(2,1)}), bf16[64,16,2560]{2,1,0:T(8,128)(2,1)}, u32[]{:S(2)}, u32[]{:S(2)}) async-start(bf16[64,16,2560]{2,1,0:T(8,128)(2,1)} %bitcast.83), calls=%async_computation.1 | async-start | bytes 10485760 | tf_op jit(solution)/shard_map/all_to_all | solution.py:808
  192.2 36.6 %collective-permute-done.1.up_o = bf16[2048,384]{1,0:T(8,128)(2,1)} collective-permute-done((bf16[2048,384]{1,0:T(8,128)(2,1)}, bf16[2048,384]{1,0:T(8,128)(2,1)}, u32[]{:S(2)}, u32[]{:S(2)}) %collective-permute-start.1) | collective-permute-done | bytes 1572896 | tf_op jit(solution)/shard_map/ppermute | solution.py:782
  228.8 26.0 %all-to-all-done.1 = bf16[64,16,2560]{2,1,0:T(8,128)(2,1)} async-done(((bf16[64,16,2560]{2,1,0:T(8,128)(2,1)}), bf16[64,16,2560]{2,1,0:T(8,128)(2,1)}, u32[]{:S(2)}, u32[]{:S(2)}) %all-to-all-start.1) | async-done | bytes 5242912 | tf_op jit(solution)/shard_map/all_to_all | solution.py:808
  254.8 39.3 %shard_map.267 = (bf16[1024,2560]{1,0:T(8,128)(2,1)}, bf16[1024,2560]{1,0:T(8,128)(2,1)}, bf16[1280,2048]{1,0:T(8,128)(2,1)}, bf16[1280,2048]{1,0:T(8,128)(2,1)}...) custom-call(bf16[1024,2560]{1,0:T(8,128)(2,1)} %bitcast.15.rows, ...), custom_call_target="tpu_custom_call" | custom-call | flops 24159191040 | bytes 45000000 | tf_op jit(solution)/shard_map/pallas_call | solution.py:573
  294.1 9.3 %all-to-all-start.2 = ((bf16[64,16,2560]{2,1,0:T(8,128)(2,1)}), bf16[64,16,2560]{2,1,0:T(8,128)(2,1)}, u32[]{:S(2)}, u32[]{:S(2)}) async-start(bf16[64,16,2560]{2,1,0:T(8,128)(2,1)} %bitcast.87), calls=%async_computation.2 | async-start | bytes 10485760 | tf_op jit(solution)/shard_map/all_to_all | solution.py:808
  304.8 6.5 %convolution_convert_fusion.4 = bf16[2048,384]{1,0:T(8,128)(2,1)S(1)} fusion(bf16[1280,2048]{1,0:T(8,128)(2,1)} %get-tuple-element.69, bf16[1280,768]{1,0:T(8,128)(2,1)} %get-tuple-element.70), kind=kOutput, calls=%fused_computation.9 | convolution fusion | flops 2014052352 | bytes 7798784 | tf_op jit(solution)/shard_map/dot_general | solution.py:600
  315.3 4.7 fusion.18
  320.0 4.0 fusion.20
  324.0 4.7 fusion.16
  328.7 4.0 convolution_convert_fusion.2.gate
  332.6 15.5 %collective-permute-done.2 = bf16[2048,384]{1,0:T(8,128)(2,1)} collective-permute-done((bf16[2048,384]{1,0:T(8,128)(2,1)S(1)}, bf16[2048,384]{1,0:T(8,128)(2,1)}, u32[]{:S(2)}, u32[]{:S(2)}) %collective-permute-start.2) | collective-permute-done | bytes 1572896 | tf_op jit(solution)/shard_map/ppermute | solution.py:782
  348.2 17.8 %all-to-all-done.2 = bf16[64,16,2560]{2,1,0:T(8,128)(2,1)} async-done(((bf16[64,16,2560]{2,1,0:T(8,128)(2,1)}), bf16[64,16,2560]{2,1,0:T(8,128)(2,1)}, u32[]{:S(2)}, u32[]{:S(2)}) %all-to-all-start.2) | async-done | bytes 5242912 | tf_op jit(solution)/shard_map/all_to_all | solution.py:808
  366.0 9.6 %all-to-all-start.3 = ((bf16[64,16,2560]{2,1,0:T(8,128)(2,1)}), bf16[64,16,2560]{2,1,0:T(8,128)(2,1)}, u32[]{:S(2)}, u32[]{:S(2)}) async-start(bf16[64,16,2560]{2,1,0:T(8,128)(2,1)} %bitcast.86), calls=%async_computation.3 | async-start | bytes 10485760 | tf_op jit(solution)/shard_map/all_to_all | solution.py:808
  383.3 3.7 add_bitcast_fusion.2
  387.0 9.5 %collective-permute-done.3 = bf16[128,2048]{1,0:T(8,128)(2,1)S(1)} collective-permute-done((bf16[128,2048]{1,0:T(8,128)(2,1)S(1)}, bf16[128,2048]{1,0:T(8,128)(2,1)S(1)}, u32[]{:S(2)}, u32[]{:S(2)}) %collective-permute-start.3) | collective-permute-done | bytes 524320 | tf_op jit(solution)/shard_map/ppermute | solution.py:782
  399.0 15.2 %shard_map.268 = (bf16[256,2560]{1,0:T(8,128)(2,1)S(1)}, f32[8,128]{1,0:T(8,128)S(1)}) custom-call(f32[256,2560]{1,0:T(8,128)} %copy-done, f32[256,128]{1,0:T(8,128)S(1)} %get-tuple-element.124.cosine, f32[256,128]{1,0:T(8,128)S(1)} %get-tuple-element.125.sine, f32[1,128]{1,0:T(1,128)S(1)} %bitcast.77, f32[1,128]{1,0:T(1,128)S(1)} %bitcast.79, ...), custom_call_target="tpu_custom_call" | custom-call | flops 1000000 | bytes 1000000 | tf_op jit(solution)/shard_map/pallas_call | solution.py:702
  414.8 5.6 fusion.35
  422.4 5.7 %convolution_convert_fusion.1 = bf16[2048,2048]{1,0:T(8,128)(2,1)} fusion(bf16[256,2048]{1,0:T(8,128)(2,1)S(1)} %copy-done.4, bf16[128,2048]{1,0:T(8,128)(2,1)S(1)} %get-tuple-element.101, bf16[128,2048]{1,0:T(8,128)(2,1)S(1)} %get-tuple-element.100), kind=kOutput, calls=%fused_computation.1 | convolution fusion | flops 2153775104 | bytes 10485760 | tf_op jit(solution)/shard_map/dot_general | solution.py:600
  428.1 5.7 %convolution_convert_fusion = bf16[2048,2560]{1,0:T(8,128)(2,1)} fusion(bf16[256,2048]{1,0:T(8,128)(2,1)S(1)} %bitcast.91, bf16[256,2560]{1,0:T(8,128)(2,1)S(1)} %get-tuple-element.75), kind=kOutput, calls=%fused_computation | convolution fusion | flops 2689597440 | bytes 12845056 | tf_op jit(solution)/shard_map/dot_general | solution.py:600
  433.8 4.5 all-to-all-done.3
  438.3 101.6 %shard_map.270 = (f32[32,2560]{1,0:T(8,128)}, f32[32,2048]{1,0:T(8,128)}, f32[8,2048]{1,0:T(8,128)}, bf16[128,2048]{1,0:T(8,128)(2,1)}, bf16[384,2048]{1,0:T(8,128)(2,1)}, /*index=5*/bf16[2048,384]{1,0:T(8,128)(2,1)}) custom-call(bf16[4,2,4,2,32,2560]{5,4,3,2,1,0:T(8,128)(2,1)} %bitcast.80, bf16[4,2,4,2,32,2048]{5,4,3,2,1,0:T(8,128)(2,1)} %bitcast.81, ...), custom_call_target="tpu_custom_call" | custom-call | flops 10000000 | bytes 300000000 | tf_op jit(solution)/shard_map/pallas_call | solution.py:265
  545.6 8.8 %shard_map.269 = (bf16[128,2048]{1,0:T(8,128)(2,1)}, f32[64,128]{1,0:T(8,128)}) custom-call(bf16[1024,2560]{1,0:T(8,128)(2,1)} %bitcast.23.returned, bf16[1024,128]{1,0:T(8,128)(2,1)} %get-tuple-element.113.place, bf16[1024,512]{1,0:T(8,128)(2,1)} %get-tuple-element.105.part, f32[1024,1]{1,0:T(8,128)} %reshape.207.refs_0_.place_weight, ...), custom_call_target="tpu_custom_call" | custom-call | flops 3000000000 | bytes 10000000 | tf_op jit(solution)/shard_map/pallas_call | solution.py:758
  556.3 4.3 add_bitcast_fusion
  (131 shorter events, 45.7 us)
Async XLA Ops:
  0.6 8.9 %copy-start.8 = (bf16[128,2048]{1,0:T(8,128)(2,1)S(1)}, bf16[128,2048]{1,0:T(8,128)(2,1)}, u32[]{:S(2)}) copy-start(bf16[128,2048]{1,0:T(8,128)(2,1)} %param.16) | copy-start | bytes 1572868
  0.7 8.9 %copy-start.23 = (f32[2048]{0:T(1024)S(1)}, f32[2048]{0:T(1024)}, u32[]{:S(2)}) copy-start(f32[2048]{0:T(1024)} %param.18) | copy-start | bytes 24580
  4.3 6.6 %copy-start.22 = (bf16[32,2048]{1,0:T(8,128)(2,1)S(1)}, bf16[32,2048]{1,0:T(8,128)(2,1)}, u32[]{:S(2)}) copy-start(bf16[32,2048]{1,0:T(8,128)(2,1)} %param.19) | copy-start | bytes 393220
  4.4 6.6 %copy-start.26 = (bf16[32,256]{1,0:T(8,128)(2,1)S(1)}, bf16[32,256]{1,0:T(8,128)(2,1)}, u32[]{:S(2)}) copy-start(bf16[32,256]{1,0:T(8,128)(2,1)} %param.21) | copy-start | bytes 49156
  4.4 6.6 %copy-start.27 = (bf16[32,256]{1,0:T(8,128)(2,1)S(1)}, bf16[32,256]{1,0:T(8,128)(2,1)}, u32[]{:S(2)}) copy-start(bf16[32,256]{1,0:T(8,128)(2,1)} %param.20) | copy-start | bytes 49156
  112.7 7.5 %copy-start.28 = (s32[256]{0:T(256)S(1)}, s32[256]{0:T(256)}, u32[]{:S(2)}) copy-start(s32[256]{0:T(256)} %param.17) | copy-start | bytes 3076
  112.7 8.2 %copy-start.14 = (bf16[2,128,2048]{2,1,0:T(8,128)(2,1)S(1)}, bf16[2,128,2048]{2,1,0:T(8,128)(2,1)}, u32[]{:S(2)}) copy-start(bf16[2,128,2048]{2,1,0:T(8,128)(2,1)} %get-tuple-element.53) | copy-start | bytes 3145732
  112.8 70.1 %all-to-all-start = ((bf16[64,16,2560]{2,1,0:T(8,128)(2,1)}), bf16[64,16,2560]{2,1,0:T(8,128)(2,1)}, u32[]{:S(2)}, u32[]{:S(2)}) async-start(bf16[64,16,2560]{2,1,0:T(8,128)(2,1)} %bitcast.82), calls=%async_computation | async-start | bytes 10485760 | tf_op jit(solution)/shard_map/all_to_all | solution.py:808
  120.9 5.8 %copy-start.5 = (f32[128]{0:T(128)S(1)}, f32[128]{0:T(128)}, u32[]{:S(2)}) copy-start(f32[128]{0:T(128)} %param.22) | copy-start | bytes 1540
  120.9 5.8 %copy-start.6 = (f32[128]{0:T(128)S(1)}, f32[128]{0:T(128)}, u32[]{:S(2)}) copy-start(f32[128]{0:T(128)} %param.23) | copy-start | bytes 1540
  126.7 18.4 %copy-start = (f32[256,2560]{1,0:T(8,128)}, f32[256,2560]{1,0:T(8,128)S(1)}, u32[]{:S(2)}) copy-start(f32[256,2560]{1,0:T(8,128)S(1)} %fusion.33.raw) | copy-start | bytes 7864324
  138.6 6.5 %copy-start.1 = (bf16[256,2048]{1,0:T(8,128)(2,1)}, bf16[256,2048]{1,0:T(8,128)(2,1)S(1)}, u32[]{:S(2)}) copy-start(bf16[256,2048]{1,0:T(8,128)(2,1)S(1)} %get-tuple-element.56.query) | copy-start | bytes 3145732
  138.6 6.5 %copy-start.3 = (bf16[256,2048]{1,0:T(8,128)(2,1)}, bf16[256,2048]{1,0:T(8,128)(2,1)S(1)}, u32[]{:S(2)}) copy-start(bf16[256,2048]{1,0:T(8,128)(2,1)S(1)} %get-tuple-element.59) | copy-start | bytes 3145732
  145.1 16.9 %copy-start.24 = (f32[2048]{0:T(1024)S(1)}, f32[2048]{0:T(1024)}, u32[]{:S(2)}) copy-start(f32[2048]{0:T(1024)} %param.25) | copy-start | bytes 24580
  146.4 13.9 %collective-permute-start = (bf16[128,2048]{1,0:T(8,128)(2,1)S(1)}, bf16[128,2048]{1,0:T(8,128)(2,1)}, u32[]{:S(2)}, u32[]{:S(2)}) collective-permute-start(bf16[128,2048]{1,0:T(8,128)(2,1)S(1)} %dynamic-slice_convert_fusion.1), channel_id=1, source_target_pairs={{0,1},{1,0},{2,3},{3,2},{4,5},{5,4},{6,7},{7,6},{8,9},{9,8},{10,11... | collective-permute-start | bytes 1572872 | tf_op jit(solution)/shard_map/ppermute | solution.py:782
  162.0 219.0 %copy-start.7 = (f32[128,2048]{1,0:T(8,128)}, f32[128,2048]{1,0:T(8,128)S(1)}, u32[]{:S(2)}) copy-start(f32[128,2048]{1,0:T(8,128)S(1)} %get-tuple-element.99.base) | copy-start | bytes 3145732
  182.8 71.9 %all-to-all-start.1 = ((bf16[64,16,2560]{2,1,0:T(8,128)(2,1)}), bf16[64,16,2560]{2,1,0:T(8,128)(2,1)}, u32[]{:S(2)}, u32[]{:S(2)}) async-start(bf16[64,16,2560]{2,1,0:T(8,128)(2,1)} %bitcast.83), calls=%async_computation.1 | async-start | bytes 10485760 | tf_op jit(solution)/shard_map/all_to_all | solution.py:808
  192.1 36.7 %collective-permute-start.1 = (bf16[2048,384]{1,0:T(8,128)(2,1)}, bf16[2048,384]{1,0:T(8,128)(2,1)}, u32[]{:S(2)}, u32[]{:S(2)}) collective-permute-start(bf16[2048,384]{1,0:T(8,128)(2,1)} %bitcast.111), channel_id=1, source_target_pairs={{0,1},{1,0},{2,3},{3,2},{4,5},{5,4},{6,7},{7,6},{8,9},{9,8},{10,11... | collective-permute-start | bytes 4718600 | tf_op jit(solution)/shard_map/ppermute | solution.py:782
  294.1 72.0 %all-to-all-start.2 = ((bf16[64,16,2560]{2,1,0:T(8,128)(2,1)}), bf16[64,16,2560]{2,1,0:T(8,128)(2,1)}, u32[]{:S(2)}, u32[]{:S(2)}) async-start(bf16[64,16,2560]{2,1,0:T(8,128)(2,1)} %bitcast.87), calls=%async_computation.2 | async-start | bytes 10485760 | tf_op jit(solution)/shard_map/all_to_all | solution.py:808
  303.4 8.4 %slice-start = ((s8[5242880]{0:T(1024)(128)(4,1)}), s8[4194304]{0:T(1024)(128)(4,1)S(1)}, s32[]{:S(2)}) async-start(s8[5242880]{0:T(1024)(128)(4,1)} %bitcast.84), calls=%async_computation.4 | async-start | bytes 8388608
  303.4 11.9 %slice-start.4 = ((s8[5242880]{0:T(1024)(128)(4,1)}), s8[4194304]{0:T(1024)(128)(4,1)S(1)}, s32[]{:S(2)}) async-start(s8[5242880]{0:T(1024)(128)(4,1)} %bitcast.113), calls=%async_computation.8 | async-start | bytes 8388608
  304.8 7.0 %slice-start.1 = ((s8[5242880]{0:T(1024)(128)(4,1)}), s8[1048576]{0:T(1024)(128)(4,1)S(1)}, s32[]{:S(2)}) async-start(s8[5242880]{0:T(1024)(128)(4,1)} %bitcast.84), calls=%async_computation.5 | async-start | bytes 2097152
  304.8 7.0 %copy-start.16 = (bf16[1280,768]{1,0:T(8,128)(2,1)S(1)}, bf16[1280,768]{1,0:T(8,128)(2,1)}, u32[]{:S(2)}) copy-start(bf16[1280,768]{1,0:T(8,128)(2,1)} %get-tuple-element.71) | copy-start | bytes 5898244
  304.8 10.5 %slice-start.5 = ((s8[5242880]{0:T(1024)(128)(4,1)}), s8[1048576]{0:T(1024)(128)(4,1)S(1)}, s32[]{:S(2)}) async-start(s8[5242880]{0:T(1024)(128)(4,1)} %bitcast.113), calls=%async_computation.9 | async-start | bytes 2097152
  311.3 36.9 %collective-permute-start.2 = (bf16[2048,384]{1,0:T(8,128)(2,1)S(1)}, bf16[2048,384]{1,0:T(8,128)(2,1)}, u32[]{:S(2)}, u32[]{:S(2)}) collective-permute-start(bf16[2048,384]{1,0:T(8,128)(2,1)S(1)} %convolution_convert_fusion.4), channel_id=1, source_target_pairs={{0,1},{1,0},{2,3},{3,2},{4,5},{5,4},{6,7},{7,6},{8,9},{9,8},{10,11... | collective-permute-start | bytes 4718600 | tf_op jit(solution)/shard_map/ppermute | solution.py:782
  366.0 9.6 %copy-start.20 = (pred[512,1024]{1,0:T(32,128)(4,1)S(1)}, pred[512,1024]{1,0:T(32,128)(4,1)}, u32[]{:S(2)}) copy-start(pred[512,1024]{1,0:T(32,128)(4,1)} %copy.50) | copy-start | bytes 1572868
  366.0 72.2 %all-to-all-start.3 = ((bf16[64,16,2560]{2,1,0:T(8,128)(2,1)}), bf16[64,16,2560]{2,1,0:T(8,128)(2,1)}, u32[]{:S(2)}, u32[]{:S(2)}) async-start(bf16[64,16,2560]{2,1,0:T(8,128)(2,1)} %bitcast.86), calls=%async_computation.3 | async-start | bytes 10485760 | tf_op jit(solution)/shard_map/all_to_all | solution.py:808
  377.7 18.9 %slice-start.2 = ((s8[8388608]{0:T(1024)(128)(4,1)}), s8[4194304]{0:T(1024)(128)(4,1)S(1)}, s32[]{:S(2)}) async-start(s8[8388608]{0:T(1024)(128)(4,1)} %bitcast.108), calls=%async_computation.6 | async-start | bytes 8388608
  381.1 15.5 %slice-start.3 = ((s8[8388608]{0:T(1024)(128)(4,1)}), s8[4194304]{0:T(1024)(128)(4,1)S(1)}, s32[]{:S(2)}) async-start(s8[8388608]{0:T(1024)(128)(4,1)} %bitcast.108), calls=%async_computation.7 | async-start | bytes 8388608
  382.5 14.0 %collective-permute-start.3 = (bf16[128,2048]{1,0:T(8,128)(2,1)S(1)}, bf16[128,2048]{1,0:T(8,128)(2,1)S(1)}, u32[]{:S(2)}, u32[]{:S(2)}) collective-permute-start(bf16[128,2048]{1,0:T(8,128)(2,1)S(1)} %get-tuple-element.96), channel_id=1, source_target_pairs={{0,1},{1,0},{2,3},{3,2},{4,5},{5,4},{6,7},{7,6},{8,9},{9,8},{10,11... | collective-permute-start | bytes 1572872 | tf_op jit(solution)/shard_map/ppermute | solution.py:782
  545.6 8.8 %copy-start.25 = (s32[128,8]{0,1:T(8,128)S(1)}, s32[128,8]{0,1:T(8,128)}, u32[]{:S(2)}) copy-start(s32[128,8]{0,1:T(8,128)} %param.26) | copy-start | bytes 12292
  545.6 10.3 %copy-start.13 = (bf16[128,2048]{1,0:T(8,128)(2,1)S(1)}, bf16[128,2048]{1,0:T(8,128)(2,1)}, u32[]{:S(2)}) copy-start(bf16[128,2048]{1,0:T(8,128)(2,1)} %get-tuple-element.81) | copy-start | bytes 1572868
  (13 other events, 38.4 us)

commit v5 on v4

--- a/solution.py
+++ b/solution.py
@@ -55,14 +55,35 @@
 STEPS = (1, 3, 2)
 
 
+def combine_rows(weights, values):
+    high = weights.astype(BF16)
+    low = (weights - high.astype(F32)).astype(BF16)
+    return dot(high, values, ((0,), (0,))) + dot(low, values, ((0,), (0,)))
+
+
+def output_rows(at, returned, place, part, place_weight, part_weight, grad, total):
+    tokens, width = grad.shape
+    step = width // CHUNKS
+    main, rest, picked = returned[at, :width], returned[at, width:], place[at].astype(F32)
+    total[...] += combine_rows(picked * place_weight[at], main)
+    products = dot(main, grad[...], ((1,), (1,))) * picked
+    for j in range(CHUNKS):
+        picked = part[at, j * tokens : (j + 1) * tokens].astype(F32)
+        columns = slice(j * step, (j + 1) * step)
+        total[:, columns] += combine_rows(picked * part_weight[at], rest)
+        products += dot(rest, grad[:, columns], ((1,), (1,))) * picked
+    return jnp.sum(products.reshape(-1, ROWS_FULL, tokens), axis=1)
+
+
 def reduce_kernel(
-    ga, gb, gain, d_own, d_sent, x_hat, down, gate,
-    oa, ob, og, d_came, down_c, gate_c,
+    ga, gb, gain, d_own, d_sent, x_hat,
+    returned, place, part, place_weight, part_weight, grad, base, down, gate,
+    oa, ob, og, d_came, output, of_expert, down_c, gate_c,
     own_a, got_a, one_a, via_a, two_a, sum_a, three_a,
     own_b, got_b, one_b, via_b, two_b, sum_b, three_b,
     vec, vecs,
     load_sem, core_send, core_recv, one_send, one_recv, two_send, two_recv,
-    three_send, three_recv, vec_send, vec_recv, pair_send, pair_recv,
+    three_send, three_recv, vec_send, vec_recv, pair_send, pair_recv, total,
 ):
     z, x, y, core = coordinates()
     tensor = lax.axis_index("tensor")
@@ -102,13 +123,13 @@
         for copy in vec_copies[stage]:
             copy.wait()
         count = vec_groups[stage][2]
-        total = vecs[stage, 0]
+        added = vecs[stage, 0]
         for i in range(1, count):
-            total = total + vecs[stage, i]
+            added = added + vecs[stage, i]
         if stage == 3:
-            og[...] = total
+            og[...] = added
         else:
-            vec[stage + 1] = total
+            vec[stage + 1] = added
 
     partner = near[1]
     d_copy = send(d_sent, d_came, pair_send.at[0], pair_recv.at[0], partner)
@@ -132,7 +153,7 @@
         def _(i):
             @pl.loop(0, shape[2])
             def _(j):
-                own[to, i, j] = (own[to, i, j].astype(F32) + got[to, i, j].astype(F32)).astype(BF16)
+                own[to, i, j] += got[to, i, j]
 
     def round_ring(own, got, via, one, at, up, down, name, row):
         n = own.shape[1] // 2
@@ -154,9 +175,7 @@
             def _(i):
                 @pl.loop(0, own.shape[2])
                 def _(j):
-                    own[to, first + i, j] = (
-                        own[to, first + i, j].astype(F32) + via[k, i, j].astype(F32)
-                    ).astype(BF16)
+                    own[to, first + i, j] += via[k, i, j]
 
         ready(2)
         copies = [step(own.at[far, halves[0]], via.at[0], 0, up), step(own.at[far, halves[1]], via.at[1], 1, down)]
@@ -183,15 +202,25 @@
         round_ring(own_b, got_b, via_b, one_b, y, along_y[0], along_y[1], "b", 1),
     ]
     firsts = [next(r) for r in rings]
-    d_copy.wait_recv()
-    vec_start(0)
-    expert = [
-        send(down, down_c, pair_send.at[1], pair_recv.at[1], partner),
-        send(gate, gate_c, pair_send.at[2], pair_recv.at[2], partner),
-    ]
-    for _ in range(5):
+    expert = [send(down, down_c, pair_send.at[1], pair_recv.at[1], partner)]
+    for i in range(5):
         for r in rings:
             next(r)
+        if i == 1:
+            d_copy.wait_recv()
+            vec_start(0)
+            expert.append(send(gate, gate_c, pair_send.at[2], pair_recv.at[2], partner))
+            total[...] = base[...]
+
+            @pl.loop(0, returned.shape[0] // 256)
+            def _(i):
+                rows = pl.ds(pl.multiple_of(i * 256, 256), 256)
+                experts = pl.ds(pl.multiple_of(i * 16, 16), 16)
+                of_expert[experts] = output_rows(
+                    rows, returned, place, part, place_weight, part_weight, grad, total
+                )
+
+            output[...] = total[...].astype(BF16)
     ones = firsts[0] + firsts[1]
     vec_finish(0)
     vec_start(1)
@@ -244,7 +273,7 @@
         copy.wait_send()
 
 
-def reduce_grads(in_grads, out_grads, gains, d_own, d_sent, x_hat, expert):
+def reduce_grads(in_grads, out_grads, gains, d_own, d_sent, x_hat, routed, expert):
     owners = lax.axis_size("dp")
     rows = in_grads.shape[0] // owners
     a_cols, b_cols = in_grads.shape[1], out_grads.shape[1]
@@ -269,10 +298,12 @@
             jax.ShapeDtypeStruct((rows, b_cols), F32),
             jax.ShapeDtypeStruct(gains.shape, F32),
             jax.ShapeDtypeStruct(d_sent.shape, BF16),
+            jax.ShapeDtypeStruct(d_sent.shape, BF16),
+            jax.ShapeDtypeStruct((owners, d_sent.shape[0]), F32),
             *[jax.ShapeDtypeStruct(half.shape, BF16) for half in expert],
         ),
-        in_specs=[ANY_SPEC] * 2 + [VMEM_SPEC] * 4 + [ANY_SPEC] * 2,
-        out_specs=[VMEM_SPEC] * 4 + [ANY_SPEC] * 2,
+        in_specs=[ANY_SPEC] * 2 + [VMEM_SPEC] * 11 + [ANY_SPEC] * 2,
+        out_specs=[VMEM_SPEC] * 6 + [ANY_SPEC] * 2,
         scratch_shapes=scratch(a_cols, (2, 4))
         + scratch(b_cols, (4, 2))
         + [
@@ -291,6 +322,7 @@
             dma((4, 3)),
             dma((3,)),
             dma((3,)),
+            vmem(d_sent.shape, F32),
         ],
         compiler_params=pltpu.CompilerParams(
             collective_id=1, has_side_effects=True, vmem_limit_bytes=56 * 1024 * 1024
@@ -303,6 +335,7 @@
         d_own,
         d_sent,
         x_hat,
+        *routed,
         *expert,
     )
 
@@ -328,18 +361,12 @@
     copies[3].wait_recv()
     arrived(turn(at, 2))
     yield
-
-
-def together(*rings):
-    copies = [next(r) for r in rings]
-    for _ in range(3):
-        for r in rings:
-            next(r)
-    return [c for group in copies for c in group]
+    yield copies
 
 
 def gather_kernel(
-    sa, sb, part, down, gate, fa, fb, whole, down_o, gate_o,
+    sa, sb, part, values, place, pieces, place_weight, piece_weight, down,
+    fa, fb, whole, packed, down_o,
     keep_sem, x_send, x_recv, one_send, one_recv, two_send, two_recv, core_send, core_recv, pair_send, pair_recv,
 ):
     z, x, y, core = coordinates()
@@ -351,16 +378,13 @@
     around_y = device(z, x, turn(y, 1), core, tensor), device(z, x, turn(y, 3), core, tensor)
     greet([sibling, across, partner, *around_z, *around_y])
 
-    pair = send(part, whole.at[tensor], pair_send.at[0], pair_recv.at[0], partner)
     a_own, b_own = fa.at[z, x, y, core], fb.at[z, x, y, core]
     over = [
         send(sa, a_own, x_send.at[0], x_recv.at[0], across),
         send(sb, b_own, x_send.at[1], x_recv.at[1], across),
     ]
-    expert = [
-        send(src, dst, pair_send.at[i], pair_recv.at[i], partner)
-        for i, (src, dst) in enumerate(((down, down_o), (gate, gate_o)), 1)
-    ]
+    pair = send(part, whole.at[tensor], pair_send.at[0], pair_recv.at[0], partner)
+    expert = [send(down, down_o, pair_send.at[1], pair_recv.at[1], partner)]
     keep = [
         pltpu.make_async_copy(part, whole.at[tensor], keep_sem.at[0]),
         pltpu.make_async_copy(sa, a_own, keep_sem.at[1]),
@@ -373,13 +397,6 @@
     over[0].wait_recv()
     over[1].wait_recv()
 
-    def skip(place):
-        return None
-
-    small = together(
-        ring(lambda i, h: fa.at[z, h, i, core], y, *around_y, one_send.at[0], one_recv.at[0], skip),
-        ring(lambda i, h: fb.at[i, h, y, core], z, *around_z, one_send.at[1], one_recv.at[1], skip),
-    )
     cores = []
 
     def hand_on(view):
@@ -389,64 +406,102 @@
 
         return arrived
 
-    def view_a(i, h):
-        return fa.at[i, h, :, core]
-
-    def view_b(i, h):
-        return fb.at[:, h, i, core]
-
-    large = [
-        ring(view_a, z, *around_z, two_send.at[0], two_recv.at[0], hand_on(view_a)),
-        ring(view_b, y, *around_y, two_send.at[1], two_recv.at[1], hand_on(view_b)),
+    large = []
+
+    def spread(kind, place):
+        if kind == 0:
+            view, at, around = (lambda i, h: fa.at[i, h, place, core]), z, around_z
+        else:
+            view, at, around = (lambda i, h: fb.at[place, h, i, core]), y, around_y
+        k = len(large) // 2
+        arrived = hand_on(view)
+        steps = ring(view, at, *around, two_send.at[kind, k], two_recv.at[kind, k], arrived)
+        large.append(steps)
+        next(steps)
+        arrived(at)
+
+    small = [
+        ring(
+            lambda i, h: fa.at[z, h, i, core], y, *around_y, one_send.at[0], one_recv.at[0],
+            lambda place: spread(0, place),
+        ),
+        ring(
+            lambda i, h: fb.at[i, h, y, core], z, *around_z, one_send.at[1], one_recv.at[1],
+            lambda place: spread(1, place),
+        ),
     ]
-    copies = [next(r) for r in large]
-    hand_on(view_a)(z)
-    hand_on(view_b)(y)
+    firsts = [next(r) for r in small]
+    spread(0, y)
+    spread(1, z)
+
+    width = values.shape[1]
+
+    @pl.loop(0, packed.shape[0] // 256)
+    def _(i):
+        at = pl.ds(pl.multiple_of(i * 256, 256), 256)
+        main, rest = pack_rows(values, place[at], pieces[at])
+        packed[at, :width] = (main * place_weight[at]).astype(BF16)
+        packed[at, width:] = (rest * piece_weight[at]).astype(BF16)
+
     for _ in range(3):
-        for r in large:
+        for r in small:
             next(r)
+    for i in range(0, len(large), 2):
+        for _ in range(3):
+            next(large[i])
+            next(large[i + 1])
     keep[0].wait()
     pair.wait_recv()
     for copy in cores + expert:
         copy.wait_recv()
-    for copy in expert + [pair] + over + small + copies[0] + copies[1] + cores:
+    for copy in expert + [pair] + over + cores:
         copy.wait_send()
-
-
-def gather_weights(in_shard, out_shard, part, expert):
+    for r in large:
+        for copy in next(r):
+            copy.wait_send()
+    for group in firsts:
+        for copy in group:
+            copy.wait_send()
+
+
+def gather_weights(in_shard, out_shard, part, to_pack, expert):
     owners = lax.axis_size("dp")
     (rows, a_cols), b_cols = in_shard.shape, out_shard.shape[1]
     dma = pltpu.SemaphoreType.DMA
-    in_full, out_full, whole, *other = pl.pallas_call(
+    in_full, out_full, whole, packed, *other = pl.pallas_call(
         gather_kernel,
         out_shape=(
             jax.ShapeDtypeStruct((4, 2, 4, 2, rows, a_cols), BF16),
             jax.ShapeDtypeStruct((4, 2, 4, 2, rows, b_cols), BF16),
             jax.ShapeDtypeStruct((2,) + part.shape, BF16),
+            jax.ShapeDtypeStruct((to_pack[1].shape[0], part.shape[1] * 5 // 4), BF16),
             *[jax.ShapeDtypeStruct(w.shape, BF16) for w in expert],
         ),
-        in_specs=[ANY_SPEC] * 5,
-        out_specs=[ANY_SPEC] * 5,
+        in_specs=[VMEM_SPEC] * 8 + [ANY_SPEC],
+        out_specs=[ANY_SPEC] * 3 + [VMEM_SPEC, ANY_SPEC],
         scratch_shapes=[
             dma((3,)),
             dma((2,)),
             dma((2,)),
             dma((2, 4)),
             dma((2, 4)),
-            dma((2, 4)),
-            dma((2, 4)),
-            dma((8,)),
-            dma((8,)),
+            dma((2, 4, 4)),
+            dma((2, 4, 4)),
+            dma((32,)),
+            dma((32,)),
             dma((4,)),
             dma((4,)),
         ],
-        compiler_params=pltpu.CompilerParams(collective_id=2, has_side_effects=True),
+        compiler_params=pltpu.CompilerParams(
+            collective_id=2, has_side_effects=True, vmem_limit_bytes=40 * 1024 * 1024
+        ),
         cost_estimate=pl.CostEstimate(flops=0, bytes_accessed=250_000_000, transcendentals=0),
-    )(in_shard, out_shard, part, *expert)
+    )(in_shard, out_shard, part, *to_pack, *expert)
     return (
         in_full.reshape(owners * rows, a_cols),
         out_full.reshape(owners * rows, b_cols),
         whole.reshape(-1, part.shape[1]),
+        packed,
         other,
     )
 
@@ -454,12 +509,10 @@
 ROWS_FULL, ROWS_PART, CHUNKS = 16, 4, 4
 
 
-def pack_kernel(weighted, values, place, part, *refs):
-    out = refs[-1]
-    width = values.shape[1]
+def pack_rows(values, place, part):
+    tokens, width = values.shape
     step = width // CHUNKS
-    tokens = values.shape[0]
-    main = jnp.dot(place[...], values[...], preferred_element_type=F32)
+    main = jnp.dot(place, values[...], preferred_element_type=F32)
     rest = jnp.zeros((place.shape[0], step), F32)
     for j in range(CHUNKS):
         rest += jnp.dot(
@@ -467,29 +520,32 @@
             values[:, j * step : (j + 1) * step],
             preferred_element_type=F32,
         )
-    if weighted:
-        main, rest = main * refs[0][...], rest * refs[1][...]
+    return main, rest
+
+
+def pack_kernel(values, place, part, out):
+    width = values.shape[1]
+    main, rest = pack_rows(values, place[...], part[...])
     out[:, :width] = main.astype(BF16)
     out[:, width:] = rest.astype(BF16)
 
 
-def pack(values, place, part, weights=()):
+def pack(values, place, part):
     total, tokens = place.shape
     width = values.shape[1]
     block = total // 4
     return pl.pallas_call(
-        functools.partial(pack_kernel, bool(weights)),
+        pack_kernel,
         grid=(4,),
         out_shape=jax.ShapeDtypeStruct((total, width + width // CHUNKS), BF16),
         in_specs=[
             pl.BlockSpec((tokens, width), lambda g: (0, 0)),
             pl.BlockSpec((block, tokens), lambda g: (g, 0)),
             pl.BlockSpec((block, CHUNKS * tokens), lambda g: (g, 0)),
-        ]
-        + [pl.BlockSpec((block, 1), lambda g: (g, 0))] * len(weights),
+        ],
         out_specs=pl.BlockSpec((block, width + width // CHUNKS), lambda g: (g, 0)),
         cost_estimate=pl.CostEstimate(flops=1_000_000_000, bytes_accessed=8_000_000, transcendentals=0),
-    )(values, place, part, *weights)
+    )(values, place, part)
 
 
 def expert_kernel(
@@ -713,63 +769,6 @@
     )(raw, cosine, sine, query_gain[None], key_gain[None], query, key, value, d_mixed)
 
 
-def output_kernel(returned, place, part, place_weight, part_weight, grad, base, out, of_expert, total):
-    step = pl.program_id(0)
-    width = grad.shape[1]
-    tokens = grad.shape[0]
-    cut = width // CHUNKS
-
-    @pl.when(step == 0)
-    def _():
-        total[...] = base[...]
-
-    def combine(weights, values):
-        high = weights.astype(BF16)
-        low = (weights - high.astype(F32)).astype(BF16)
-        return dot(high, values, ((0,), (0,))) + dot(low, values, ((0,), (0,)))
-
-    main, rest = returned[:, :width], returned[:, width:]
-    total[...] += combine(place[...].astype(F32) * place_weight[...], main)
-    products = dot(main, grad[...], ((1,), (1,))) * place[...].astype(F32)
-    for j in range(CHUNKS):
-        chosen = part[:, j * tokens : (j + 1) * tokens].astype(F32)
-        at = slice(j * cut, (j + 1) * cut)
-        total[:, at] += combine(chosen * part_weight[...], rest)
-        products += dot(rest, grad[:, at], ((1,), (1,))) * chosen
-    of_expert[...] = jnp.sum(products.reshape(-1, ROWS_FULL, tokens), axis=1)
-
-    @pl.when(step == pl.num_programs(0) - 1)
-    def _():
-        out[...] = total[...].astype(BF16)
-
-
-def finish_output(returned, place, part, place_weight, part_weight, grad, base):
-    total, packed = returned.shape
-    tokens, width = grad.shape
-    groups = 4
-    block = total // groups
-
-    def cut(rows, cols):
-        return pl.BlockSpec((rows, cols), lambda g: (g, 0))
-
-    def fixed(cols):
-        return pl.BlockSpec((tokens, cols), lambda g: (0, 0))
-
-    return pl.pallas_call(
-        output_kernel,
-        grid=(groups,),
-        out_shape=(
-            jax.ShapeDtypeStruct((tokens, width), BF16),
-            jax.ShapeDtypeStruct((total // ROWS_FULL, tokens), F32),
-        ),
-        in_specs=[cut(block, packed), cut(block, tokens), cut(block, CHUNKS * tokens), cut(block, 1), cut(block, 1)]
-        + [fixed(width), fixed(width)],
-        out_specs=[fixed(width), cut(block // ROWS_FULL, tokens)],
-        scratch_shapes=[pltpu.VMEM((tokens, width), F32)],
-        cost_estimate=pl.CostEstimate(flops=3_000_000_000, bytes_accessed=10_000_000, transcendentals=0),
-    )(returned, place, part, place_weight, part_weight, grad, base)
-
-
 def rope_tables(positions, head_size):
     half = head_size // 2
     freqs = jnp.exp(jnp.arange(half, dtype=F32) * (-2.0 * math.log(THETA) / head_size))
@@ -837,12 +836,6 @@
     in_scale = rms_scale(inputs)
     normed = (inputs * in_scale * norm_in).astype(BF16)
     gate_w, up_w, down_w = gate_weight[0], up_weight[0], down_weight[0]
-    in_full, out_full, whole, (down_o, gate_o) = gather_weights(
-        jnp.concatenate([query_weight, key_weight, value_weight], axis=1),
-        out_weight.T,
-        normed,
-        (down_w, gate_w),
-    )
     q_cols, k_cols = query_weight.shape[1], key_weight.shape[1]
     query_heads, key_heads = q_cols // HD, k_cols // HD
 
@@ -875,8 +868,15 @@
         return first + rest.reshape(CHUNKS, rows, -1).transpose(1, 0, 2).reshape(rows, width)
 
     grad = out_grad.astype(F32)
-    d_rows = pack(out_grad, place, part, (place_weight, part_weight))
-    d_rows, whole = lax.optimization_barrier((d_rows, whole))
+    in_full, out_full, whole, d_rows, (down_o,) = gather_weights(
+        jnp.concatenate([query_weight, key_weight, value_weight], axis=1),
+        out_weight.T,
+        normed,
+        (out_grad, place, part, place_weight, part_weight),
+        (down_w,),
+    )
+    d_rows, whole, gate_s = lax.optimization_barrier((d_rows, whole, gate_w))
+    gate_o = swap(gate_s)
     expert_grads = to_experts(d_rows)
 
     cosine, sine = rope_tables(positions, HD)
@@ -884,7 +884,8 @@
     query, key, value, mixed = attend(
         raw, cosine, sine, query_gain, key_gain, query_heads, key_heads
     )
-    attended = sum_sequence(dot(mixed, out_full, ((1,), (1,))), rows)
+    attended, gate_o = lax.optimization_barrier((dot(mixed, out_full, ((1,), (1,))), gate_o))
+    attended = sum_sequence(attended, rows)
     hidden_in = inputs + attended
     mid_scale = rms_scale(hidden_in)
     normed_mid = (hidden_in * mid_scale * norm_mid).astype(BF16)
@@ -897,13 +898,16 @@
     )
     back_rows = to_experts(d_row)
     units = down_w.shape[0]
-    halves, others = [
-        ((hidden[:, of], grads_in), (rows_in, d_gate[:, of]), (rows_in, d_up[:, of]))
-        for of in (slice(0, units), slice(units, 2 * units))
+    others = ((hidden[:, units:], grads_in), (rows_in, d_gate[:, units:]), (rows_in, d_up[:, units:]))
+    sent = [dot(left, right, ((0,), (0,))).astype(BF16) for left, right in others]
+    gate_came = swap(sent[1])
+    *sent, rows_k, grads_k = lax.optimization_barrier((*sent, rows_in, grads_in))
+    kept = [
+        dot(left, right, ((0,), (0,)))
+        for left, right in (
+            (hidden[:, :units], grads_k), (rows_k, d_gate[:, :units]), (rows_k, d_up[:, :units])
+        )
     ]
-    sent = [dot(left, right, ((0,), (0,))).astype(BF16) for left, right in others]
-    kept = [dot(left, right, ((0,), (0,))) for left, right in halves]
-    gate_came = swap(sent[1])
 
     back_rows, result, gate_came, *kept = lax.optimization_barrier((back_rows, result, gate_came, *kept))
     d_mid = to_tokens(back_rows, place, part)
@@ -924,14 +928,12 @@
     gain_row = jnp.pad(gain_sums[:2].reshape(1, -1), ((0, 0), (0, width - 2 * HD)))
     gains = jnp.pad(jnp.concatenate([grad_norm_mid[None], gain_row]), ((1, 5), (0, 0)))
     in_grads, returned = lax.optimization_barrier((in_grads, returned))
-    in_total, out_total, gains, d_came, down_came, up_came = reduce_grads(
-        in_grads, out_grads, gains, d_own, d_sent.astype(BF16), inputs * in_scale, (sent[0], sent[2])
-    )
-    output, of_expert = finish_output(
-        returned, place, part, place_weight, part_weight, out_grad, hidden_in
-    )
-    of_expert = of_expert.T
-    grad_route = jnp.sum(jnp.where(names, of_expert[:, None, :], 0.0), axis=2)
+    in_total, out_total, gains, d_came, output, of_expert, down_came, up_came = reduce_grads(
+        in_grads, out_grads, gains, d_own, d_sent.astype(BF16), inputs * in_scale,
+        (returned, place, part, place_weight, part_weight, out_grad, hidden_in),
+        (sent[0], sent[2]),
+    )
+    grad_route = jnp.sum(jnp.where(names, of_expert.T[:, None, :], 0.0), axis=2)
     d_normed = d_own + d_came.astype(F32)
     d_inputs, _ = norm_back(inputs, in_scale, norm_in, d_normed)
     grad_tokens = (d_hidden_in + d_inputs).astype(BF16)

time: 574 us -> 547 us (0.953)
  Pallas kernels: 284 us -> 254 us
  waiting for transfers between devices: 137 us -> 126 us
  starting transfers between devices: 36.4 us -> 46.6 us
  local copies, waits for them, and re-layouts: 15.1 us -> 22.2 us
    all_to_all x4, waiting for transfers between devices: 62.2 us -> 40.1 us  [exchange(): lax.all_to_all(buffer, ('dp', 'tensor'), split_axis=0, concat_axis=0, til...]
    pallas_call x1, Pallas kernels: 94.9 us -> 79.1 us  [gather_weights(): pl.pallas_call(gather_kernel, out_shape=(jax.ShapeDtypeStruct((4, 2, 4, 2...]
    pallas_call x3 -> x1, Pallas kernels: 20.8 us -> 5.79 us  [pack(): pl.pallas_call(pack_kernel, grid=(4,), out_shape=jax.ShapeDtypeStruct((to...]
    ppermute x4 -> x5, starting transfers between devices: 0.81 us -> 11.8 us  [swap(): return lax.ppermute(values, 'tensor', [(0, 1), (1, 0)])]
    ppermute x4 -> x5, waiting for transfers between devices: 75.3 us -> 85.5 us  [swap(): return lax.ppermute(values, 'tensor', [(0, 1), (1, 0)])]
    unnamed x75 -> x94, local copies, waits for them, and re-layouts: 2.93 us -> 9.43 us
  transfers between devices with their start and end apart: 8 -> 9, of which waited for: 8 -> 9; matrix products, arithmetic and copies ran while one was open for 14% -> 15% of each run, Pallas kernels for 6% -> 6%
where the time goes in v5:
time: 547 us; the launch traced here: 538 us
  Pallas kernels  254 us (46%)
  waiting for transfers between devices  126 us (23%)
  matrix products  63.6 us (12%)
  starting transfers between devices  46.6 us (9%)
  other arithmetic  23.7 us (4%)
  local copies, waits for them, and re-layouts  22.2 us (4%)
    pallas_call x1, Pallas kernels, reduce_grads(): pl.pallas_call(reduce_kernel, out_shape=(jax.ShapeDtypeStruct((rows, a_co...  103 us
    ppermute x5, waiting for transfers between devices, swap(): return lax.ppermute(values, 'tensor', [(0, 1), (1, 0)])  85.5 us
    pallas_call x1, Pallas kernels, gather_weights(): pl.pallas_call(gather_kernel, out_shape=(jax.ShapeDtypeStruct((4, 2, 4, 2...  79.1 us
    dot_general x15, matrix products, dot(): lax.dot_general(left, right, (contract, ((), ())), preferred_element_type...  63.6 us
    all_to_all x4, waiting for transfers between devices, exchange(): lax.all_to_all(buffer, ('dp', 'tensor'), split_axis=0, concat_axis=0, til...  40.1 us
    pallas_call x1, Pallas kernels, run_expert(): pl.pallas_call(expert_kernel, grid=(groups,), out_shape=(jax.ShapeDtypeSt...  39.3 us
    all_to_all x4, starting transfers between devices, exchange(): lax.all_to_all(buffer, ('dp', 'tensor'), split_axis=0, concat_axis=0, til...  34.8 us
    pallas_call x1, Pallas kernels, attend_back(): pl.pallas_call(functools.partial(attend_back_kernel, query_heads, key_hea...  15.2 us
  transfers between devices with their start and end apart: 9, of which 9 were waited for; matrix products, arithmetic and copies ran while one was open for 15% of the time, Pallas kernels for 6%

profile of v5, /device:TPU:0, one launch (start us, length us, event | category | flops | bytes accessed | tf_op | source)
XLA Modules:
  0.0 537.6 jit_solution(3878868664333046825)
XLA Ops:
  9.9 79.1 %shard_map.263 = (bf16[4,2,4,2,32,2560]{5,4,3,2,1,0:T(8,128)(2,1)}, bf16[4,2,4,2,32,2048]{5,4,3,2,1,0:T(8,128)(2,1)}, bf16[2,128,2048]{2,1,0:T(8,128)(2,1)S(1)},...) custom-call(bf16[32,2560]{1,0:T(8,128)(2,1)S(1)} %pad_maximum_fusion.3.sa, bf16[32,2048]{1,0:T(8,128)(2,1)S(1)} %bitcast.81, ...), custom_call_target="tpu_custom_call" | custom-call | bytes 250000000 | tf_op jit(solution)/shard_map/pallas_call | solution.py:471
  92.6 6.9 %all-to-all-start = ((bf16[64,16,2560]{2,1,0:T(8,128)(2,1)}), bf16[64,16,2560]{2,1,0:T(8,128)(2,1)}, u32[]{:S(2)}, u32[]{:S(2)}) async-start(bf16[64,16,2560]{2,1,0:T(8,128)(2,1)} %bitcast.76), calls=%async_computation | async-start | bytes 10485760 | tf_op jit(solution)/shard_map/all_to_all | solution.py:807
  101.0 5.6 %fusion.33.raw = f32[256,2560]{1,0:T(8,128)S(1)} fusion(bf16[256,2048]{1,0:T(8,128)(2,1)S(1)} %bitcast.77, bf16[2048,2560]{1,0:T(8,128)(2,1)} %bitcast.103), kind=kOutput, calls=%fused_computation.93 | convolution fusion | flops 2684354560 | bytes 14155776 | tf_op jit(solution)/shard_map/dot_general | solution.py:656
  106.6 11.9 %shard_map.264 = (bf16[256,2048]{1,0:T(8,128)(2,1)S(1)}, bf16[256,256]{1,0:T(8,128)(2,1)S(1)}, bf16[256,256]{1,0:T(8,128)(2,1)S(1)}, bf16[256,2048]{1,0:T(8,128)(2,1)S(1)}) custom-call(f32[256,2560]{1,0:T(8,128)S(1)} %fusion.33.raw, f32[256,128]{1,0:T(8,128)S(1)} %get-tuple-element.138.cosine, f32[256,128]{1,0:T(8,128)S(1)} %get-tuple-element.139.sine, ...), custom_call_target="tpu_custom_call" | custom-call | flops 600000000 | bytes 6000000 | tf_op jit(solution)/shard_map/pallas_call | solution.py:707
  118.5 6.1 %fusion.34 = f32[256,2048]{1,0:T(8,128)S(1)} fusion(bf16[256,2048]{1,0:T(8,128)(2,1)S(1)} %get-tuple-element.67, bf16[2048,2048]{1,0:T(8,128)(2,1)} %bitcast.105), kind=kOutput, calls=%fused_computation.94 | convolution fusion | flops 2147483648 | bytes 11534336 | tf_op jit(solution)/shard_map/dot_general | solution.py:656
  124.7 11.5 %collective-permute-done.gate_o = bf16[2048,384]{1,0:T(8,128)(2,1)} collective-permute-done((bf16[2048,384]{1,0:T(8,128)(2,1)}, bf16[2048,384]{1,0:T(8,128)(2,1)}, u32[]{:S(2)}, u32[]{:S(2)}) %collective-permute-start) | collective-permute-done | bytes 1572896 | tf_op jit(solution)/shard_map/ppermute | solution.py:781
  137.9 12.6 %collective-permute-done.1 = bf16[128,2048]{1,0:T(8,128)(2,1)} collective-permute-done((bf16[128,2048]{1,0:T(8,128)(2,1)}, bf16[128,2048]{1,0:T(8,128)(2,1)}, u32[]{:S(2)}, u32[]{:S(2)}) %collective-permute-start.1) | collective-permute-done | bytes 524320 | tf_op jit(solution)/shard_map/ppermute | solution.py:781
  154.3 5.8 %shard_map.265 = bf16[1024,2560]{1,0:T(8,128)(2,1)} custom-call(bf16[128,2048]{1,0:T(8,128)(2,1)} %multiply_convert_fusion.values, bf16[1024,128]{1,0:T(8,128)(2,1)} %copy-done.6, bf16[1024,512]{1,0:T(8,128)(2,1)} %copy-done), custom_call_target="tpu_custom_call" | custom-call | flops 1000000000 | bytes 8000000 | tf_op jit(solution)/shard_map/pallas_call | solution.py:537
  162.1 9.3 %all-to-all-start.1 = ((bf16[64,16,2560]{2,1,0:T(8,128)(2,1)}), bf16[64,16,2560]{2,1,0:T(8,128)(2,1)}, u32[]{:S(2)}, u32[]{:S(2)}) async-start(bf16[64,16,2560]{2,1,0:T(8,128)(2,1)} %bitcast.88), calls=%async_computation.1 | async-start | bytes 10485760 | tf_op jit(solution)/shard_map/all_to_all | solution.py:807
  171.7 36.4 %collective-permute-done.2.up_o = bf16[2048,384]{1,0:T(8,128)(2,1)} collective-permute-done((bf16[2048,384]{1,0:T(8,128)(2,1)}, bf16[2048,384]{1,0:T(8,128)(2,1)}, u32[]{:S(2)}, u32[]{:S(2)}) %collective-permute-start.2) | collective-permute-done | bytes 1572896 | tf_op jit(solution)/shard_map/ppermute | solution.py:781
  208.1 26.0 %all-to-all-done.1 = bf16[64,16,2560]{2,1,0:T(8,128)(2,1)} async-done(((bf16[64,16,2560]{2,1,0:T(8,128)(2,1)}), bf16[64,16,2560]{2,1,0:T(8,128)(2,1)}, u32[]{:S(2)}, u32[]{:S(2)}) %all-to-all-start.1) | async-done | bytes 5242912 | tf_op jit(solution)/shard_map/all_to_all | solution.py:807
  234.1 39.3 %shard_map.266 = (bf16[1024,2560]{1,0:T(8,128)(2,1)}, bf16[1024,2560]{1,0:T(8,128)(2,1)}, bf16[1280,2048]{1,0:T(8,128)(2,1)}, bf16[1280,2048]{1,0:T(8,128)(2,1)}...) custom-call(bf16[1024,2560]{1,0:T(8,128)(2,1)} %bitcast.15.rows, ...), custom_call_target="tpu_custom_call" | custom-call | flops 24159191040 | bytes 45000000 | tf_op jit(solution)/shard_map/pallas_call | solution.py:629
  273.4 9.3 %all-to-all-start.2 = ((bf16[64,16,2560]{2,1,0:T(8,128)(2,1)}), bf16[64,16,2560]{2,1,0:T(8,128)(2,1)}, u32[]{:S(2)}, u32[]{:S(2)}) async-start(bf16[64,16,2560]{2,1,0:T(8,128)(2,1)} %bitcast.92), calls=%async_computation.2 | async-start | bytes 10485760 | tf_op jit(solution)/shard_map/all_to_all | solution.py:807
  285.4 5.9 %convolution_convert_fusion.4 = bf16[2048,384]{1,0:T(8,128)(2,1)S(1)} fusion(bf16[1280,2048]{1,0:T(8,128)(2,1)} %get-tuple-element.85, bf16[1280,768]{1,0:T(8,128)(2,1)} %get-tuple-element.80), kind=kOutput, calls=%fused_computation.9 | convolution fusion | flops 2014052352 | bytes 7798784 | tf_op jit(solution)/shard_map/dot_general | solution.py:656
  291.3 9.7 %collective-permute-start.3 = (bf16[2048,384]{1,0:T(8,128)(2,1)S(1)}, bf16[2048,384]{1,0:T(8,128)(2,1)}, u32[]{:S(2)}, u32[]{:S(2)}) collective-permute-start(bf16[2048,384]{1,0:T(8,128)(2,1)S(1)} %convolution_convert_fusion.4), channel_id=1, source_target_pairs={{0,1},{1,0},{2,3},{3,2},{4,5},{5,4},{6,7},{7,6},{8,9},{9,8},{10,11... | collective-permute-start | bytes 4718600 | tf_op jit(solution)/shard_map/ppermute | solution.py:781
  301.0 3.5 convolution_convert_fusion.3.down
  304.6 4.0 convolution_convert_fusion.2.gate
  308.6 4.0 fusion.20
  312.6 4.7 fusion.14
  317.3 4.7 fusion.16
  321.9 15.4 %collective-permute-done.3 = bf16[2048,384]{1,0:T(8,128)(2,1)} collective-permute-done((bf16[2048,384]{1,0:T(8,128)(2,1)S(1)}, bf16[2048,384]{1,0:T(8,128)(2,1)}, u32[]{:S(2)}, u32[]{:S(2)}) %collective-permute-start.3) | collective-permute-done | bytes 1572896 | tf_op jit(solution)/shard_map/ppermute | solution.py:781
  337.4 8.0 %all-to-all-done.2 = bf16[64,16,2560]{2,1,0:T(8,128)(2,1)} async-done(((bf16[64,16,2560]{2,1,0:T(8,128)(2,1)}), bf16[64,16,2560]{2,1,0:T(8,128)(2,1)}, u32[]{:S(2)}, u32[]{:S(2)}) %all-to-all-start.2) | async-done | bytes 5242912 | tf_op jit(solution)/shard_map/all_to_all | solution.py:807
  345.3 9.3 %all-to-all-start.3 = ((bf16[64,16,2560]{2,1,0:T(8,128)(2,1)}), bf16[64,16,2560]{2,1,0:T(8,128)(2,1)}, u32[]{:S(2)}, u32[]{:S(2)}) async-start(bf16[64,16,2560]{2,1,0:T(8,128)(2,1)} %bitcast.91), calls=%async_computation.3 | async-start | bytes 10485760 | tf_op jit(solution)/shard_map/all_to_all | solution.py:807
  356.9 3.4 multiply_reduce_fusion
  362.6 3.7 add_bitcast_fusion.2
  366.2 9.5 %collective-permute-done.4 = bf16[128,2048]{1,0:T(8,128)(2,1)S(1)} collective-permute-done((bf16[128,2048]{1,0:T(8,128)(2,1)S(1)}, bf16[128,2048]{1,0:T(8,128)(2,1)S(1)}, u32[]{:S(2)}, u32[]{:S(2)}) %collective-permute-start.4) | collective-permute-done | bytes 524320 | tf_op jit(solution)/shard_map/ppermute | solution.py:781
  378.1 15.2 %shard_map.267 = (bf16[256,2560]{1,0:T(8,128)(2,1)S(1)}, f32[8,128]{1,0:T(8,128)S(1)}) custom-call(f32[256,2560]{1,0:T(8,128)} %copy-done.1, f32[256,128]{1,0:T(8,128)S(1)} %get-tuple-element.138.cosine, f32[256,128]{1,0:T(8,128)S(1)} %get-tuple-element.139.sine, f32[1,128]{1,0:T(1,128)S(1)} %bitcast.83, f32[1,128]{1,0:T(1,128)S(1)} %bitcast.85, ...), custom_call_target="tpu_custom_call" | custom-call | flops 1000000 | bytes 1000000 | tf_op jit(solution)/shard_map/pallas_call | solution.py:758
  394.0 5.6 %fusion.35 = f32[256,2048]{1,0:T(8,128)S(1)} fusion(bf16[256,2560]{1,0:T(8,128)(2,1)S(1)} %get-tuple-element.87, bf16[2048,2560]{1,0:T(8,128)(2,1)} %bitcast.104), kind=kOutput, calls=%fused_computation.95 | convolution fusion | flops 2684354560 | bytes 13893632 | tf_op jit(solution)/shard_map/dot_general | solution.py:656
  401.6 5.7 %convolution_convert_fusion.1 = bf16[2048,2048]{1,0:T(8,128)(2,1)} fusion(bf16[256,2048]{1,0:T(8,128)(2,1)S(1)} %copy-done.9, bf16[128,2048]{1,0:T(8,128)(2,1)S(1)} %get-tuple-element.115, bf16[128,2048]{1,0:T(8,128)(2,1)S(1)} %get-tuple-element.114), kind=kOutput, calls=%fused_computation.1 | convolution fusion | flops 2153775104 | bytes 10485760 | tf_op jit(solution)/shard_map/dot_general | solution.py:656
  407.4 5.8 %convolution_convert_fusion = bf16[2048,2560]{1,0:T(8,128)(2,1)} fusion(bf16[256,2048]{1,0:T(8,128)(2,1)S(1)} %bitcast.78, bf16[256,2560]{1,0:T(8,128)(2,1)S(1)} %get-tuple-element.87), kind=kOutput, calls=%fused_computation | convolution fusion | flops 2689597440 | bytes 12845056 | tf_op jit(solution)/shard_map/dot_general | solution.py:656
  413.1 4.1 all-to-all-done.3
  417.3 102.9 %shard_map.268 = (f32[32,2560]{1,0:T(8,128)}, f32[32,2048]{1,0:T(8,128)}, f32[8,2048]{1,0:T(8,128)}, bf16[128,2048]{1,0:T(8,128)(2,1)}, bf16[128,2048]{1,0:T(8,1...) custom-call(bf16[4,2,4,2,32,2560]{5,4,3,2,1,0:T(8,128)(2,1)} %bitcast.86, ...), custom_call_target="tpu_custom_call" | custom-call | flops 10000000 | bytes 300000000 | tf_op jit(solution)/shard_map/pallas_call | solution.py:294
  (150 shorter events, 51.0 us)
Async XLA Ops:
  0.6 6.4 %copy-start.16 = (bf16[128,2048]{1,0:T(8,128)(2,1)S(1)}, bf16[128,2048]{1,0:T(8,128)(2,1)}, u32[]{:S(2)}) copy-start(bf16[128,2048]{1,0:T(8,128)(2,1)} %param.16) | copy-start | bytes 1572868
  0.7 6.4 %copy-start.32 = (f32[2048]{0:T(1024)S(1)}, f32[2048]{0:T(1024)}, u32[]{:S(2)}) copy-start(f32[2048]{0:T(1024)} %param.18) | copy-start | bytes 24580
  4.9 84.1 %copy-start.4 = (f32[1024,1]{1,0:T(8,128)}, f32[1024,1]{1,0:T(8,128)S(1)}, u32[]{:S(2)}) copy-start(f32[1024,1]{1,0:T(8,128)S(1)} %reshape.208.piece_weight.part_weight) | copy-start | bytes 12292
  5.2 83.8 %copy-start.5 = (f32[1024,1]{1,0:T(8,128)}, f32[1024,1]{1,0:T(8,128)S(1)}, u32[]{:S(2)}) copy-start(f32[1024,1]{1,0:T(8,128)S(1)} %reshape.207.place_weight) | copy-start | bytes 12292
  7.1 82.0 %copy-start = (bf16[1024,512]{1,0:T(8,128)(2,1)}, bf16[1024,512]{1,0:T(8,128)(2,1)S(1)}, u32[]{:S(2)}) copy-start(bf16[1024,512]{1,0:T(8,128)(2,1)S(1)} %get-tuple-element.119.pieces.part) | copy-start | bytes 3145732
  92.6 7.7 %copy-start.37 = (s32[256]{0:T(256)S(1)}, s32[256]{0:T(256)}, u32[]{:S(2)}) copy-start(s32[256]{0:T(256)} %param.17) | copy-start | bytes 3076
  92.6 69.6 %all-to-all-start = ((bf16[64,16,2560]{2,1,0:T(8,128)(2,1)}), bf16[64,16,2560]{2,1,0:T(8,128)(2,1)}, u32[]{:S(2)}, u32[]{:S(2)}) async-start(bf16[64,16,2560]{2,1,0:T(8,128)(2,1)} %bitcast.76), calls=%async_computation | async-start | bytes 10485760 | tf_op jit(solution)/shard_map/all_to_all | solution.py:807
  99.5 36.7 %collective-permute-start = (bf16[2048,384]{1,0:T(8,128)(2,1)}, bf16[2048,384]{1,0:T(8,128)(2,1)}, u32[]{:S(2)}, u32[]{:S(2)}) collective-permute-start(bf16[2048,384]{1,0:T(8,128)(2,1)} %bitcast.6.gate_m), channel_id=1, source_target_pairs={{0,1},{1,0},{2,3},{3,2},{4,5},{5,4},{6,7},{7,6},{8,9},{9,8},{10,11... | collective-permute-start | bytes 4718600 | tf_op jit(solution)/shard_map/ppermute | solution.py:781
  106.6 18.0 %copy-start.1 = (f32[256,2560]{1,0:T(8,128)}, f32[256,2560]{1,0:T(8,128)S(1)}, u32[]{:S(2)}) copy-start(f32[256,2560]{1,0:T(8,128)S(1)} %fusion.33.raw) | copy-start | bytes 7864324
  118.5 6.2 %copy-start.8 = (bf16[256,2048]{1,0:T(8,128)(2,1)}, bf16[256,2048]{1,0:T(8,128)(2,1)S(1)}, u32[]{:S(2)}) copy-start(bf16[256,2048]{1,0:T(8,128)(2,1)S(1)} %get-tuple-element.67) | copy-start | bytes 3145732
  124.6 11.5 %copy-start.28 = (f32[256,2048]{1,0:T(8,128)}, f32[256,2048]{1,0:T(8,128)S(1)}, u32[]{:S(2)}) copy-start(f32[256,2048]{1,0:T(8,128)S(1)} %fusion.34) | copy-start | bytes 6291460
  124.6 28.7 %copy-start.33 = (f32[2048]{0:T(1024)S(1)}, f32[2048]{0:T(1024)}, u32[]{:S(2)}) copy-start(f32[2048]{0:T(1024)} %param.25) | copy-start | bytes 24580
  137.0 13.5 %collective-permute-start.1 = (bf16[128,2048]{1,0:T(8,128)(2,1)}, bf16[128,2048]{1,0:T(8,128)(2,1)}, u32[]{:S(2)}, u32[]{:S(2)}) collective-permute-start(bf16[128,2048]{1,0:T(8,128)(2,1)} %dynamic-slice_convert_fusion.1), channel_id=1, source_target_pairs={{0,1},{1,0},{2,3},{3,2},{4,5},{5,4},{6,7},{7,6},{8,9},{9,8},{10,11... | collective-permute-start | bytes 1572872 | tf_op jit(solution)/shard_map/ppermute | solution.py:781
  162.1 71.9 %all-to-all-start.1 = ((bf16[64,16,2560]{2,1,0:T(8,128)(2,1)}), bf16[64,16,2560]{2,1,0:T(8,128)(2,1)}, u32[]{:S(2)}, u32[]{:S(2)}) async-start(bf16[64,16,2560]{2,1,0:T(8,128)(2,1)} %bitcast.88), calls=%async_computation.1 | async-start | bytes 10485760 | tf_op jit(solution)/shard_map/all_to_all | solution.py:807
  171.4 36.7 %collective-permute-start.2 = (bf16[2048,384]{1,0:T(8,128)(2,1)}, bf16[2048,384]{1,0:T(8,128)(2,1)}, u32[]{:S(2)}, u32[]{:S(2)}) collective-permute-start(bf16[2048,384]{1,0:T(8,128)(2,1)} %bitcast.109), channel_id=1, source_target_pairs={{0,1},{1,0},{2,3},{3,2},{4,5},{5,4},{6,7},{7,6},{8,9},{9,8},{10,11... | collective-permute-start | bytes 4718600 | tf_op jit(solution)/shard_map/ppermute | solution.py:781
  273.4 72.0 %all-to-all-start.2 = ((bf16[64,16,2560]{2,1,0:T(8,128)(2,1)}), bf16[64,16,2560]{2,1,0:T(8,128)(2,1)}, u32[]{:S(2)}, u32[]{:S(2)}) async-start(bf16[64,16,2560]{2,1,0:T(8,128)(2,1)} %bitcast.92), calls=%async_computation.2 | async-start | bytes 10485760 | tf_op jit(solution)/shard_map/all_to_all | solution.py:807
  282.7 18.3 %slice-start = ((s8[5242880]{0:T(1024)(128)(4,1)}), s8[4194304]{0:T(1024)(128)(4,1)S(1)}, s32[]{:S(2)}) async-start(s8[5242880]{0:T(1024)(128)(4,1)} %bitcast.89), calls=%async_computation.4 | async-start | bytes 8388608
  282.7 21.9 %slice-start.4 = ((s8[5242880]{0:T(1024)(128)(4,1)}), s8[4194304]{0:T(1024)(128)(4,1)S(1)}, s32[]{:S(2)}) async-start(s8[5242880]{0:T(1024)(128)(4,1)} %bitcast.111), calls=%async_computation.8 | async-start | bytes 8388608
  285.4 15.7 %slice-start.1 = ((s8[5242880]{0:T(1024)(128)(4,1)}), s8[1048576]{0:T(1024)(128)(4,1)S(1)}, s32[]{:S(2)}) async-start(s8[5242880]{0:T(1024)(128)(4,1)} %bitcast.89), calls=%async_computation.5 | async-start | bytes 2097152
  285.4 15.7 %copy-start.25 = (bf16[1280,768]{1,0:T(8,128)(2,1)S(1)}, bf16[1280,768]{1,0:T(8,128)(2,1)}, u32[]{:S(2)}) copy-start(bf16[1280,768]{1,0:T(8,128)(2,1)} %get-tuple-element.81) | copy-start | bytes 5898244
  285.4 19.2 %slice-start.5 = ((s8[5242880]{0:T(1024)(128)(4,1)}), s8[1048576]{0:T(1024)(128)(4,1)S(1)}, s32[]{:S(2)}) async-start(s8[5242880]{0:T(1024)(128)(4,1)} %bitcast.111), calls=%async_computation.9 | async-start | bytes 2097152
  291.3 46.1 %collective-permute-start.3 = (bf16[2048,384]{1,0:T(8,128)(2,1)S(1)}, bf16[2048,384]{1,0:T(8,128)(2,1)}, u32[]{:S(2)}, u32[]{:S(2)}) collective-permute-start(bf16[2048,384]{1,0:T(8,128)(2,1)S(1)} %convolution_convert_fusion.4), channel_id=1, source_target_pairs={{0,1},{1,0},{2,3},{3,2},{4,5},{5,4},{6,7},{7,6},{8,9},{9,8},{10,11... | collective-permute-start | bytes 4718600 | tf_op jit(solution)/shard_map/ppermute | solution.py:781
  345.3 71.9 %all-to-all-start.3 = ((bf16[64,16,2560]{2,1,0:T(8,128)(2,1)}), bf16[64,16,2560]{2,1,0:T(8,128)(2,1)}, u32[]{:S(2)}, u32[]{:S(2)}) async-start(bf16[64,16,2560]{2,1,0:T(8,128)(2,1)} %bitcast.91), calls=%async_computation.3 | async-start | bytes 10485760 | tf_op jit(solution)/shard_map/all_to_all | solution.py:807
  356.9 18.9 %slice-start.2 = ((s8[8388608]{0:T(1024)(128)(4,1)}), s8[4194304]{0:T(1024)(128)(4,1)S(1)}, s32[]{:S(2)}) async-start(s8[8388608]{0:T(1024)(128)(4,1)} %bitcast.106), calls=%async_computation.6 | async-start | bytes 8388608
  360.3 15.5 %slice-start.3 = ((s8[8388608]{0:T(1024)(128)(4,1)}), s8[4194304]{0:T(1024)(128)(4,1)S(1)}, s32[]{:S(2)}) async-start(s8[8388608]{0:T(1024)(128)(4,1)} %bitcast.106), calls=%async_computation.7 | async-start | bytes 8388608
  361.7 14.0 %collective-permute-start.4 = (bf16[128,2048]{1,0:T(8,128)(2,1)S(1)}, bf16[128,2048]{1,0:T(8,128)(2,1)S(1)}, u32[]{:S(2)}, u32[]{:S(2)}) collective-permute-start(bf16[128,2048]{1,0:T(8,128)(2,1)S(1)} %get-tuple-element.110), channel_id=1, source_target_pairs={{0,1},{1,0},{2,3},{3,2},{4,5},{5,4},{6,7},{7,6},{8,9},{9,8},{10,11... | collective-permute-start | bytes 1572872 | tf_op jit(solution)/shard_map/ppermute | solution.py:781
  399.6 7.7 %copy-start.19 = (f32[256,2048]{1,0:T(8,128)}, f32[256,2048]{1,0:T(8,128)S(1)}, u32[]{:S(2)}) copy-start(f32[256,2048]{1,0:T(8,128)S(1)} %fusion.35) | copy-start | bytes 6291460
  417.3 108.9 %copy-start.17 = (bf16[128,2048]{1,0:T(8,128)(2,1)S(1)}, bf16[128,2048]{1,0:T(8,128)(2,1)}, u32[]{:S(2)}) copy-start(bf16[128,2048]{1,0:T(8,128)(2,1)} %param.16) | copy-start | bytes 1572868
  417.3 108.9 %copy-start.20 = (f32[256,2048]{1,0:T(8,128)S(1)}, f32[256,2048]{1,0:T(8,128)}, u32[]{:S(2)}) copy-start(f32[256,2048]{1,0:T(8,128)} %copy-done.19) | copy-start | bytes 6291460
  417.3 110.2 %copy-start.34 = (s32[128,8]{0,1:T(8,128)S(1)}, s32[128,8]{0,1:T(8,128)}, u32[]{:S(2)}) copy-start(s32[128,8]{0,1:T(8,128)} %param.26) | copy-start | bytes 12292
  417.3 111.6 %copy-start.18 = (f32[384,2048]{1,0:T(8,128)S(1)}, f32[384,2048]{1,0:T(8,128)}, u32[]{:S(2)}) copy-start(f32[384,2048]{1,0:T(8,128)} %fusion.20) | copy-start | bytes 9437188
  520.2 8.7 %copy-start.27 = (bf16[384,2048]{1,0:T(8,128)(2,1)S(1)}, bf16[384,2048]{1,0:T(8,128)(2,1)}, u32[]{:S(2)}) copy-start(bf16[384,2048]{1,0:T(8,128)(2,1)} %get-tuple-element.105) | copy-start | bytes 4718596
  (23 other events, 69.2 us)

commit v6 on v5

--- a/solution.py
+++ b/solution.py
@@ -900,7 +900,7 @@
     units = down_w.shape[0]
     others = ((hidden[:, units:], grads_in), (rows_in, d_gate[:, units:]), (rows_in, d_up[:, units:]))
     sent = [dot(left, right, ((0,), (0,))).astype(BF16) for left, right in others]
-    gate_came = swap(sent[1])
+    gate_came, up_first = swap(sent[1]), swap(sent[2][: width // 2])
     *sent, rows_k, grads_k = lax.optimization_barrier((*sent, rows_in, grads_in))
     kept = [
         dot(left, right, ((0,), (0,)))
@@ -913,7 +913,7 @@
     d_mid = to_tokens(back_rows, place, part)
     d_mid_in, grad_norm_mid = norm_back(hidden_in, mid_scale, norm_mid, d_mid)
     d_hidden_in = grad + d_mid_in
-    d_attended = d_hidden_in.astype(BF16)
+    d_attended, up_first = lax.optimization_barrier((d_hidden_in.astype(BF16), up_first))
     d_whole = share_sequence(d_attended)
     d_mixed = dot(d_whole, out_full, ((1,), (0,))).astype(BF16)
     d_raw, gain_sums = attend_back(
@@ -928,17 +928,17 @@
     gain_row = jnp.pad(gain_sums[:2].reshape(1, -1), ((0, 0), (0, width - 2 * HD)))
     gains = jnp.pad(jnp.concatenate([grad_norm_mid[None], gain_row]), ((1, 5), (0, 0)))
     in_grads, returned = lax.optimization_barrier((in_grads, returned))
-    in_total, out_total, gains, d_came, output, of_expert, down_came, up_came = reduce_grads(
+    in_total, out_total, gains, d_came, output, of_expert, down_came, up_second = reduce_grads(
         in_grads, out_grads, gains, d_own, d_sent.astype(BF16), inputs * in_scale,
         (returned, place, part, place_weight, part_weight, out_grad, hidden_in),
-        (sent[0], sent[2]),
+        (sent[0], sent[2][width // 2 :]),
     )
     grad_route = jnp.sum(jnp.where(names, of_expert.T[:, None, :], 0.0), axis=2)
     d_normed = d_own + d_came.astype(F32)
     d_inputs, _ = norm_back(inputs, in_scale, norm_in, d_normed)
     grad_tokens = (d_hidden_in + d_inputs).astype(BF16)
     grad_down, grad_gate, grad_up = [
-        (own + half.astype(F32))[None] for own, half in zip(kept, (down_came, gate_came, up_came))
+        (own + half.astype(F32))[None] for own, half in zip(kept, (down_came, gate_came, jnp.concatenate([up_first, up_second])))
     ]
     grad_norm_in, grad_norm_mid = gains[0], gains[1]
     grad_query_gain, grad_key_gain = gains[2, :HD], gains[2, HD : 2 * HD]

time: 547 us -> 543 us (level)
  Pallas kernels: 254 us -> 247 us
  waiting for transfers between devices: 126 us -> 133 us
  starting transfers between devices: 46.6 us -> 40.6 us
    ppermute x5 -> x6, waiting for transfers between devices: 85.5 us -> 101 us  [swap(): return lax.ppermute(values, 'tensor', [(0, 1), (1, 0)])]
    all_to_all x4, waiting for transfers between devices: 40.1 us -> 32.2 us  [exchange(): lax.all_to_all(buffer, ('dp', 'tensor'), split_axis=0, concat_axis=0, til...]
    ppermute x5 -> x6, starting transfers between devices: 11.8 us -> 4.3 us  [swap(): return lax.ppermute(values, 'tensor', [(0, 1), (1, 0)])]
    pallas_call x1, Pallas kernels: 103 us -> 95.8 us  [reduce_grads(): pl.pallas_call(reduce_kernel, out_shape=(jax.ShapeDtypeStruct((rows, a_co...]
  transfers between devices with their start and end apart: 9 -> 10, of which waited for: 9 -> 8; matrix products, arithmetic and copies ran while one was open for 15% -> 15% of each run, Pallas kernels for 6% -> 6%
where the time goes in v6:
time: 543 us; the launch traced here: 533 us
  Pallas kernels  247 us (45%)
  waiting for transfers between devices  133 us (24%)
  matrix products  62.4 us (11%)
  starting transfers between devices  40.6 us (7%)
  other arithmetic  25 us (5%)
  local copies, waits for them, and re-layouts  23.9 us (4%)
    ppermute x6, waiting for transfers between devices, swap(): return lax.ppermute(values, 'tensor', [(0, 1), (1, 0)])  101 us
    pallas_call x1, Pallas kernels, reduce_grads(): pl.pallas_call(reduce_kernel, out_shape=(jax.ShapeDtypeStruct((rows, a_co...  95.8 us
    pallas_call x1, Pallas kernels, gather_weights(): pl.pallas_call(gather_kernel, out_shape=(jax.ShapeDtypeStruct((4, 2, 4, 2...  79.1 us
    dot_general x15, matrix products, dot(): lax.dot_general(left, right, (contract, ((), ())), preferred_element_type...  62.4 us
    pallas_call x1, Pallas kernels, run_expert(): pl.pallas_call(expert_kernel, grid=(groups,), out_shape=(jax.ShapeDtypeSt...  39.3 us
    all_to_all x4, starting transfers between devices, exchange(): lax.all_to_all(buffer, ('dp', 'tensor'), split_axis=0, concat_axis=0, til...  36.3 us
    all_to_all x4, waiting for transfers between devices, exchange(): lax.all_to_all(buffer, ('dp', 'tensor'), split_axis=0, concat_axis=0, til...  32.2 us
    pallas_call x1, Pallas kernels, attend_back(): pl.pallas_call(functools.partial(attend_back_kernel, query_heads, key_hea...  15.2 us
  transfers between devices with their start and end apart: 10, of which 8 were waited for; matrix products, arithmetic and copies ran while one was open for 15% of the time, Pallas kernels for 6%

profile of v6, /device:TPU:0, one launch (start us, length us, event | category | flops | bytes accessed | tf_op | source)
XLA Modules:
  0.0 533.4 jit_solution(547430478594926283)
XLA Ops:
  9.9 79.1 %shard_map.263 = (bf16[4,2,4,2,32,2560]{5,4,3,2,1,0:T(8,128)(2,1)}, bf16[4,2,4,2,32,2048]{5,4,3,2,1,0:T(8,128)(2,1)}, bf16[2,128,2048]{2,1,0:T(8,128)(2,1)S(1)},...) custom-call(bf16[32,2560]{1,0:T(8,128)(2,1)S(1)} %pad_maximum_fusion.3.sa, bf16[32,2048]{1,0:T(8,128)(2,1)S(1)} %bitcast.81, ...), custom_call_target="tpu_custom_call" | custom-call | bytes 250000000 | tf_op jit(solution)/shard_map/pallas_call | solution.py:471
  92.6 6.9 %all-to-all-start = ((bf16[64,16,2560]{2,1,0:T(8,128)(2,1)}), bf16[64,16,2560]{2,1,0:T(8,128)(2,1)}, u32[]{:S(2)}, u32[]{:S(2)}) async-start(bf16[64,16,2560]{2,1,0:T(8,128)(2,1)} %bitcast.76), calls=%async_computation | async-start | bytes 10485760 | tf_op jit(solution)/shard_map/all_to_all | solution.py:807
  100.9 5.7 %fusion.33.raw = f32[256,2560]{1,0:T(8,128)S(1)} fusion(bf16[256,2048]{1,0:T(8,128)(2,1)S(1)} %bitcast.77, bf16[2048,2560]{1,0:T(8,128)(2,1)} %bitcast.103), kind=kOutput, calls=%fused_computation.93 | convolution fusion | flops 2684354560 | bytes 14155776 | tf_op jit(solution)/shard_map/dot_general | solution.py:656
  106.7 11.9 %shard_map.264 = (bf16[256,2048]{1,0:T(8,128)(2,1)S(1)}, bf16[256,256]{1,0:T(8,128)(2,1)S(1)}, bf16[256,256]{1,0:T(8,128)(2,1)S(1)}, bf16[256,2048]{1,0:T(8,128)(2,1)S(1)}) custom-call(f32[256,2560]{1,0:T(8,128)S(1)} %fusion.33.raw, f32[256,128]{1,0:T(8,128)S(1)} %get-tuple-element.142.cosine, f32[256,128]{1,0:T(8,128)S(1)} %get-tuple-element.143.sine, ...), custom_call_target="tpu_custom_call" | custom-call | flops 600000000 | bytes 6000000 | tf_op jit(solution)/shard_map/pallas_call | solution.py:707
  118.5 6.1 %fusion.34 = f32[256,2048]{1,0:T(8,128)S(1)} fusion(bf16[256,2048]{1,0:T(8,128)(2,1)S(1)} %get-tuple-element.69, bf16[2048,2048]{1,0:T(8,128)(2,1)} %bitcast.105), kind=kOutput, calls=%fused_computation.94 | convolution fusion | flops 2147483648 | bytes 11534336 | tf_op jit(solution)/shard_map/dot_general | solution.py:656
  124.7 11.4 %collective-permute-done.gate_o = bf16[2048,384]{1,0:T(8,128)(2,1)} collective-permute-done((bf16[2048,384]{1,0:T(8,128)(2,1)}, bf16[2048,384]{1,0:T(8,128)(2,1)}, u32[]{:S(2)}, u32[]{:S(2)}) %collective-permute-start) | collective-permute-done | bytes 1572896 | tf_op jit(solution)/shard_map/ppermute | solution.py:781
  137.9 12.6 %collective-permute-done.1 = bf16[128,2048]{1,0:T(8,128)(2,1)} collective-permute-done((bf16[128,2048]{1,0:T(8,128)(2,1)}, bf16[128,2048]{1,0:T(8,128)(2,1)}, u32[]{:S(2)}, u32[]{:S(2)}) %collective-permute-start.1) | collective-permute-done | bytes 524320 | tf_op jit(solution)/shard_map/ppermute | solution.py:781
  154.2 5.8 %shard_map.265 = bf16[1024,2560]{1,0:T(8,128)(2,1)} custom-call(bf16[128,2048]{1,0:T(8,128)(2,1)} %multiply_convert_fusion.values, bf16[1024,128]{1,0:T(8,128)(2,1)} %copy-done.6, bf16[1024,512]{1,0:T(8,128)(2,1)} %copy-done), custom_call_target="tpu_custom_call" | custom-call | flops 1000000000 | bytes 8000000 | tf_op jit(solution)/shard_map/pallas_call | solution.py:537
  162.1 9.3 %all-to-all-start.1 = ((bf16[64,16,2560]{2,1,0:T(8,128)(2,1)}), bf16[64,16,2560]{2,1,0:T(8,128)(2,1)}, u32[]{:S(2)}, u32[]{:S(2)}) async-start(bf16[64,16,2560]{2,1,0:T(8,128)(2,1)} %bitcast.88), calls=%async_computation.1 | async-start | bytes 10485760 | tf_op jit(solution)/shard_map/all_to_all | solution.py:807
  171.7 36.4 %collective-permute-done.2.up_o = bf16[2048,384]{1,0:T(8,128)(2,1)} collective-permute-done((bf16[2048,384]{1,0:T(8,128)(2,1)}, bf16[2048,384]{1,0:T(8,128)(2,1)}, u32[]{:S(2)}, u32[]{:S(2)}) %collective-permute-start.2) | collective-permute-done | bytes 1572896 | tf_op jit(solution)/shard_map/ppermute | solution.py:781
  208.1 26.0 %all-to-all-done.1 = bf16[64,16,2560]{2,1,0:T(8,128)(2,1)} async-done(((bf16[64,16,2560]{2,1,0:T(8,128)(2,1)}), bf16[64,16,2560]{2,1,0:T(8,128)(2,1)}, u32[]{:S(2)}, u32[]{:S(2)}) %all-to-all-start.1) | async-done | bytes 5242912 | tf_op jit(solution)/shard_map/all_to_all | solution.py:807
  234.1 39.3 %shard_map.266 = (bf16[1024,2560]{1,0:T(8,128)(2,1)}, bf16[1024,2560]{1,0:T(8,128)(2,1)}, bf16[1280,2048]{1,0:T(8,128)(2,1)}, bf16[1280,2048]{1,0:T(8,128)(2,1)}...) custom-call(bf16[1024,2560]{1,0:T(8,128)(2,1)} %bitcast.15.rows, ...), custom_call_target="tpu_custom_call" | custom-call | flops 24159191040 | bytes 45000000 | tf_op jit(solution)/shard_map/pallas_call | solution.py:629
  273.4 9.7 %all-to-all-start.2 = ((bf16[64,16,2560]{2,1,0:T(8,128)(2,1)}), bf16[64,16,2560]{2,1,0:T(8,128)(2,1)}, u32[]{:S(2)}, u32[]{:S(2)}) async-start(bf16[64,16,2560]{2,1,0:T(8,128)(2,1)} %bitcast.92), calls=%async_computation.2 | async-start | bytes 10485760 | tf_op jit(solution)/shard_map/all_to_all | solution.py:807
  283.1 2.6 copy.50
  285.7 5.8 %convolution_convert_fusion.2 = bf16[2048,384]{1,0:T(8,128)(2,1)S(1)} fusion(bf16[1280,2048]{1,0:T(8,128)(2,1)} %get-tuple-element.87, bf16[1280,768]{1,0:T(8,128)(2,1)} %get-tuple-element.85), kind=kOutput, calls=%fused_computation.7 | convolution fusion | flops 2014052352 | bytes 7798784 | tf_op jit(solution)/shard_map/dot_general | solution.py:656
  292.6 3.0 convolution_convert_fusion.4
  297.9 3.4 convolution_convert_fusion.3.down
  302.4 4.0 fusion.20
  306.4 4.7 fusion.14
  311.0 4.7 fusion.16
  315.7 30.5 %collective-permute-done.3 = bf16[2048,384]{1,0:T(8,128)(2,1)} collective-permute-done((bf16[2048,384]{1,0:T(8,128)(2,1)S(1)}, bf16[2048,384]{1,0:T(8,128)(2,1)}, u32[]{:S(2)}, u32[]{:S(2)}) %collective-permute-start.3) | collective-permute-done | bytes 1572896 | tf_op jit(solution)/shard_map/ppermute | solution.py:781
  346.2 10.4 %all-to-all-start.3 = ((bf16[64,16,2560]{2,1,0:T(8,128)(2,1)}), bf16[64,16,2560]{2,1,0:T(8,128)(2,1)}, u32[]{:S(2)}, u32[]{:S(2)}) async-start(bf16[64,16,2560]{2,1,0:T(8,128)(2,1)} %bitcast.91), calls=%async_computation.3 | async-start | bytes 10485760 | tf_op jit(solution)/shard_map/all_to_all | solution.py:807
  358.9 3.4 multiply_reduce_fusion
  364.6 3.7 add_bitcast_fusion.2
  368.2 9.5 %collective-permute-done.5 = bf16[128,2048]{1,0:T(8,128)(2,1)S(1)} collective-permute-done((bf16[128,2048]{1,0:T(8,128)(2,1)S(1)}, bf16[128,2048]{1,0:T(8,128)(2,1)S(1)}, u32[]{:S(2)}, u32[]{:S(2)}) %collective-permute-start.5) | collective-permute-done | bytes 524320 | tf_op jit(solution)/shard_map/ppermute | solution.py:781
  380.2 15.2 %shard_map.267 = (bf16[256,2560]{1,0:T(8,128)(2,1)S(1)}, f32[8,128]{1,0:T(8,128)S(1)}) custom-call(f32[256,2560]{1,0:T(8,128)} %copy-done.1, f32[256,128]{1,0:T(8,128)S(1)} %get-tuple-element.142.cosine, f32[256,128]{1,0:T(8,128)S(1)} %get-tuple-element.143.sine, f32[1,128]{1,0:T(1,128)S(1)} %bitcast.83, f32[1,128]{1,0:T(1,128)S(1)} %bitcast.85, ...), custom_call_target="tpu_custom_call" | custom-call | flops 1000000 | bytes 1000000 | tf_op jit(solution)/shard_map/pallas_call | solution.py:758
  396.0 5.6 %fusion.35 = f32[256,2048]{1,0:T(8,128)S(1)} fusion(bf16[256,2560]{1,0:T(8,128)(2,1)S(1)} %get-tuple-element.90, bf16[2048,2560]{1,0:T(8,128)(2,1)} %bitcast.104), kind=kOutput, calls=%fused_computation.95 | convolution fusion | flops 2684354560 | bytes 13893632 | tf_op jit(solution)/shard_map/dot_general | solution.py:656
  403.7 5.7 %convolution_convert_fusion.1 = bf16[2048,2048]{1,0:T(8,128)(2,1)} fusion(bf16[256,2048]{1,0:T(8,128)(2,1)S(1)} %copy-done.9, bf16[128,2048]{1,0:T(8,128)(2,1)S(1)} %get-tuple-element.119, bf16[128,2048]{1,0:T(8,128)(2,1)S(1)} %get-tuple-element.118), kind=kOutput, calls=%fused_computation.1 | convolution fusion | flops 2153775104 | bytes 10485760 | tf_op jit(solution)/shard_map/dot_general | solution.py:656
  409.4 5.7 %convolution_convert_fusion = bf16[2048,2560]{1,0:T(8,128)(2,1)} fusion(bf16[256,2048]{1,0:T(8,128)(2,1)S(1)} %bitcast.78, bf16[256,2560]{1,0:T(8,128)(2,1)S(1)} %get-tuple-element.90), kind=kOutput, calls=%fused_computation | convolution fusion | flops 2689597440 | bytes 12845056 | tf_op jit(solution)/shard_map/dot_general | solution.py:656
  415.1 4.2 all-to-all-done.3
  419.3 95.8 %shard_map.268 = (f32[32,2560]{1,0:T(8,128)}, f32[32,2048]{1,0:T(8,128)}, f32[8,2048]{1,0:T(8,128)}, bf16[128,2048]{1,0:T(8,128)(2,1)}, bf16[128,2048]{1,0:T(8,1...) custom-call(bf16[4,2,4,2,32,2560]{5,4,3,2,1,0:T(8,128)(2,1)} %bitcast.86, ...), custom_call_target="tpu_custom_call" | custom-call | flops 10000000 | bytes 300000000 | tf_op jit(solution)/shard_map/pallas_call | solution.py:294
  527.0 3.2 add_bitcast_fusion.1
  (154 shorter events, 50.4 us)
Async XLA Ops:
  0.6 6.4 %copy-start.16 = (bf16[128,2048]{1,0:T(8,128)(2,1)S(1)}, bf16[128,2048]{1,0:T(8,128)(2,1)}, u32[]{:S(2)}) copy-start(bf16[128,2048]{1,0:T(8,128)(2,1)} %param.16) | copy-start | bytes 1572868
  0.7 6.4 %copy-start.32 = (f32[2048]{0:T(1024)S(1)}, f32[2048]{0:T(1024)}, u32[]{:S(2)}) copy-start(f32[2048]{0:T(1024)} %param.18) | copy-start | bytes 24580
  4.9 84.1 %copy-start.4 = (f32[1024,1]{1,0:T(8,128)}, f32[1024,1]{1,0:T(8,128)S(1)}, u32[]{:S(2)}) copy-start(f32[1024,1]{1,0:T(8,128)S(1)} %reshape.208.piece_weight.part_weight) | copy-start | bytes 12292
  5.2 83.8 %copy-start.5 = (f32[1024,1]{1,0:T(8,128)}, f32[1024,1]{1,0:T(8,128)S(1)}, u32[]{:S(2)}) copy-start(f32[1024,1]{1,0:T(8,128)S(1)} %reshape.207.place_weight) | copy-start | bytes 12292
  7.1 82.0 %copy-start = (bf16[1024,512]{1,0:T(8,128)(2,1)}, bf16[1024,512]{1,0:T(8,128)(2,1)S(1)}, u32[]{:S(2)}) copy-start(bf16[1024,512]{1,0:T(8,128)(2,1)S(1)} %get-tuple-element.123.pieces.part) | copy-start | bytes 3145732
  92.6 7.7 %copy-start.37 = (s32[256]{0:T(256)S(1)}, s32[256]{0:T(256)}, u32[]{:S(2)}) copy-start(s32[256]{0:T(256)} %param.17) | copy-start | bytes 3076
  92.6 69.6 %all-to-all-start = ((bf16[64,16,2560]{2,1,0:T(8,128)(2,1)}), bf16[64,16,2560]{2,1,0:T(8,128)(2,1)}, u32[]{:S(2)}, u32[]{:S(2)}) async-start(bf16[64,16,2560]{2,1,0:T(8,128)(2,1)} %bitcast.76), calls=%async_computation | async-start | bytes 10485760 | tf_op jit(solution)/shard_map/all_to_all | solution.py:807
  99.5 36.7 %collective-permute-start = (bf16[2048,384]{1,0:T(8,128)(2,1)}, bf16[2048,384]{1,0:T(8,128)(2,1)}, u32[]{:S(2)}, u32[]{:S(2)}) collective-permute-start(bf16[2048,384]{1,0:T(8,128)(2,1)} %bitcast.6.gate_m), channel_id=1, source_target_pairs={{0,1},{1,0},{2,3},{3,2},{4,5},{5,4},{6,7},{7,6},{8,9},{9,8},{10,11... | collective-permute-start | bytes 4718600 | tf_op jit(solution)/shard_map/ppermute | solution.py:781
  106.6 18.0 %copy-start.1 = (f32[256,2560]{1,0:T(8,128)}, f32[256,2560]{1,0:T(8,128)S(1)}, u32[]{:S(2)}) copy-start(f32[256,2560]{1,0:T(8,128)S(1)} %fusion.33.raw) | copy-start | bytes 7864324
  118.5 6.2 %copy-start.8 = (bf16[256,2048]{1,0:T(8,128)(2,1)}, bf16[256,2048]{1,0:T(8,128)(2,1)S(1)}, u32[]{:S(2)}) copy-start(bf16[256,2048]{1,0:T(8,128)(2,1)S(1)} %get-tuple-element.69) | copy-start | bytes 3145732
  124.7 11.5 %copy-start.27 = (f32[256,2048]{1,0:T(8,128)}, f32[256,2048]{1,0:T(8,128)S(1)}, u32[]{:S(2)}) copy-start(f32[256,2048]{1,0:T(8,128)S(1)} %fusion.34) | copy-start | bytes 6291460
  124.7 28.6 %copy-start.33 = (f32[2048]{0:T(1024)S(1)}, f32[2048]{0:T(1024)}, u32[]{:S(2)}) copy-start(f32[2048]{0:T(1024)} %param.25) | copy-start | bytes 24580
  137.0 13.5 %collective-permute-start.1 = (bf16[128,2048]{1,0:T(8,128)(2,1)}, bf16[128,2048]{1,0:T(8,128)(2,1)}, u32[]{:S(2)}, u32[]{:S(2)}) collective-permute-start(bf16[128,2048]{1,0:T(8,128)(2,1)} %dynamic-slice_convert_fusion.1), channel_id=1, source_target_pairs={{0,1},{1,0},{2,3},{3,2},{4,5},{5,4},{6,7},{7,6},{8,9},{9,8},{10,11... | collective-permute-start | bytes 1572872 | tf_op jit(solution)/shard_map/ppermute | solution.py:781
  162.1 71.9 %all-to-all-start.1 = ((bf16[64,16,2560]{2,1,0:T(8,128)(2,1)}), bf16[64,16,2560]{2,1,0:T(8,128)(2,1)}, u32[]{:S(2)}, u32[]{:S(2)}) async-start(bf16[64,16,2560]{2,1,0:T(8,128)(2,1)} %bitcast.88), calls=%async_computation.1 | async-start | bytes 10485760 | tf_op jit(solution)/shard_map/all_to_all | solution.py:807
  171.4 36.7 %collective-permute-start.2 = (bf16[2048,384]{1,0:T(8,128)(2,1)}, bf16[2048,384]{1,0:T(8,128)(2,1)}, u32[]{:S(2)}, u32[]{:S(2)}) collective-permute-start(bf16[2048,384]{1,0:T(8,128)(2,1)} %bitcast.109), channel_id=1, source_target_pairs={{0,1},{1,0},{2,3},{3,2},{4,5},{5,4},{6,7},{7,6},{8,9},{9,8},{10,11... | collective-permute-start | bytes 4718600 | tf_op jit(solution)/shard_map/ppermute | solution.py:781
  273.4 72.9 %all-to-all-start.2 = ((bf16[64,16,2560]{2,1,0:T(8,128)(2,1)}), bf16[64,16,2560]{2,1,0:T(8,128)(2,1)}, u32[]{:S(2)}, u32[]{:S(2)}) async-start(bf16[64,16,2560]{2,1,0:T(8,128)(2,1)} %bitcast.92), calls=%async_computation.2 | async-start | bytes 10485760 | tf_op jit(solution)/shard_map/all_to_all | solution.py:807
  283.1 9.5 %slice-start.4 = ((s8[5242880]{0:T(1024)(128)(4,1)}), s8[4194304]{0:T(1024)(128)(4,1)S(1)}, s32[]{:S(2)}) async-start(s8[5242880]{0:T(1024)(128)(4,1)} %bitcast.111), calls=%async_computation.8 | async-start | bytes 8388608
  285.7 6.8 %slice-start.5 = ((s8[5242880]{0:T(1024)(128)(4,1)}), s8[1048576]{0:T(1024)(128)(4,1)S(1)}, s32[]{:S(2)}) async-start(s8[5242880]{0:T(1024)(128)(4,1)} %bitcast.111), calls=%async_computation.9 | async-start | bytes 2097152
  285.7 6.9 %copy-start.38 = (bf16[1280,768]{1,0:T(8,128)(2,1)S(1)}, bf16[1280,768]{1,0:T(8,128)(2,1)}, u32[]{:S(2)}) copy-start(bf16[1280,768]{1,0:T(8,128)(2,1)} %get-tuple-element.82) | copy-start | bytes 5898244
  291.6 6.3 %slice-start = ((s8[5242880]{0:T(1024)(128)(4,1)}), s8[4194304]{0:T(1024)(128)(4,1)S(1)}, s32[]{:S(2)}) async-start(s8[5242880]{0:T(1024)(128)(4,1)} %bitcast.89), calls=%async_computation.4 | async-start | bytes 8388608
  292.6 71.2 %collective-permute-start.4 = (bf16[1024,384]{1,0:T(8,128)(2,1)}, bf16[1024,384]{1,0:T(8,128)(2,1)}, u32[]{:S(2)}, u32[]{:S(2)}) collective-permute-start(bf16[1024,384]{1,0:T(8,128)(2,1)} %slice.72), channel_id=1, source_target_pairs={{0,1},{1,0},{2,3},{3,2},{4,5},{5,4},{6,7},{7,6},{8,9},{9,8},{10,11... | collective-permute-start | bytes 2359304 | tf_op jit(solution)/shard_map/ppermute | solution.py:781
  295.6 50.6 %collective-permute-start.3 = (bf16[2048,384]{1,0:T(8,128)(2,1)S(1)}, bf16[2048,384]{1,0:T(8,128)(2,1)}, u32[]{:S(2)}, u32[]{:S(2)}) collective-permute-start(bf16[2048,384]{1,0:T(8,128)(2,1)S(1)} %convolution_convert_fusion.4), channel_id=1, source_target_pairs={{0,1},{1,0},{2,3},{3,2},{4,5},{5,4},{6,7},{7,6},{8,9},{9,8},{10,11... | collective-permute-start | bytes 4718600 | tf_op jit(solution)/shard_map/ppermute | solution.py:781
  346.2 73.0 %all-to-all-start.3 = ((bf16[64,16,2560]{2,1,0:T(8,128)(2,1)}), bf16[64,16,2560]{2,1,0:T(8,128)(2,1)}, u32[]{:S(2)}, u32[]{:S(2)}) async-start(bf16[64,16,2560]{2,1,0:T(8,128)(2,1)} %bitcast.91), calls=%async_computation.3 | async-start | bytes 10485760 | tf_op jit(solution)/shard_map/all_to_all | solution.py:807
  358.9 18.9 %slice-start.2 = ((s8[8388608]{0:T(1024)(128)(4,1)}), s8[4194304]{0:T(1024)(128)(4,1)S(1)}, s32[]{:S(2)}) async-start(s8[8388608]{0:T(1024)(128)(4,1)} %bitcast.106), calls=%async_computation.6 | async-start | bytes 8388608
  362.3 15.5 %slice-start.3 = ((s8[8388608]{0:T(1024)(128)(4,1)}), s8[4194304]{0:T(1024)(128)(4,1)S(1)}, s32[]{:S(2)}) async-start(s8[8388608]{0:T(1024)(128)(4,1)} %bitcast.106), calls=%async_computation.7 | async-start | bytes 8388608
  363.7 14.0 %collective-permute-start.5 = (bf16[128,2048]{1,0:T(8,128)(2,1)S(1)}, bf16[128,2048]{1,0:T(8,128)(2,1)S(1)}, u32[]{:S(2)}, u32[]{:S(2)}) collective-permute-start(bf16[128,2048]{1,0:T(8,128)(2,1)S(1)} %get-tuple-element.89), channel_id=1, source_target_pairs={{0,1},{1,0},{2,3},{3,2},{4,5},{5,4},{6,7},{7,6},{8,9},{9,8},{10,11... | collective-permute-start | bytes 1572872 | tf_op jit(solution)/shard_map/ppermute | solution.py:781
  401.7 7.7 %copy-start.19 = (f32[256,2048]{1,0:T(8,128)}, f32[256,2048]{1,0:T(8,128)S(1)}, u32[]{:S(2)}) copy-start(f32[256,2048]{1,0:T(8,128)S(1)} %fusion.35) | copy-start | bytes 6291460
  419.3 101.8 %copy-start.17 = (bf16[128,2048]{1,0:T(8,128)(2,1)S(1)}, bf16[128,2048]{1,0:T(8,128)(2,1)}, u32[]{:S(2)}) copy-start(bf16[128,2048]{1,0:T(8,128)(2,1)} %param.16) | copy-start | bytes 1572868
  419.3 101.8 %copy-start.20 = (f32[256,2048]{1,0:T(8,128)S(1)}, f32[256,2048]{1,0:T(8,128)}, u32[]{:S(2)}) copy-start(f32[256,2048]{1,0:T(8,128)} %copy-done.19) | copy-start | bytes 6291460
  419.3 103.1 %copy-start.34 = (s32[128,8]{0,1:T(8,128)S(1)}, s32[128,8]{0,1:T(8,128)}, u32[]{:S(2)}) copy-start(s32[128,8]{0,1:T(8,128)} %param.26) | copy-start | bytes 12292
  419.3 104.5 %copy-start.18 = (f32[384,2048]{1,0:T(8,128)S(1)}, f32[384,2048]{1,0:T(8,128)}, u32[]{:S(2)}) copy-start(f32[384,2048]{1,0:T(8,128)} %fusion.20) | copy-start | bytes 9437188
  515.1 8.7 %copy-start.26 = (bf16[384,2048]{1,0:T(8,128)(2,1)S(1)}, bf16[384,2048]{1,0:T(8,128)(2,1)}, u32[]{:S(2)}) copy-start(bf16[384,2048]{1,0:T(8,128)(2,1)} %get-tuple-element.109) | copy-start | bytes 4718596
  (24 other events, 77.9 us)
